TPU v7x, 32 devices: a whole 2x2x4 slice. The times are simulated.
32 devices in a mesh: groups: 2 (over x), tm: 2 (over core), space: 8 (over z, y).
Axes of the slice: x: 2, y: 2, z: 4, core: 2. Of those that a mesh axis runs over, the one named last changes fastest.
Arguments:
- nodes: float32 [4, 3, 32, 256, 256], P(('groups', 'tm'), None, 'space'), parts along dimension 0, may hold values from -1 to 1
Outputs:
- updated: float32 [4, 3, 32, 256, 256], P(('groups', 'tm'), None, 'space'), parts along dimension 0
There are 2 independent parts, one for each index of `groups`. A program takes and returns all parts, laid end to end along the dimension named above; each array names one. Nothing has to cross between parts.
All inputs are finite; a program needn't handle non-finite values.
Results may differ from a plain program's by a relative error of at most 0.0001.
Values sent between devices are 32-bit elements; how exact they have to be, the bound alone decides.
No kernel may reach another device: no remote copies, remote signals or barrier semaphores. Data moves between devices by JAX's collectives and lax.ppermute only.
A program may use at most 448 MiB of HBM per device.

v0:
```python
import jax
import jax.numpy as jnp
from jax import lax
from jax.sharding import PartitionSpec as P

DIFFUSE = 0.12
GROWTH = 0.5
WEIGHTS = ((5.0 / 24.0, 1.0 / 3.0, -1.0 / 24.0), (-1.0 / 24.0, 1.0 / 3.0, 5.0 / 24.0))


def padded_2(value, sides, width):
    for axis, dim in sides:
        peers, length = (lax.axis_size(axis), value.shape[dim])
        up = [(i, (i + 1) % peers) for i in range(peers)]
        down = [(j, i) for i, j in up]
        last = lax.slice_in_dim(value, length - width, length, axis=dim)
        leading = lax.slice_in_dim(value, 0, width, axis=dim)
        before = lax.ppermute(last, axis, up)
        after = lax.ppermute(leading, axis, down)
        value = jnp.concatenate([before, value, after], axis=dim)
    return value


def passed_along(value, axis, steps):
    count = lax.axis_size(axis)
    leading, last = (max(0, -steps), min(count, count - steps))
    return lax.ppermute(value, axis, [(source, source + steps) for source in range(leading, last)])


def padded_force(padded, coeff):
    center = padded[..., 1:-1, :, :]
    laplace = padded[..., 2:, :, :] + padded[..., :-2, :, :]
    laplace = laplace + jnp.roll(center, 1, -2) + jnp.roll(center, -1, -2)
    laplace = laplace + jnp.roll(center, 1, -1) + jnp.roll(center, -1, -1) - 6.0 * center
    return coeff * laplace + GROWTH * (center - center * center * center)


def quadrature(row, stacked):
    return (
        WEIGHTS[row][0] * stacked[0] + WEIGHTS[row][1] * stacked[1] + WEIGHTS[row][2] * stacked[2]
    )


def restrict(field):
    shape = field.shape
    blocks = field.reshape(shape[:-3] + (shape[-3] // 2, 2, shape[-2] // 2, 2, shape[-1] // 2, 2))
    return jnp.mean(blocks, axis=(-5, -3, -1))


def prolong(field):
    for axis_at in (-3, -2, -1):
        field = jnp.repeat(field, 2, axis=axis_at)
    return field


def fine_spread(stacked):
    return padded_2(stacked, (("space", 1),), 1)


def coarse_spread(stacked):
    return padded_2(stacked, (("space", 1),), 1)


def pass_on(coarse_end):
    return passed_along(coarse_end, "tm", 1)


def local(nodes):
    current = nodes[0]
    coarse_coeff = DIFFUSE / 4.0
    forces = padded_force(fine_spread(current), DIFFUSE)
    node_one = current[0] + quadrature(0, forces)
    force_one = padded_force(fine_spread(node_one[None]), DIFFUSE)[0]
    node_two = node_one + 0.5 * (force_one - forces[1]) + quadrature(1, forces)
    force_two = padded_force(fine_spread(node_two[None]), DIFFUSE)[0]
    section = lax.axis_index("tm")
    moved = passed_along(node_two, "tm", 1)
    start = jnp.where(section == 0, current[0], moved)
    coarse_nodes = restrict(jnp.stack([current[0], node_one, node_two]))
    restricted = restrict(jnp.stack([forces[0], force_one, force_two]))
    coarse_start = restrict(start)
    first = coarse_start
    sections = lax.axis_size("tm")
    coarse_forces = padded_force(coarse_spread(coarse_nodes), coarse_coeff)
    difference = restricted - coarse_forces
    coarse_one = first
    coarse_two = first
    for turn in range(sections):
        if turn == 0:
            force_first = coarse_forces[0]
        else:
            force_first = padded_force(coarse_spread(first[None]), coarse_coeff)[0]
        coarse_one = (
            first
            + 0.5 * (force_first - coarse_forces[0])
            + quadrature(0, coarse_forces)
            + quadrature(0, difference)
        )
        force_next = padded_force(coarse_spread(coarse_one[None]), coarse_coeff)[0]
        coarse_two = (
            coarse_one
            + 0.5 * (force_next - coarse_forces[1])
            + quadrature(1, coarse_forces)
            + quadrature(1, difference)
        )
        if turn + 1 < sections:
            passed = pass_on(coarse_two)
            first = jnp.where(section == turn + 1, passed, first)
    new_zero = start + prolong(first - coarse_start)
    new_one = node_one + prolong(coarse_one - coarse_nodes[1])
    new_two = node_two + prolong(coarse_two - coarse_nodes[2])
    return jnp.stack([new_zero, new_one, new_two])[None]


def solution(mesh):
    in_specs = (P(("groups", "tm"), None, "space", None, None),)
    out_specs = P(("groups", "tm"), None, "space", None, None)
    return jax.shard_map(local, mesh=mesh, in_specs=in_specs, out_specs=out_specs, check_vma=False)
```

profile of v0, /device:TPU:1, one launch (start us, length us, event | category | flops | bytes accessed | tf_op | source)
XLA Modules:
  0.0 830.0 jit_solution(7730923762984314208)
XLA Ops:
  0.0 3.3 copy.21
  7.8 3.0 collective-permute-start
  10.8 3.5 fusion.92
  15.5 69.3 %reshape.154 = f32[1,2,2,128,2,128,2]{4,3,2,1,6,5,0:T(8,128)} reshape(f32[1,1,4,256,256]{3,2,4,1,0:T(4,128)} %slice.461) | data formatting | bytes 2097152 | tf_op jit(solution)/shard_map/stack | solution.py:79
  84.8 45.9 %copy.27 = f32[1,2,2,128,2,128,2]{5,3,6,4,2,1,0:T(8,128)} copy(f32[1,2,2,128,2,128,2]{4,3,2,1,6,5,0:T(8,128)} %reshape.154) | data formatting | bytes 2097152 | tf_op jit(solution)/shard_map/stack | solution.py:79
  134.6 11.1 %fusion.1 = f32[3,4,256,256]{2,1,3,0:T(4,128)S(1)} fusion(f32[3,4,256,256]{2,1,3,0:T(4,128)S(1)} %bitcast.150, f32[3,1,256,256]{2,1,3,0:T(1,128)} %collective-permute-done.1, f32[3,1,256,256]{2,1,3,0:T(1,128)} %collective-permute-done, f32[3,4,255,256]{2,1,3,0:T(4,128)S(1)} %get-tuple-element.21, f32[3,4,1,256]{2,1,3,0:T(4,128)S(1)} %get-tuple-element.23, ...), kind=kLoop, calls=%fused_computation.2 | loop fusion | flops 14942208 | bytes 20447232 | tf_op jit(solution)/shard_map/add | solution.py:35
  151.7 69.3 %reshape.155 = f32[1,2,2,128,2,128,2]{4,3,2,1,6,5,0:T(8,128)} reshape(f32[1,4,256,256]{2,1,3,0:T(4,128)} %copy-done.1) | data formatting | bytes 2097152 | tf_op jit(solution)/shard_map/stack | solution.py:79
  221.2 4.2 collective-permute-start.2
  225.4 45.9 %copy.28 = f32[1,2,2,128,2,128,2]{5,3,6,4,2,1,0:T(8,128)} copy(f32[1,2,2,128,2,128,2]{4,3,2,1,6,5,0:T(8,128)} %reshape.155) | data formatting | bytes 2097152 | tf_op jit(solution)/shard_map/stack | solution.py:79
  272.9 8.0 bitcast_add_fusion.3
  282.9 68.5 %reshape.156 = f32[1,2,2,128,2,128,2]{4,3,2,1,6,5,0:T(8,128)} reshape(f32[1,4,256,256]{2,1,3,0:T(4,128)S(1)} %get-tuple-element.15) | data formatting | bytes 2097152 | tf_op jit(solution)/shard_map/stack | solution.py:79
  357.7 46.1 %copy.29 = f32[1,2,2,128,2,128,2]{5,3,6,4,2,1,0:T(8,128)} copy(f32[1,2,2,128,2,128,2]{4,3,2,1,6,5,0:T(8,128)} %reshape.156) | data formatting | bytes 2097152 | tf_op jit(solution)/shard_map/stack | solution.py:79
  409.1 4.2 collective-permute-start.7
  414.6 4.3 collective-permute-start.5
  418.9 5.6 collective-permute-done.8
  424.7 3.4 fusion.12
  428.8 2.8 copy.30
  431.6 203.3 %reshape.144 = f32[3,2,2,128,2,128,2]{6,5,4,3,2,1,0:T(8,128)} reshape(f32[3,4,256,256]{3,2,1,0:T(8,128)} %copy.30) | data formatting | bytes 6291456 | tf_op jit(solution)/shard_map/reshape | solution.py:46
  634.9 60.3 %reduce_sum.29 = f32[3,2,128,128]{3,2,1,0:T(8,128)S(1)} reduce(f32[3,2,2,128,2,128,2]{6,5,4,3,2,1,0:T(8,128)} %reshape.144, f32[]{:T(128)} %constant.24.clone.1), dimensions={2,4,6}, to_apply=%region_2.3 | reduce | flops 688128 | bytes 3538948 | tf_op jit(solution)/shard_map/reduce_sum | solution.py:47
  699.2 68.4 %reshape.143 = f32[2,2,128,2,128,2]{5,4,3,2,1,0:T(8,128)} reshape(f32[4,256,256]{2,1,0:T(8,128)S(1)} %copy.23) | data formatting | bytes 2097152 | tf_op jit(solution)/shard_map/reshape | solution.py:46
  767.6 20.8 %reduce_sum.27 = f32[2,128,128]{2,1,0:T(8,128)S(1)} reduce(f32[2,2,128,2,128,2]{5,4,3,2,1,0:T(8,128)} %reshape.143, f32[]{:T(128)} %constant.24.clone.1), dimensions={1,3,5}, to_apply=%region_0.1 | reduce | flops 229376 | bytes 1179652 | tf_op jit(solution)/shard_map/reduce_sum | solution.py:47
  796.3 6.6 collective-permute-done.11
  803.2 4.5 collective-permute-start.12
  813.0 4.4 collective-permute-start.14
  (145 shorter events, 62.2 us)
Async XLA Ops:
  3.3 269.6 %copy-start = (f32[1,3,4,256,256]{3,2,4,1,0:T(4,128)}, f32[1,3,4,256,256]{3,2,4,1,0:T(4,128)S(1)}, u32[]{:S(2)}) copy-start(f32[1,3,4,256,256]{3,2,4,1,0:T(4,128)S(1)} %copy.21) | copy-start | bytes 9437188
  5.7 128.3 %collective-permute-start.1 = (f32[3,1,256,256]{2,1,3,0:T(1,128)}, f32[3,1,256,256]{2,1,3,0:T(1,128)}, u32[]{:S(2)}, u32[]{:S(2)}) collective-permute-start(f32[3,1,256,256]{2,1,3,0:T(1,128)} %get-tuple-element.25), channel_id=1, source_target_pairs={{0,1},{1,2},{2,3},{3,4},{4,5},{5,6},{6,7},{7,0},{8,9},{9,10},{10,1... | collective-permute-start | bytes 2359304 | tf_op jit(solution)/shard_map/ppermute | solution.py:18
  7.8 126.2 %collective-permute-start = (f32[3,1,256,256]{2,1,3,0:T(1,128)}, f32[3,1,256,256]{2,1,3,0:T(1,128)}, u32[]{:S(2)}, u32[]{:S(2)}) collective-permute-start(f32[3,1,256,256]{2,1,3,0:T(1,128)} %get-tuple-element.24), channel_id=1, source_target_pairs={{1,0},{2,1},{3,2},{4,3},{5,4},{6,5},{7,6},{0,7},{9,8},{10,9},{11,1... | collective-permute-start | bytes 2359304 | tf_op jit(solution)/shard_map/ppermute | solution.py:19
  221.0 51.8 %collective-permute-start.3 = (f32[1,1,256,256]{2,1,3,0:T(1,128)}, f32[1,1,256,256]{2,1,3,0:T(1,128)S(1)}, u32[]{:S(2)}, u32[]{:S(2)}) collective-permute-start(f32[1,1,256,256]{2,1,3,0:T(1,128)} %get-tuple-element.37), channel_id=1, source_target_pairs={{0,1},{1,2},{2,3},{3,4},{4,5},{5,6},{6,7},{7,0},{8,9},{9,10},{10,1... | collective-permute-start | bytes 786440 | tf_op jit(solution)/shard_map/ppermute | solution.py:18
  221.2 51.6 %collective-permute-start.2 = (f32[1,1,256,256]{2,1,3,0:T(1,128)}, f32[1,1,256,256]{2,1,3,0:T(1,128)}, u32[]{:S(2)}, u32[]{:S(2)}) collective-permute-start(f32[1,1,256,256]{2,1,3,0:T(1,128)} %get-tuple-element.36), channel_id=1, source_target_pairs={{1,0},{2,1},{3,2},{4,3},{5,4},{6,5},{7,6},{0,7},{9,8},{10,9},{11,1... | collective-permute-start | bytes 786440 | tf_op jit(solution)/shard_map/ppermute | solution.py:19
  282.9 141.7 %copy-start.4 = (f32[1,4,256,256]{2,1,3,0:T(4,128)}, f32[1,4,256,256]{2,1,3,0:T(4,128)S(1)}, u32[]{:S(2)}) copy-start(f32[1,4,256,256]{2,1,3,0:T(4,128)S(1)} %get-tuple-element.15) | copy-start | bytes 3145732
  357.7 46.1 %copy-start.14 = (f32[1,2,2,128,2,128,2]{5,3,6,4,2,1,0:T(8,128)S(1)}, f32[1,2,2,128,2,128,2]{5,3,6,4,2,1,0:T(8,128)}, u32[]{:S(2)}) copy-start(f32[1,2,2,128,2,128,2]{5,3,6,4,2,1,0:T(8,128)} %copy.28) | copy-start | bytes 3145732
  409.1 15.5 %collective-permute-start.8 = (f32[1,1,256,256]{2,1,3,0:T(1,128)S(1)}, f32[1,1,256,256]{2,1,3,0:T(1,128)S(1)}, u32[]{:S(2)}, u32[]{:S(2)}) collective-permute-start(f32[1,1,256,256]{2,1,3,0:T(1,128)S(1)} %copy-done.29), channel_id=1, source_target_pairs={{0,1},{1,2},{2,3},{3,4},{4,5},{5,6},{6,7},{7,0},{8,9},{9,10},{10,1... | collective-permute-start | bytes 786440 | tf_op jit(solution)/shard_map/ppermute | solution.py:18
  409.1 15.5 %collective-permute-start.7 = (f32[1,1,256,256]{2,1,3,0:T(1,128)S(1)}, f32[1,1,256,256]{2,1,3,0:T(1,128)S(1)}, u32[]{:S(2)}, u32[]{:S(2)}) collective-permute-start(f32[1,1,256,256]{2,1,3,0:T(1,128)S(1)} %copy-done.28), channel_id=1, source_target_pairs={{1,0},{2,1},{3,2},{4,3},{5,4},{6,5},{7,6},{0,7},{9,8},{10,9},{11,1... | collective-permute-start | bytes 786440 | tf_op jit(solution)/shard_map/ppermute | solution.py:19
  413.2 283.7 %collective-permute-start.4 = (f32[4,256,256]{1,0,2:T(4,128)}, f32[4,256,256]{1,0,2:T(4,128)}, u32[]{:S(2)}, u32[]{:S(2)}) collective-permute-start(f32[4,256,256]{1,0,2:T(4,128)} %get-tuple-element.10), channel_id=1, source_target_pairs={{0,8},{1,9},{2,10},{3,11},{4,12},{5,13},{6,14},{7,15},{16,24},{17,... | collective-permute-start | bytes 3145736 | tf_op jit(solution)/shard_map/ppermute | solution.py:27
  414.5 280.6 %collective-permute-start.6 = (f32[3,1,128,128]{3,2,1,0:T(8,128)}, f32[3,1,128,128]{3,2,1,0:T(8,128)}, u32[]{:S(2)}, u32[]{:S(2)}) collective-permute-start(f32[3,1,128,128]{3,2,1,0:T(8,128)} %get-tuple-element.47), channel_id=1, source_target_pairs={{0,1},{1,2},{2,3},{3,4},{4,5},{5,6},{6,7},{7,0},{8,9},{9,10},{10,1... | collective-permute-start | bytes 589832 | tf_op jit(solution)/shard_map/ppermute | solution.py:18
  414.6 280.6 %collective-permute-start.5 = (f32[3,1,128,128]{3,2,1,0:T(8,128)}, f32[3,1,128,128]{3,2,1,0:T(8,128)}, u32[]{:S(2)}, u32[]{:S(2)}) collective-permute-start(f32[3,1,128,128]{3,2,1,0:T(8,128)} %get-tuple-element.46), channel_id=1, source_target_pairs={{1,0},{2,1},{3,2},{4,3},{5,4},{6,5},{7,6},{0,7},{9,8},{10,9},{11,1... | collective-permute-start | bytes 589832 | tf_op jit(solution)/shard_map/ppermute | solution.py:19
  634.8 60.3 %copy-start.22 = (f32[3,2,128,128]{3,2,1,0:T(8,128)S(1)}, f32[3,2,128,128]{3,2,1,0:T(8,128)}, u32[]{:S(2)}) copy-start(f32[3,2,128,128]{3,2,1,0:T(8,128)} %copy-done.21) | copy-start | bytes 1179652
  634.9 60.4 %copy-start.25 = (f32[3,2,128,1]{3,2,1,0:T(8,128)S(1)}, f32[3,2,128,1]{3,2,1,0:T(8,128)}, u32[]{:S(2)}) copy-start(f32[3,2,128,1]{3,2,1,0:T(8,128)} %get-tuple-element.52) | copy-start | bytes 9220
  634.9 60.4 %copy-start.26 = (f32[3,2,128,1]{3,2,1,0:T(8,128)S(1)}, f32[3,2,128,1]{3,2,1,0:T(8,128)}, u32[]{:S(2)}) copy-start(f32[3,2,128,1]{3,2,1,0:T(8,128)} %get-tuple-element.53) | copy-start | bytes 9220
  634.9 60.4 %copy-start.27 = (f32[3,2,128,127]{3,2,1,0:T(8,128)S(1)}, f32[3,2,128,127]{3,2,1,0:T(8,128)}, u32[]{:S(2)}) copy-start(f32[3,2,128,127]{3,2,1,0:T(8,128)} %get-tuple-element.54) | copy-start | bytes 1170436
  698.8 68.8 %copy-start.12 = (f32[4,256,256]{1,0,2:T(4,128)}, f32[4,256,256]{1,0,2:T(4,128)S(1)}, u32[]{:S(2)}) copy-start(f32[4,256,256]{1,0,2:T(4,128)S(1)} %bitcast_select_fusion) | copy-start | bytes 3145732
  788.7 6.0 collective-permute-start.10
  791.0 3.8 collective-permute-start.9
  795.0 7.9 collective-permute-start.11
  803.1 6.8 collective-permute-start.13
  803.2 6.7 collective-permute-start.12
  813.0 9.6 %collective-permute-start.15 = (f32[1,1,128,128]{3,2,1,0:T(8,128)}, f32[1,1,128,128]{3,2,1,0:T(8,128)}, u32[]{:S(2)}, u32[]{:S(2)}) collective-permute-start(f32[1,1,128,128]{3,2,1,0:T(8,128)} %get-tuple-element.66), channel_id=1, source_target_pairs={{0,1},{1,2},{2,3},{3,4},{4,5},{5,6},{6,7},{7,0},{8,9},{9,10},{10,1... | collective-permute-start | bytes 196616 | tf_op jit(solution)/shard_map/ppermute | solution.py:18
  813.0 9.6 %collective-permute-start.14 = (f32[1,1,128,128]{3,2,1,0:T(8,128)}, f32[1,1,128,128]{3,2,1,0:T(8,128)}, u32[]{:S(2)}, u32[]{:S(2)}) collective-permute-start(f32[1,1,128,128]{3,2,1,0:T(8,128)} %get-tuple-element.65), channel_id=1, source_target_pairs={{1,0},{2,1},{3,2},{4,3},{5,4},{6,5},{7,6},{0,7},{9,8},{10,9},{11,1... | collective-permute-start | bytes 196616 | tf_op jit(solution)/shard_map/ppermute | solution.py:19
  (22 other events, 221.0 us)
where the time goes:
time: 844 us; the launch traced here: 830 us
  local copies, waits for them, and re-layouts  660 us (78%)
  other arithmetic  119 us (14%)
  starting transfers between devices  33.7 us (4%)
  waiting for transfers between devices  16.4 us (2%)
    another operation x6, local copies, waits for them, and re-layouts, local(): coarse_nodes = restrict(jnp.stack([current[0], node_one, node_two]))  345 us
    reshape x2, local copies, waits for them, and re-layouts, restrict(): field.reshape(shape[:-3] + (shape[-3] // 2, 2, shape[-2] // 2, 2, shape[-...  272 us
    reduce_sum x3, other arithmetic, restrict(): return jnp.mean(blocks, axis=(-5, -3, -1))  82.5 us
    ppermute x7, starting transfers between devices, padded_2(): after = lax.ppermute(leading, axis, down)  26.5 us
  transfers between devices with their start and end apart: 16, of which 5 were waited for; matrix products, arithmetic and copies ran while one was open for 54% of the time, Pallas kernels for 0%

commit v1 on v0

v1 whole, which is shorter than its diff:
```python
import jax
import jax.numpy as jnp
from jax import lax
from jax.experimental import pallas as pl
from jax.experimental.pallas import tpu as pltpu
from jax.sharding import PartitionSpec as P

DIFFUSE = 0.12
COARSE = DIFFUSE / 4.0
GROWTH = 0.5
WEIGHTS = ((5.0 / 24.0, 1.0 / 3.0, -1.0 / 24.0), (-1.0 / 24.0, 1.0 / 3.0, 5.0 / 24.0))
SECOND = (WEIGHTS[1][0], WEIGHTS[1][1] - 0.5, WEIGHTS[1][2])
LANES = 128
F32 = jnp.float32
BF16 = jnp.bfloat16
VMEM_LIMIT = 32 * 1024 * 1024


def combine(weights, parts):
    return weights[0] * parts[0] + weights[1] * parts[1] + weights[2] * parts[2]


def cube(v):
    return v * v * v


def z_neighbours(halves):
    count = len(halves)
    lane = lax.broadcasted_iota(jnp.int32, halves[0].shape, 1)
    fwd = [pltpu.roll(v, 1, 1) for v in halves]
    back = [pltpu.roll(v, LANES - 1, 1) for v in halves]
    out = []
    for k in range(count):
        before = jnp.where(lane == 0, fwd[(k - 1) % count], fwd[k])
        after = jnp.where(lane == LANES - 1, back[(k + 1) % count], back[k])
        out.append(before + after)
    return out


def y_neighbours(other, parity):
    rows = other.shape[0]
    return other + pltpu.roll(other, 1 if parity == 0 else rows - 1, 0)


def laplace_planes(ref, plane, planes, halves):
    for parity in range(2):
        own = [ref[plane, h, parity] for h in range(halves)]
        side = z_neighbours(own)
        for h in range(halves):
            total = side[h] + y_neighbours(ref[plane, h, 1 - parity], parity) - 6.0 * own[h]
            if plane > 0:
                total = total + ref[plane - 1, h, parity]
            if plane < planes - 1:
                total = total + ref[plane + 1, h, parity]
            yield h, parity, own[h], total


def coarse_force(field):
    planes = len(field)
    out = []
    for p in range(planes):
        v = field[p]
        rows, lanes = v.shape
        total = pltpu.roll(v, 1, 0) + pltpu.roll(v, rows - 1, 0)
        total = total + pltpu.roll(v, 1, 1) + pltpu.roll(v, lanes - 1, 1) - 6.0 * v
        if p > 0:
            total = total + field[p - 1]
        if p < planes - 1:
            total = total + field[p + 1]
        out.append(COARSE * total + GROWTH * (v - cube(v)))
    return out


def split(v):
    high = v.astype(BF16)
    low = (v - high.astype(F32)).astype(BF16)
    return high, low


def pair_matrix(size):
    row = lax.broadcasted_iota(jnp.int32, (size, size // 2), 0)
    col = lax.broadcasted_iota(jnp.int32, (size, size // 2), 1)
    offset = lax.rem(row - 2 * col + size, size)
    inner = offset < 2
    outer = (offset == 2) | (offset == size - 1)
    sums = jnp.where(inner, 1.0, 0.0).astype(F32)
    bends = jnp.where(outer, 1.0, 0.0).astype(F32) - sums
    return sums.astype(BF16), bends.astype(BF16)


def spread_matrix(size):
    row = lax.broadcasted_iota(jnp.int32, (size, 2 * size), 0)
    col = lax.broadcasted_iota(jnp.int32, (size, 2 * size), 1)
    return jnp.where((col == 2 * row) | (col == 2 * row + 1), 1.0, 0.0).astype(F32).astype(BF16)


def times(v, matrix):
    high, low = split(v)
    return jnp.dot(high, matrix, preferred_element_type=F32) + jnp.dot(
        low, matrix, preferred_element_type=F32
    )


def restrict_field(ref, planes, halves):
    size = halves * LANES
    sums, bends = pair_matrix(size)

    def y_sum(p):
        return [ref[p, h, 0] + ref[p, h, 1] for h in range(halves)]

    means, forces = [], []
    flat = [y_sum(p) for p in range(planes)]
    for top in range(0, planes, 2):
        total, rest = [], []
        for h in range(halves):
            even = ref[top, h, 0] + ref[top + 1, h, 0]
            odd = ref[top, h, 1] + ref[top + 1, h, 1]
            both = even + odd
            rows = both.shape[0]
            flux = pltpu.roll(odd, 1, 0) + pltpu.roll(even, rows - 1, 0) - 2.0 * both
            if top > 0:
                flux = flux + flat[top - 1][h]
            if top + 2 < planes:
                flux = flux + flat[top + 2][h]
            cubes = cube(ref[top, h, 0]) + cube(ref[top + 1, h, 0])
            cubes = cubes + cube(ref[top, h, 1]) + cube(ref[top + 1, h, 1])
            total.append(both)
            rest.append(DIFFUSE * flux + GROWTH * (both - cubes))
        total = jnp.concatenate(total, axis=1)
        rest = jnp.concatenate(rest, axis=1)
        means.append(times(total, sums) * 0.125)
        forces.append((times(rest, sums) + DIFFUSE * times(total, bends)) * 0.125)
    edges = [times(jnp.concatenate(flat[p], axis=1), sums) for p in (0, planes - 1)]
    return means, forces, edges


def store_coarse(out, means, forces, edges):
    for k, parts in enumerate((means, forces, edges)):
        for p, v in enumerate(parts):
            out[k, p] = v


def edge_kernel(nodes, first, last, held, sem):
    planes, halves = nodes.shape[2], held.shape[2]
    copies = []
    for e, p in enumerate((0, planes - 1)):
        for m in range(3):
            for h in range(halves):
                copies.append(
                    pltpu.make_async_copy(
                        nodes.at[0, m, p, :, pl.ds(h * LANES, LANES)],
                        held.at[e, m, h],
                        sem.at[e, m, h],
                    )
                )
    for copy in copies:
        copy.start()
    for copy in copies:
        copy.wait()
    rows = first.shape[2]
    for e, out in enumerate((first, last)):
        for h in range(halves):
            for q in range(2):
                parts = [held[e, m, h, pl.ds(q, rows, stride=2), :] for m in range(3)]
                out[h, q] = combine(WEIGHTS[0], parts)


def first_kernel(nodes, one, slope, rest, edge_low, edge_high, coarse, held, start, mix, sem):
    planes, halves = nodes.shape[2], held.shape[2]
    rows = one.shape[3]
    copies = [
        [
            pltpu.make_async_copy(
                nodes.at[0, m, p, :, pl.ds(h * LANES, LANES)], held.at[m, p, h], sem.at[m, p, h]
            )
            for m in range(3)
            for h in range(halves)
        ]
        for p in range(planes)
    ]
    for group in copies:
        for copy in group:
            copy.start()
    for p in range(planes):
        for copy in copies[p]:
            copy.wait()
        for h in range(halves):
            for q in range(2):
                parts = [held[m, p, h, pl.ds(q, rows, stride=2), :] for m in range(3)]
                cubes = [cube(v) for v in parts]
                a = combine(WEIGHTS[0], parts)
                d = combine(SECOND, parts)
                start[p, h, q] = parts[0]
                mix[p, h, q] = a
                slope[p, h, q] = d
                one[p, h, q] = parts[0] + GROWTH * (a - combine(WEIGHTS[0], cubes))
                rest[p, h, q] = GROWTH * (d - combine(SECOND, cubes))
    for p in range(planes):
        for h, q, _, laplace in laplace_planes(mix, p, planes, halves):
            value = one[p, h, q] + DIFFUSE * laplace
            one[p, h, q] = value
            if p == 0:
                edge_low[h, q] = 0.5 * value + slope[p, h, q]
            if p == planes - 1:
                edge_high[h, q] = 0.5 * value + slope[p, h, q]
    store_coarse(coarse, *restrict_field(start, planes, halves))


def second_kernel(one_in, slope, rest, low, high, own_low, own_high, one, two, coarse, mix):
    planes, halves = one_in.shape[0], one_in.shape[1]
    for p in range(planes):
        for h in range(halves):
            for q in range(2):
                value = one_in[p, h, q]
                if p == 0:
                    value = value + DIFFUSE * low[h, q]
                if p == planes - 1:
                    value = value + DIFFUSE * high[h, q]
                one[p, h, q] = value
                mix[p, h, q] = 0.5 * value + slope[p, h, q]
    for p in range(planes):
        for h, q, _, laplace in laplace_planes(mix, p, planes, halves):
            if p == 0:
                laplace = laplace + (0.5 * DIFFUSE) * own_low[h, q]
            if p == planes - 1:
                laplace = laplace + (0.5 * DIFFUSE) * own_high[h, q]
            value = one[p, h, q]
            two[p, h, q] = (
                value + DIFFUSE * laplace + (0.5 * GROWTH) * (value - cube(value)) + rest[p, h, q]
            )
    store_coarse(coarse, *restrict_field(one, planes, halves))


def third_kernel(two_in, low, high, coarse_zero, coarse_one, two, send_low, send_high, work):
    planes, halves = two_in.shape[0], two_in.shape[1]
    later = lax.axis_index("tm").astype(F32)
    for p in range(planes):
        for h in range(halves):
            for q in range(2):
                value = two_in[p, h, q]
                if p == 0:
                    value = value + DIFFUSE * low[h, q]
                if p == planes - 1:
                    value = value + DIFFUSE * high[h, q]
                two[p, h, q] = value
    means_two, forces_two, edges_two = restrict_field(two, planes, halves)
    half = planes // 2
    zero = [coarse_zero[0, p] for p in range(half)]
    mean_one = [coarse_one[0, p] for p in range(half)]
    force_zero = coarse_force(zero)
    force_one = coarse_force(mean_one)
    sweep_zero, sweep_one = [], []
    for p in range(half):
        parts = (coarse_zero[1, p], coarse_one[1, p], forces_two[p])
        sweep_zero.append(combine(WEIGHTS[0], parts))
        sweep_one.append(combine(WEIGHTS[1], parts))
    for e, (p, out) in enumerate(((0, send_low), (half - 1, send_high))):
        parts = (coarse_zero[2, e], coarse_one[2, e], edges_two[e])
        partial = sweep_zero[p] - mean_one[p] + (1.0 - later) * zero[p] - (0.5 * later) * force_zero[p]
        out[0] = (DIFFUSE / 8.0) * combine(WEIGHTS[0], parts) - (0.5 * COARSE * later) * zero[p]
        out[1] = (DIFFUSE / 8.0) * combine(WEIGHTS[1], parts) + (0.5 * COARSE) * partial
    for p in range(half):
        work[0, p] = zero[p]
        work[1, p] = mean_one[p]
        work[2, p] = means_two[p]
        work[3, p] = sweep_zero[p] - 0.5 * force_zero[p]
        work[4, p] = sweep_one[p] - 0.5 * force_one[p]


def coarse_chain(first, first_low, first_high, bend_low, bend_high, work, low, high, own_low, own_high):
    half = len(first)
    force = coarse_force(first)
    one = []
    for p in range(half):
        v = first[p] + 0.5 * force[p] + work[3, p]
        if p == 0:
            v = v + low[0] + first_low
        if p == half - 1:
            v = v + high[0] + first_high
        one.append(v)
    force = coarse_force(one)
    two = []
    for p in range(half):
        v = one[p] + 0.5 * force[p] + work[4, p]
        if p == 0:
            v = v + low[1] + (0.5 * COARSE) * (own_low[0] + bend_low)
        if p == half - 1:
            v = v + high[1] + (0.5 * COARSE) * (own_high[0] + bend_high)
        two.append(v)
    return one, two


def fourth_kernel(work, low, high, own_low, own_high, partner, send_low, send_high):
    half = work.shape[1]
    first = [work[0, p] for p in range(half)]
    one, two = coarse_chain(first, 0.0, 0.0, 0.0, 0.0, work, low, high, own_low, own_high)
    force = coarse_force(two)
    for p in range(half):
        partner[0, p] = two[p]
        partner[1, p] = two[p] - work[2, p]
    for p, out in ((0, send_low), (half - 1, send_high)):
        out[0] = two[p]
        out[1] = two[p] + 0.5 * force[p]


def last_kernel(
    nodes, one, two, moved, work, low, high, own_low, own_high, partner, ring_low, ring_high,
    updated, held, result, load_sem, store_sem,
):
    planes, halves = one.shape[0], one.shape[1]
    rows = one.shape[3]
    half = planes // 2
    section = lax.axis_index("tm")
    later = section.astype(F32)
    loads = [
        pltpu.make_async_copy(
            nodes.at[0, 0, :, :, pl.ds(h * LANES, LANES)], held.at[:, h], load_sem.at[h]
        )
        for h in range(halves)
    ]
    for copy in loads:
        copy.start()
    first, change = [], []
    for p in range(half):
        first.append(jnp.where(section == 0, work[0, p], partner[0, p]))
        change.append(jnp.where(section == 0, first[p] - work[0, p], partner[1, p]))
    scale = 0.5 * COARSE
    coarse_one, coarse_two = coarse_chain(
        first,
        (scale * later) * ring_low[0],
        (scale * later) * ring_high[0],
        later * (ring_low[1] + scale * first[0]),
        later * (ring_high[1] + scale * first[half - 1]),
        work, low, high, own_low, own_high,
    )
    spread = spread_matrix(LANES * halves // 2)
    stores = []

    def put(node, p):
        for h in range(halves):
            copy = pltpu.make_async_copy(
                result.at[node, p, h],
                updated.at[0, node, p, :, pl.ds(h * LANES, LANES)],
                store_sem.at[node, p, h],
            )
            copy.start()
            stores.append(copy)

    for node, base in ((1, one), (2, two)):
        for top in range(half):
            diff = (coarse_one[top] if node == 1 else coarse_two[top]) - work[node, top]
            wide = times(diff, spread)
            for p in (2 * top, 2 * top + 1):
                for h in range(halves):
                    for q in range(2):
                        result[node, p, h, pl.ds(q, rows, stride=2), :] = (
                            base[p, h, q] + wide[:, h * LANES : (h + 1) * LANES]
                        )
                put(node, p)
    for copy in loads:
        copy.wait()
    for top in range(half):
        wide = times(change[top], spread)
        for p in (2 * top, 2 * top + 1):
            for h in range(halves):
                for q in range(2):
                    own = held[p, h, pl.ds(q, rows, stride=2), :]
                    start = jnp.where(section == 0, own, moved[p, h, q])
                    result[0, p, h, pl.ds(q, rows, stride=2), :] = (
                        start + wide[:, h * LANES : (h + 1) * LANES]
                    )
            put(0, p)
    for copy in stores:
        copy.wait()


def call(kernel, name, inputs, any_inputs, outs, scratch=(), any_out=False, flops=0, size=0):
    vmem = pl.BlockSpec(memory_space=pltpu.VMEM)
    hbm = pl.BlockSpec(memory_space=pl.ANY)
    return pl.pallas_call(
        kernel,
        name=name,
        out_shape=[jax.ShapeDtypeStruct(s, F32) for s in outs],
        in_specs=[hbm if k < any_inputs else vmem for k in range(len(inputs))],
        out_specs=[hbm if any_out else vmem for _ in outs],
        scratch_shapes=list(scratch),
        compiler_params=pltpu.CompilerParams(vmem_limit_bytes=VMEM_LIMIT),
        cost_estimate=pl.CostEstimate(flops=flops, bytes_accessed=size, transcendentals=0),
    )(*inputs)


def exchange(low, high, axis):
    peers = lax.axis_size(axis)
    up = [(i, (i + 1) % peers) for i in range(peers)]
    down = [(j, i) for i, j in up]
    return lax.ppermute(high, axis, up), lax.ppermute(low, axis, down)


def local(nodes):
    _, _, planes, ny, nz = nodes.shape
    halves, rows, half = nz // LANES, ny // 2, planes // 2
    plane = (halves, 2, rows, LANES)
    field = (planes,) + plane
    quarter = (rows, nz // 2)
    pair = (2,) + quarter
    packed = (3, half) + quarter
    size = planes * ny * nz * 4

    a_low, a_high = call(
        edge_kernel, "edge_mix", (nodes,), 1, [plane, plane],
        [pltpu.VMEM((2, 3, halves, ny, LANES), F32), pltpu.SemaphoreType.DMA((2, 3, halves))],
        size=size * 2, flops=size,
    )
    a_below, a_above = exchange(a_low, a_high, "space")
    one_part, slope, rest, b_low, b_high, coarse_zero = call(
        first_kernel, "first_stage", (nodes,), 1, [field, field, field, plane, plane, packed],
        [
            pltpu.VMEM((3, planes, halves, ny, LANES), F32),
            pltpu.VMEM(field, F32),
            pltpu.VMEM(field, F32),
            pltpu.SemaphoreType.DMA((3, planes, halves)),
        ],
        size=size * 6, flops=size * 10,
    )
    b_below, b_above = exchange(b_low, b_high, "space")
    one, two_part, coarse_mid = call(
        second_kernel, "second_stage",
        (one_part, slope, rest, a_below, a_above, a_low, a_high), 0,
        [field, field, packed], [pltpu.VMEM(field, F32)],
        size=size * 6, flops=size * 10,
    )
    two, h_low, h_high, work = call(
        third_kernel, "third_stage", (two_part, b_below, b_above, coarse_zero, coarse_mid), 0,
        [field, pair, pair, (5, half) + quarter],
        size=size * 3, flops=size * 5,
    )
    below, above = exchange(h_low, h_high, "space")
    moved = lax.ppermute(two, "tm", [(0, 1)])
    partner, f_low, f_high = call(
        fourth_kernel, "coarse_chain", (work, below, above, h_low, h_high), 0,
        [(2, half) + quarter, pair, pair],
        size=size, flops=size,
    )
    peers = lax.axis_size("space")
    to_above = [(i, peers + (i + 1) % peers) for i in range(peers)]
    to_below = [(i, peers + (i - 1) % peers) for i in range(peers)]
    ring_below = lax.ppermute(f_high, ("tm", "space"), to_above)
    ring_above = lax.ppermute(f_low, ("tm", "space"), to_below)
    partner = lax.ppermute(partner, "tm", [(0, 1)])
    updated, = call(
        last_kernel, "update",
        (nodes, one, two, moved, work, below, above, h_low, h_high, partner, ring_below, ring_above),
        1, [(1, 3, planes, ny, nz)],
        [
            pltpu.VMEM((planes, halves, ny, LANES), F32),
            pltpu.VMEM((3, planes, halves, ny, LANES), F32),
            pltpu.SemaphoreType.DMA((halves,)),
            pltpu.SemaphoreType.DMA((3, planes, halves)),
        ],
        any_out=True, size=size * 6, flops=size * 5,
    )
    return updated


def solution(mesh):
    in_specs = (P(("groups", "tm"), None, "space", None, None),)
    out_specs = P(("groups", "tm"), None, "space", None, None)
    return jax.shard_map(local, mesh=mesh, in_specs=in_specs, out_specs=out_specs, check_vma=False)
```

time: 844 us -> 54.5 us (0.06); the launches traced: 830 us -> 54.3 us
  local copies, waits for them, and re-layouts: 660 us -> 1.89 us
  other arithmetic: 119 us -> 0 us
  starting transfers between devices: 33.7 us -> 18.8 us
  waiting for transfers between devices: 16.4 us -> 25.2 us
    another operation x7 -> x0, local copies, waits for them, and re-layouts: 348 us -> none  [the longest x6 345 us: local(): coarse_nodes = restrict(jnp.stack([current[0], node_one, node_two]))]
    reshape x5 -> x0, local copies, waits for them, and re-layouts: 274 us -> none  [the longest x2 272 us: restrict(): field.reshape(shape[:-3] + (shape[-3] // 2, 2, shape[-2] // 2, 2, shape[-...]
    reduce_sum x3 -> x0, other arithmetic: 82.5 us -> none  [restrict(): return jnp.mean(blocks, axis=(-5, -3, -1))]
    slice x36 -> x0, local copies, waits for them, and re-layouts: 30.2 us -> none  [the longest x14 11.8 us: padded_force(): laplace = laplace + jnp.roll(center, 1, -2) + jnp.roll(center, -1, -2)]
    add x8 -> x0, other arithmetic: 27.9 us -> none  [the longest x2 14.5 us: padded_force(): return coeff * laplace + GROWTH * (center - center * center * center)]
    ppermute x16 -> x10, starting transfers between devices: 33.7 us -> 18.8 us  [the longest x6 13.6 us: exchange(): return (lax.ppermute(high, axis, up), lax.ppermute(low, axis, down))]
    ppermute x16 -> x10, waiting for transfers between devices: 16.4 us -> 25.2 us  [the longest x6 17.4 us: exchange(): return (lax.ppermute(high, axis, up), lax.ppermute(low, axis, down))]
  transfers between devices with their start and end apart: 16 -> 10, of which waited for: 5 -> 8; matrix products, arithmetic and copies ran while one was open for 54% -> 0% of each run, Pallas kernels for 0% -> 9%
where the time goes in v1:
time: 54.5 us; the launch traced here: 54.3 us
  waiting for transfers between devices  25.2 us (46%)
  starting transfers between devices  18.8 us (34%)
  Pallas kernels  8.27 us (15%)
  local copies, waits for them, and re-layouts  1.89 us (3%)
    ppermute x6, waiting for transfers between devices, exchange(): return (lax.ppermute(high, axis, up), lax.ppermute(low, axis, down))  17.4 us
    ppermute x6, starting transfers between devices, exchange(): return (lax.ppermute(high, axis, up), lax.ppermute(low, axis, down))  13.6 us
    pallas_call x6, Pallas kernels, call(): pl.pallas_call(kernel, name=name, out_shape=[jax.ShapeDtypeStruct(s, F32)...  8.27 us
    ppermute x1, waiting for transfers between devices, local(): ring_below = lax.ppermute(f_high, ('tm', 'space'), to_above)  6.49 us
    unnamed x4, local copies, waits for them, and re-layouts  1.89 us
    ppermute x1, waiting for transfers between devices, local(): ring_above = lax.ppermute(f_low, ('tm', 'space'), to_below)  1.3 us
    ppermute x1, starting transfers between devices, local(): moved = lax.ppermute(two, 'tm', [(0, 1)])  1.29 us
    ppermute x1, starting transfers between devices, local(): partner = lax.ppermute(partner, 'tm', [(0, 1)])  1.29 us
  transfers between devices with their start and end apart: 10, of which 8 were waited for; matrix products, arithmetic and copies ran while one was open for 0% of the time, Pallas kernels for 9%

profile of v1, /device:TPU:1, one launch (start us, length us, event | category | flops | bytes accessed | tf_op | source)
XLA Modules:
  0.0 54.3 jit_solution(5325626848658503046)
XLA Ops:
  0.0 1.9 %copy-done = f32[1,3,4,256,256]{4,3,2,1,0:T(8,128)S(1)} copy-done((f32[1,3,4,256,256]{4,3,2,1,0:T(8,128)S(1)}, f32[1,3,4,256,256]{4,3,2,1,0:T(8,128)}, u32[]{:S(2)}) %copy-start) | copy-done | bytes 3145752
  1.9 0.4 edge_mix.1
  2.3 2.1 %collective-permute-start = (f32[2,2,128,128]{3,2,1,0:T(8,128)S(1)}, f32[2,2,128,128]{3,2,1,0:T(8,128)S(1)}, u32[]{:S(2)}, u32[]{:S(2)}) collective-permute-start(f32[2,2,128,128]{3,2,1,0:T(8,128)S(1)} %get-tuple-element.26.own_high), channel_id=1, source_target_pairs={{0,1},{1,2},{2,3},{3,4},{4,5},{5,6},{6,7},{7,0},{8,9},{9,10},{10,1... | collective-permute-start | bytes 786440 | tf_op jit(solution)/shard_map/ppermute | solution.py:396
  4.4 3.1 %collective-permute-start.1 = (f32[2,2,128,128]{3,2,1,0:T(8,128)S(1)}, f32[2,2,128,128]{3,2,1,0:T(8,128)S(1)}, u32[]{:S(2)}, u32[]{:S(2)}) collective-permute-start(f32[2,2,128,128]{3,2,1,0:T(8,128)S(1)} %get-tuple-element.27.own_low), channel_id=1, source_target_pairs={{1,0},{2,1},{3,2},{4,3},{5,4},{6,5},{7,6},{0,7},{9,8},{10,9},{11,1... | collective-permute-start | bytes 786440 | tf_op jit(solution)/shard_map/ppermute | solution.py:396
  7.5 2.8 %first_stage.1 = (f32[4,2,2,128,128]{4,3,2,1,0:T(8,128)S(1)}, f32[4,2,2,128,128]{4,3,2,1,0:T(8,128)S(1)}, f32[4,2,2,128,128]{4,3,2,1,0:T(8,128)S(1)}, f32[2,2,12...) custom-call(f32[1,3,4,256,256]{4,3,2,1,0:T(8,128)S(1)} %copy-done), custom_call_target="tpu_custom_call" | custom-call | flops 10485760 | bytes 6291456 | tf_op jit(solution)/shard_map/first_stage/pallas_call | solution.py:380
  10.4 4.1 %collective-permute-start.3 = (f32[2,2,128,128]{3,2,1,0:T(8,128)S(1)}, f32[2,2,128,128]{3,2,1,0:T(8,128)S(1)}, u32[]{:S(2)}, u32[]{:S(2)}) collective-permute-start(f32[2,2,128,128]{3,2,1,0:T(8,128)S(1)} %get-tuple-element.31), channel_id=1, source_target_pairs={{1,0},{2,1},{3,2},{4,3},{5,4},{6,5},{7,6},{0,7},{9,8},{10,9},{11,1... | collective-permute-start | bytes 786440 | tf_op jit(solution)/shard_map/ppermute | solution.py:396
  14.6 6.0 %collective-permute-done.low = f32[2,2,128,128]{3,2,1,0:T(8,128)S(1)} collective-permute-done((f32[2,2,128,128]{3,2,1,0:T(8,128)S(1)}, f32[2,2,128,128]{3,2,1,0:T(8,128)S(1)}, u32[]{:S(2)}, u32[]{:S(2)}) %collective-permute-start) | collective-permute-done | bytes 262176 | tf_op jit(solution)/shard_map/ppermute | solution.py:396
  20.6 1.9 %collective-permute-done.1.high = f32[2,2,128,128]{3,2,1,0:T(8,128)S(1)} collective-permute-done((f32[2,2,128,128]{3,2,1,0:T(8,128)S(1)}, f32[2,2,128,128]{3,2,1,0:T(8,128)S(1)}, u32[]{:S(2)}, u32[]{:S(2)}) %collective-permute-start.1) | collective-permute-done | bytes 262176 | tf_op jit(solution)/shard_map/ppermute | solution.py:396
  22.5 1.5 %second_stage.1 = (f32[4,2,2,128,128]{4,3,2,1,0:T(8,128)S(1)}, f32[4,2,2,128,128]{4,3,2,1,0:T(8,128)S(1)}, f32[3,2,128,128]{3,2,1,0:T(8,128)S(1)}) custom-call(f32[4,2,2,128,128]{4,3,2,1,0:T(8,128)S(1)} %get-tuple-element.23.one_in, f32[4,2,2,128,128]{4,3,2,1,0:T(8,128)S(1)} %get-tuple-element.24.slope, f32[4,2,2,128,128]{4,3,2,1,0:T(8,128)S(1)} %get-tuple-element.25.rest, ...), custom_call_target="tpu_custom_call" | custom-call | flops 10485760 | bytes 6291456 | tf_op jit(solution)/shard_map/second_stage/pallas_call | solution.py:380
  24.0 2.2 %collective-permute-done.2.low = f32[2,2,128,128]{3,2,1,0:T(8,128)S(1)} collective-permute-done((f32[2,2,128,128]{3,2,1,0:T(8,128)S(1)}, f32[2,2,128,128]{3,2,1,0:T(8,128)S(1)}, u32[]{:S(2)}, u32[]{:S(2)}) %collective-permute-start.2) | collective-permute-done | bytes 262176 | tf_op jit(solution)/shard_map/ppermute | solution.py:396
  26.2 1.9 %collective-permute-done.3.high = f32[2,2,128,128]{3,2,1,0:T(8,128)S(1)} collective-permute-done((f32[2,2,128,128]{3,2,1,0:T(8,128)S(1)}, f32[2,2,128,128]{3,2,1,0:T(8,128)S(1)}, u32[]{:S(2)}, u32[]{:S(2)}) %collective-permute-start.3) | collective-permute-done | bytes 262176 | tf_op jit(solution)/shard_map/ppermute | solution.py:396
  28.1 0.9 %third_stage.1 = (f32[4,2,2,128,128]{4,3,2,1,0:T(8,128)S(1)}, f32[2,128,128]{2,1,0:T(8,128)S(1)}, f32[2,128,128]{2,1,0:T(8,128)S(1)}, f32[5,2,128,128]{3,2,1,0:T(8,128)S(1)}) custom-call(f32[4,2,2,128,128]{4,3,2,1,0:T(8,128)S(1)} %get-tuple-element.29.two_in, f32[2,2,128,128]{3,2,1,0:T(8,128)S(1)} %collective-permute-done.2.low, ...), custom_call_target="tpu_custom_call" | custom-call | flops 5242880 | bytes 3145728 | tf_op jit(solution)/shard_map/third_stage/pallas_call | solution.py:380
  29.0 1.3 %collective-permute-start.4 = (f32[4,2,2,128,128]{4,3,2,1,0:T(8,128)S(1)}, f32[4,2,2,128,128]{4,3,2,1,0:T(8,128)S(1)}, u32[]{:S(2)}, u32[]{:S(2)}) collective-permute-start(f32[4,2,2,128,128]{4,3,2,1,0:T(8,128)S(1)} %get-tuple-element.34.two), channel_id=1, source_target_pairs={{0,8},{1,9},{2,10},{3,11},{4,12},{5,13},{6,14},{7,15},{16,24},{17,... | collective-permute-start | bytes 3145736 | tf_op jit(solution)/shard_map/ppermute | solution.py:438
  30.3 0.4 collective-permute-start.5
  30.7 3.8 %collective-permute-start.6 = (f32[2,128,128]{2,1,0:T(8,128)S(1)}, f32[2,128,128]{2,1,0:T(8,128)S(1)}, u32[]{:S(2)}, u32[]{:S(2)}) collective-permute-start(f32[2,128,128]{2,1,0:T(8,128)S(1)} %get-tuple-element.37.own_low), channel_id=1, source_target_pairs={{1,0},{2,1},{3,2},{4,3},{5,4},{6,5},{7,6},{0,7},{9,8},{10,9},{11,1... | collective-permute-start | bytes 393224 | tf_op jit(solution)/shard_map/ppermute | solution.py:396
  34.5 2.5 %collective-permute-done.5.low = f32[2,128,128]{2,1,0:T(8,128)S(1)} collective-permute-done((f32[2,128,128]{2,1,0:T(8,128)S(1)}, f32[2,128,128]{2,1,0:T(8,128)S(1)}, u32[]{:S(2)}, u32[]{:S(2)}) %collective-permute-start.5) | collective-permute-done | bytes 131104 | tf_op jit(solution)/shard_map/ppermute | solution.py:396
  37.0 2.9 %collective-permute-done.6.high = f32[2,128,128]{2,1,0:T(8,128)S(1)} collective-permute-done((f32[2,128,128]{2,1,0:T(8,128)S(1)}, f32[2,128,128]{2,1,0:T(8,128)S(1)}, u32[]{:S(2)}, u32[]{:S(2)}) %collective-permute-start.6) | collective-permute-done | bytes 131104 | tf_op jit(solution)/shard_map/ppermute | solution.py:396
  39.9 0.4 coarse_chain.1
  40.3 1.3 %collective-permute-start.7 = (f32[2,2,128,128]{3,2,1,0:T(8,128)S(1)}, f32[2,2,128,128]{3,2,1,0:T(8,128)S(1)}, u32[]{:S(2)}, u32[]{:S(2)}) collective-permute-start(f32[2,2,128,128]{3,2,1,0:T(8,128)S(1)} %get-tuple-element.38), channel_id=1, source_target_pairs={{0,8},{1,9},{2,10},{3,11},{4,12},{5,13},{6,14},{7,15},{16,24},{17,... | collective-permute-start | bytes 786440 | tf_op jit(solution)/shard_map/ppermute | solution.py:449
  41.6 1.3 %collective-permute-start.8 = (f32[2,128,128]{2,1,0:T(8,128)S(1)}, f32[2,128,128]{2,1,0:T(8,128)S(1)}, u32[]{:S(2)}, u32[]{:S(2)}) collective-permute-start(f32[2,128,128]{2,1,0:T(8,128)S(1)} %get-tuple-element.39), channel_id=1, source_target_pairs={{0,9},{1,10},{2,11},{3,12},{4,13},{5,14},{6,15},{7,8},{16,25},{17,... | collective-permute-start | bytes 393224 | tf_op jit(solution)/shard_map/ppermute | solution.py:447
  42.9 1.3 %collective-permute-start.9 = (f32[2,128,128]{2,1,0:T(8,128)S(1)}, f32[2,128,128]{2,1,0:T(8,128)S(1)}, u32[]{:S(2)}, u32[]{:S(2)}) collective-permute-start(f32[2,128,128]{2,1,0:T(8,128)S(1)} %get-tuple-element.40), channel_id=1, source_target_pairs={{0,15},{1,8},{2,9},{3,10},{4,11},{5,12},{6,13},{7,14},{16,31},{17,... | collective-permute-start | bytes 393224 | tf_op jit(solution)/shard_map/ppermute | solution.py:448
  44.2 6.5 %collective-permute-done.8.ring_low = f32[2,128,128]{2,1,0:T(8,128)S(1)} collective-permute-done((f32[2,128,128]{2,1,0:T(8,128)S(1)}, f32[2,128,128]{2,1,0:T(8,128)S(1)}, u32[]{:S(2)}, u32[]{:S(2)}) %collective-permute-start.8) | collective-permute-done | bytes 131104 | tf_op jit(solution)/shard_map/ppermute | solution.py:447
  50.7 1.3 %collective-permute-done.9.ring_high = f32[2,128,128]{2,1,0:T(8,128)S(1)} collective-permute-done((f32[2,128,128]{2,1,0:T(8,128)S(1)}, f32[2,128,128]{2,1,0:T(8,128)S(1)}, u32[]{:S(2)}, u32[]{:S(2)}) %collective-permute-start.9) | collective-permute-done | bytes 131104 | tf_op jit(solution)/shard_map/ppermute | solution.py:448
  52.0 2.3 %update.1 = f32[1,3,4,256,256]{4,3,2,1,0:T(8,128)} custom-call(f32[1,3,4,256,256]{4,3,2,1,0:T(8,128)S(1)} %copy-done.1, f32[4,2,2,128,128]{4,3,2,1,0:T(8,128)S(1)} %get-tuple-element.28.one, f32[4,2,2,128,128]{4,3,2,1,0:T(8,128)S(1)} %get-tuple-element.34.two, f32[4,2,2,128,128]{4,3,2,1,0:T(8,128)S(1)} %collective-permute-done.4.moved, ...), custom_call_target="tpu_custom_call" | custom-call | flops 5242880 | bytes 6291456 | tf_op jit(solution)/shard_map/update/pallas_call | solution.py:380
  (6 shorter events, 0.1 us)
Async XLA Ops:
  0.0 1.9 %copy-start = (f32[1,3,4,256,256]{4,3,2,1,0:T(8,128)S(1)}, f32[1,3,4,256,256]{4,3,2,1,0:T(8,128)}, u32[]{:S(2)}) copy-start(f32[1,3,4,256,256]{4,3,2,1,0:T(8,128)} %nodes.5) | copy-start | bytes 9437188
  2.3 18.3 %collective-permute-start = (f32[2,2,128,128]{3,2,1,0:T(8,128)S(1)}, f32[2,2,128,128]{3,2,1,0:T(8,128)S(1)}, u32[]{:S(2)}, u32[]{:S(2)}) collective-permute-start(f32[2,2,128,128]{3,2,1,0:T(8,128)S(1)} %get-tuple-element.26.own_high), channel_id=1, source_target_pairs={{0,1},{1,2},{2,3},{3,4},{4,5},{5,6},{6,7},{7,0},{8,9},{9,10},{10,1... | collective-permute-start | bytes 786440 | tf_op jit(solution)/shard_map/ppermute | solution.py:396
  4.4 18.1 %collective-permute-start.1 = (f32[2,2,128,128]{3,2,1,0:T(8,128)S(1)}, f32[2,2,128,128]{3,2,1,0:T(8,128)S(1)}, u32[]{:S(2)}, u32[]{:S(2)}) collective-permute-start(f32[2,2,128,128]{3,2,1,0:T(8,128)S(1)} %get-tuple-element.27.own_low), channel_id=1, source_target_pairs={{1,0},{2,1},{3,2},{4,3},{5,4},{6,5},{7,6},{0,7},{9,8},{10,9},{11,1... | collective-permute-start | bytes 786440 | tf_op jit(solution)/shard_map/ppermute | solution.py:396
  10.4 15.9 %collective-permute-start.2 = (f32[2,2,128,128]{3,2,1,0:T(8,128)S(1)}, f32[2,2,128,128]{3,2,1,0:T(8,128)S(1)}, u32[]{:S(2)}, u32[]{:S(2)}) collective-permute-start(f32[2,2,128,128]{3,2,1,0:T(8,128)S(1)} %get-tuple-element.30), channel_id=1, source_target_pairs={{0,1},{1,2},{2,3},{3,4},{4,5},{5,6},{6,7},{7,0},{8,9},{9,10},{10,1... | collective-permute-start | bytes 786440 | tf_op jit(solution)/shard_map/ppermute | solution.py:396
  10.4 17.7 %collective-permute-start.3 = (f32[2,2,128,128]{3,2,1,0:T(8,128)S(1)}, f32[2,2,128,128]{3,2,1,0:T(8,128)S(1)}, u32[]{:S(2)}, u32[]{:S(2)}) collective-permute-start(f32[2,2,128,128]{3,2,1,0:T(8,128)S(1)} %get-tuple-element.31), channel_id=1, source_target_pairs={{1,0},{2,1},{3,2},{4,3},{5,4},{6,5},{7,6},{0,7},{9,8},{10,9},{11,1... | collective-permute-start | bytes 786440 | tf_op jit(solution)/shard_map/ppermute | solution.py:396
  22.5 29.5 %copy-start.1 = (f32[1,3,4,256,256]{4,3,2,1,0:T(8,128)S(1)}, f32[1,3,4,256,256]{4,3,2,1,0:T(8,128)}, u32[]{:S(2)}) copy-start(f32[1,3,4,256,256]{4,3,2,1,0:T(8,128)} %nodes.5) | copy-start | bytes 9437188
  29.0 23.0 %collective-permute-start.4 = (f32[4,2,2,128,128]{4,3,2,1,0:T(8,128)S(1)}, f32[4,2,2,128,128]{4,3,2,1,0:T(8,128)S(1)}, u32[]{:S(2)}, u32[]{:S(2)}) collective-permute-start(f32[4,2,2,128,128]{4,3,2,1,0:T(8,128)S(1)} %get-tuple-element.34.two), channel_id=1, source_target_pairs={{0,8},{1,9},{2,10},{3,11},{4,12},{5,13},{6,14},{7,15},{16,24},{17,... | collective-permute-start | bytes 3145736 | tf_op jit(solution)/shard_map/ppermute | solution.py:438
  30.3 6.7 %collective-permute-start.5 = (f32[2,128,128]{2,1,0:T(8,128)S(1)}, f32[2,128,128]{2,1,0:T(8,128)S(1)}, u32[]{:S(2)}, u32[]{:S(2)}) collective-permute-start(f32[2,128,128]{2,1,0:T(8,128)S(1)} %get-tuple-element.36.own_high), channel_id=1, source_target_pairs={{0,1},{1,2},{2,3},{3,4},{4,5},{5,6},{6,7},{7,0},{8,9},{9,10},{10,1... | collective-permute-start | bytes 393224 | tf_op jit(solution)/shard_map/ppermute | solution.py:396
  30.7 9.2 %collective-permute-start.6 = (f32[2,128,128]{2,1,0:T(8,128)S(1)}, f32[2,128,128]{2,1,0:T(8,128)S(1)}, u32[]{:S(2)}, u32[]{:S(2)}) collective-permute-start(f32[2,128,128]{2,1,0:T(8,128)S(1)} %get-tuple-element.37.own_low), channel_id=1, source_target_pairs={{1,0},{2,1},{3,2},{4,3},{5,4},{6,5},{7,6},{0,7},{9,8},{10,9},{11,1... | collective-permute-start | bytes 393224 | tf_op jit(solution)/shard_map/ppermute | solution.py:396
  40.3 11.7 %collective-permute-start.7 = (f32[2,2,128,128]{3,2,1,0:T(8,128)S(1)}, f32[2,2,128,128]{3,2,1,0:T(8,128)S(1)}, u32[]{:S(2)}, u32[]{:S(2)}) collective-permute-start(f32[2,2,128,128]{3,2,1,0:T(8,128)S(1)} %get-tuple-element.38), channel_id=1, source_target_pairs={{0,8},{1,9},{2,10},{3,11},{4,12},{5,13},{6,14},{7,15},{16,24},{17,... | collective-permute-start | bytes 786440 | tf_op jit(solution)/shard_map/ppermute | solution.py:449
  41.6 9.1 %collective-permute-start.8 = (f32[2,128,128]{2,1,0:T(8,128)S(1)}, f32[2,128,128]{2,1,0:T(8,128)S(1)}, u32[]{:S(2)}, u32[]{:S(2)}) collective-permute-start(f32[2,128,128]{2,1,0:T(8,128)S(1)} %get-tuple-element.39), channel_id=1, source_target_pairs={{0,9},{1,10},{2,11},{3,12},{4,13},{5,14},{6,15},{7,8},{16,25},{17,... | collective-permute-start | bytes 393224 | tf_op jit(solution)/shard_map/ppermute | solution.py:447
  42.9 9.1 %collective-permute-start.9 = (f32[2,128,128]{2,1,0:T(8,128)S(1)}, f32[2,128,128]{2,1,0:T(8,128)S(1)}, u32[]{:S(2)}, u32[]{:S(2)}) collective-permute-start(f32[2,128,128]{2,1,0:T(8,128)S(1)} %get-tuple-element.40), channel_id=1, source_target_pairs={{0,15},{1,8},{2,9},{3,10},{4,11},{5,12},{6,13},{7,14},{16,31},{17,... | collective-permute-start | bytes 393224 | tf_op jit(solution)/shard_map/ppermute | solution.py:448

commit v2 on v1

--- a/solution.py
+++ b/solution.py
@@ -140,10 +140,15 @@
             out[k, p] = v
 
 
-def edge_kernel(nodes, first, last, held, sem):
+def outer_planes(planes):
+    odd = lax.rem(lax.axis_index("space"), 2)
+    return (1 - odd) * (planes - 1), odd * (planes - 1)
+
+
+def edge_kernel(nodes, near, far, held, sem):
     planes, halves = nodes.shape[2], held.shape[2]
     copies = []
-    for e, p in enumerate((0, planes - 1)):
+    for e, p in enumerate(outer_planes(planes)):
         for m in range(3):
             for h in range(halves):
                 copies.append(
@@ -157,15 +162,15 @@
         copy.start()
     for copy in copies:
         copy.wait()
-    rows = first.shape[2]
-    for e, out in enumerate((first, last)):
+    rows = near.shape[2]
+    for e, out in enumerate((near, far)):
         for h in range(halves):
             for q in range(2):
                 parts = [held[e, m, h, pl.ds(q, rows, stride=2), :] for m in range(3)]
                 out[h, q] = combine(WEIGHTS[0], parts)
 
 
-def first_kernel(nodes, one, slope, rest, edge_low, edge_high, coarse, held, start, mix, sem):
+def first_kernel(nodes, one, slope, rest, near, far, coarse, held, start, mix, sem):
     planes, halves = nodes.shape[2], held.shape[2]
     rows = one.shape[3]
     copies = [
@@ -197,52 +202,39 @@
                 rest[p, h, q] = GROWTH * (d - combine(SECOND, cubes))
     for p in range(planes):
         for h, q, _, laplace in laplace_planes(mix, p, planes, halves):
-            value = one[p, h, q] + DIFFUSE * laplace
-            one[p, h, q] = value
-            if p == 0:
-                edge_low[h, q] = 0.5 * value + slope[p, h, q]
-            if p == planes - 1:
-                edge_high[h, q] = 0.5 * value + slope[p, h, q]
+            one[p, h, q] = one[p, h, q] + DIFFUSE * laplace
+    for p, out in zip(outer_planes(planes), (near, far)):
+        out[...] = 0.5 * one[p] + slope[p]
     store_coarse(coarse, *restrict_field(start, planes, halves))
 
 
-def second_kernel(one_in, slope, rest, low, high, own_low, own_high, one, two, coarse, mix):
+def second_kernel(one_in, slope, rest, near, far, own_near, own_far, one, two, coarse, mix):
     planes, halves = one_in.shape[0], one_in.shape[1]
+    outer = outer_planes(planes)
+    for p in range(1, planes - 1):
+        one[p] = one_in[p]
+    for p, halo in zip(outer, (near, far)):
+        one[p] = one_in[p] + DIFFUSE * halo[...]
     for p in range(planes):
-        for h in range(halves):
-            for q in range(2):
-                value = one_in[p, h, q]
-                if p == 0:
-                    value = value + DIFFUSE * low[h, q]
-                if p == planes - 1:
-                    value = value + DIFFUSE * high[h, q]
-                one[p, h, q] = value
-                mix[p, h, q] = 0.5 * value + slope[p, h, q]
+        mix[p] = 0.5 * one[p] + slope[p]
     for p in range(planes):
         for h, q, _, laplace in laplace_planes(mix, p, planes, halves):
-            if p == 0:
-                laplace = laplace + (0.5 * DIFFUSE) * own_low[h, q]
-            if p == planes - 1:
-                laplace = laplace + (0.5 * DIFFUSE) * own_high[h, q]
             value = one[p, h, q]
             two[p, h, q] = (
                 value + DIFFUSE * laplace + (0.5 * GROWTH) * (value - cube(value)) + rest[p, h, q]
             )
+    for p, own in zip(outer, (own_near, own_far)):
+        two[p] = two[p] + (0.5 * DIFFUSE * DIFFUSE) * own[...]
     store_coarse(coarse, *restrict_field(one, planes, halves))
 
 
-def third_kernel(two_in, low, high, coarse_zero, coarse_one, two, send_low, send_high, work):
+def third_kernel(two_in, near, far, coarse_zero, coarse_one, two, send_near, send_far, work):
     planes, halves = two_in.shape[0], two_in.shape[1]
     later = lax.axis_index("tm").astype(F32)
-    for p in range(planes):
-        for h in range(halves):
-            for q in range(2):
-                value = two_in[p, h, q]
-                if p == 0:
-                    value = value + DIFFUSE * low[h, q]
-                if p == planes - 1:
-                    value = value + DIFFUSE * high[h, q]
-                two[p, h, q] = value
+    for p in range(1, planes - 1):
+        two[p] = two_in[p]
+    for p, halo in zip(outer_planes(planes), (near, far)):
+        two[p] = two_in[p] + DIFFUSE * halo[...]
     means_two, forces_two, edges_two = restrict_field(two, planes, halves)
     half = planes // 2
     zero = [coarse_zero[0, p] for p in range(half)]
@@ -254,17 +246,32 @@
         parts = (coarse_zero[1, p], coarse_one[1, p], forces_two[p])
         sweep_zero.append(combine(WEIGHTS[0], parts))
         sweep_one.append(combine(WEIGHTS[1], parts))
-    for e, (p, out) in enumerate(((0, send_low), (half - 1, send_high))):
+    sends = []
+    for e, p in enumerate((0, half - 1)):
         parts = (coarse_zero[2, e], coarse_one[2, e], edges_two[e])
         partial = sweep_zero[p] - mean_one[p] + (1.0 - later) * zero[p] - (0.5 * later) * force_zero[p]
-        out[0] = (DIFFUSE / 8.0) * combine(WEIGHTS[0], parts) - (0.5 * COARSE * later) * zero[p]
-        out[1] = (DIFFUSE / 8.0) * combine(WEIGHTS[1], parts) + (0.5 * COARSE) * partial
+        sends.append((
+            (DIFFUSE / 8.0) * combine(WEIGHTS[0], parts) - (0.5 * COARSE * later) * zero[p],
+            (DIFFUSE / 8.0) * combine(WEIGHTS[1], parts) + (0.5 * COARSE) * partial,
+        ))
+    for k in range(2):
+        send_near[k], send_far[k] = low_high(sends[0][k], sends[1][k])
     for p in range(half):
         work[0, p] = zero[p]
         work[1, p] = mean_one[p]
         work[2, p] = means_two[p]
         work[3, p] = sweep_zero[p] - 0.5 * force_zero[p]
         work[4, p] = sweep_one[p] - 0.5 * force_one[p]
+
+
+def low_high(near, far):
+    odd = lax.rem(lax.axis_index("space"), 2)
+    return jnp.where(odd == 1, near, far), jnp.where(odd == 1, far, near)
+
+
+def sides(near, far):
+    pairs = [low_high(near[k], far[k]) for k in range(2)]
+    return [v[0] for v in pairs], [v[1] for v in pairs]
 
 
 def coarse_chain(first, first_low, first_high, bend_low, bend_high, work, low, high, own_low, own_high):
@@ -290,28 +297,34 @@
     return one, two
 
 
-def fourth_kernel(work, low, high, own_low, own_high, partner, send_low, send_high):
+def fourth_kernel(work, near, far, own_near, own_far, held, partner, send_near, send_far, passed):
+    del held, passed
     half = work.shape[1]
     first = [work[0, p] for p in range(half)]
+    low, high = sides(near, far)
+    own_low, own_high = sides(own_near, own_far)
     one, two = coarse_chain(first, 0.0, 0.0, 0.0, 0.0, work, low, high, own_low, own_high)
     force = coarse_force(two)
     for p in range(half):
         partner[0, p] = two[p]
         partner[1, p] = two[p] - work[2, p]
-    for p, out in ((0, send_low), (half - 1, send_high)):
-        out[0] = two[p]
-        out[1] = two[p] + 0.5 * force[p]
+    send_near[0], send_far[0] = low_high(two[0], two[half - 1])
+    send_near[1], send_far[1] = low_high(
+        two[0] + 0.5 * force[0], two[half - 1] + 0.5 * force[half - 1]
+    )
 
 
 def last_kernel(
-    nodes, one, two, moved, work, low, high, own_low, own_high, partner, ring_low, ring_high,
+    nodes, one, two, moved, work, near, far, own_near, own_far, partner, ring_near, ring_far,
     updated, held, result, load_sem, store_sem,
 ):
     planes, halves = one.shape[0], one.shape[1]
     rows = one.shape[3]
     half = planes // 2
     section = lax.axis_index("tm")
-    later = section.astype(F32)
+    low, high = sides(near, far)
+    own_low, own_high = sides(own_near, own_far)
+    ring_low, ring_high = sides(ring_near, ring_far)
     loads = [
         pltpu.make_async_copy(
             nodes.at[0, 0, :, :, pl.ds(h * LANES, LANES)], held.at[:, h], load_sem.at[h]
@@ -327,10 +340,10 @@
     scale = 0.5 * COARSE
     coarse_one, coarse_two = coarse_chain(
         first,
-        (scale * later) * ring_low[0],
-        (scale * later) * ring_high[0],
-        later * (ring_low[1] + scale * first[0]),
-        later * (ring_high[1] + scale * first[half - 1]),
+        jnp.where(section == 0, 0.0, scale * ring_low[0]),
+        jnp.where(section == 0, 0.0, scale * ring_high[0]),
+        jnp.where(section == 0, 0.0, ring_low[1] + scale * first[0]),
+        jnp.where(section == 0, 0.0, ring_high[1] + scale * first[half - 1]),
         work, low, high, own_low, own_high,
     )
     spread = spread_matrix(LANES * halves // 2)
@@ -374,26 +387,51 @@
         copy.wait()
 
 
-def call(kernel, name, inputs, any_inputs, outs, scratch=(), any_out=False, flops=0, size=0):
-    vmem = pl.BlockSpec(memory_space=pltpu.VMEM)
-    hbm = pl.BlockSpec(memory_space=pl.ANY)
+def call(kernel, name, inputs, any_inputs, outs, scratch=(), any_outs=(), limit=VMEM_LIMIT,
+         aliases=None, flops=0, size=0):
+    def spec(far, passed):
+        return pl.BlockSpec(
+            memory_space=pl.ANY if passed else pltpu.HBM if far else pltpu.VMEM
+        )
+
     return pl.pallas_call(
         kernel,
         name=name,
         out_shape=[jax.ShapeDtypeStruct(s, F32) for s in outs],
-        in_specs=[hbm if k < any_inputs else vmem for k in range(len(inputs))],
-        out_specs=[hbm if any_out else vmem for _ in outs],
+        in_specs=[spec(k in any_inputs, k in (aliases or {})) for k in range(len(inputs))],
+        out_specs=[spec(k in any_outs, k in (aliases or {}).values()) for k in range(len(outs))],
         scratch_shapes=list(scratch),
-        compiler_params=pltpu.CompilerParams(vmem_limit_bytes=VMEM_LIMIT),
+        input_output_aliases=aliases or {},
+        compiler_params=pltpu.CompilerParams(vmem_limit_bytes=limit),
         cost_estimate=pl.CostEstimate(flops=flops, bytes_accessed=size, transcendentals=0),
     )(*inputs)
 
 
-def exchange(low, high, axis):
-    peers = lax.axis_size(axis)
-    up = [(i, (i + 1) % peers) for i in range(peers)]
-    down = [(j, i) for i, j in up]
-    return lax.ppermute(high, axis, up), lax.ppermute(low, axis, down)
+def pairings(peers):
+    near = [i ^ 1 for i in range(peers)]
+    far = [(i + 1) % peers if i % 2 else (i - 1) % peers for i in range(peers)]
+    return near, far
+
+
+def exchange(near, far):
+    to_near, to_far = pairings(lax.axis_size("space"))
+    return (
+        lax.ppermute(near, "space", list(enumerate(to_near))),
+        lax.ppermute(far, "space", list(enumerate(to_far))),
+    )
+
+
+def swapped(value):
+    return lax.ppermute(value, "tm", [(0, 1), (1, 0)])
+
+
+def handed_on(near, far):
+    peers = lax.axis_size("space")
+    out = []
+    for value, to in zip((near, far), pairings(peers)):
+        perm = [(i, peers + to[i]) for i in range(peers)] + [(peers + i, i) for i in range(peers)]
+        out.append(lax.ppermute(value, ("tm", "space"), perm))
+    return out
 
 
 def local(nodes):
@@ -406,14 +444,14 @@
     packed = (3, half) + quarter
     size = planes * ny * nz * 4
 
-    a_low, a_high = call(
-        edge_kernel, "edge_mix", (nodes,), 1, [plane, plane],
+    a_near, a_far = call(
+        edge_kernel, "edge_mix", (nodes,), (0,), [plane, plane],
         [pltpu.VMEM((2, 3, halves, ny, LANES), F32), pltpu.SemaphoreType.DMA((2, 3, halves))],
         size=size * 2, flops=size,
     )
-    a_below, a_above = exchange(a_low, a_high, "space")
-    one_part, slope, rest, b_low, b_high, coarse_zero = call(
-        first_kernel, "first_stage", (nodes,), 1, [field, field, field, plane, plane, packed],
+    got_a_near, got_a_far = exchange(a_near, a_far)
+    one_part, slope, rest, b_near, b_far, coarse_zero = call(
+        first_kernel, "first_stage", (nodes,), (0,), [field, field, field, plane, plane, packed],
         [
             pltpu.VMEM((3, planes, halves, ny, LANES), F32),
             pltpu.VMEM(field, F32),
@@ -422,42 +460,38 @@
         ],
         size=size * 6, flops=size * 10,
     )
-    b_below, b_above = exchange(b_low, b_high, "space")
+    got_b_near, got_b_far = exchange(b_near, b_far)
     one, two_part, coarse_mid = call(
         second_kernel, "second_stage",
-        (one_part, slope, rest, a_below, a_above, a_low, a_high), 0,
+        (one_part, slope, rest, got_a_near, got_a_far, a_near, a_far), (),
         [field, field, packed], [pltpu.VMEM(field, F32)],
         size=size * 6, flops=size * 10,
     )
-    two, h_low, h_high, work = call(
-        third_kernel, "third_stage", (two_part, b_below, b_above, coarse_zero, coarse_mid), 0,
+    two, h_near, h_far, work = call(
+        third_kernel, "third_stage", (two_part, got_b_near, got_b_far, coarse_zero, coarse_mid), (),
         [field, pair, pair, (5, half) + quarter],
         size=size * 3, flops=size * 5,
     )
-    below, above = exchange(h_low, h_high, "space")
-    moved = lax.ppermute(two, "tm", [(0, 1)])
-    partner, f_low, f_high = call(
-        fourth_kernel, "coarse_chain", (work, below, above, h_low, h_high), 0,
-        [(2, half) + quarter, pair, pair],
+    got_near, got_far = exchange(h_near, h_far)
+    partner, f_near, f_far, two = call(
+        fourth_kernel, "coarse_chain", (work, got_near, got_far, h_near, h_far, two), (5,),
+        [(2, half) + quarter, pair, pair, field], any_outs=(3,), aliases={5: 3},
         size=size, flops=size,
     )
-    peers = lax.axis_size("space")
-    to_above = [(i, peers + (i + 1) % peers) for i in range(peers)]
-    to_below = [(i, peers + (i - 1) % peers) for i in range(peers)]
-    ring_below = lax.ppermute(f_high, ("tm", "space"), to_above)
-    ring_above = lax.ppermute(f_low, ("tm", "space"), to_below)
-    partner = lax.ppermute(partner, "tm", [(0, 1)])
+    ring_near, ring_far = handed_on(f_near, f_far)
+    partner = swapped(partner)
+    moved = swapped(two)
     updated, = call(
         last_kernel, "update",
-        (nodes, one, two, moved, work, below, above, h_low, h_high, partner, ring_below, ring_above),
-        1, [(1, 3, planes, ny, nz)],
+        (nodes, one, two, moved, work, got_near, got_far, h_near, h_far, partner, ring_near, ring_far),
+        (0,), [(1, 3, planes, ny, nz)],
         [
             pltpu.VMEM((planes, halves, ny, LANES), F32),
             pltpu.VMEM((3, planes, halves, ny, LANES), F32),
             pltpu.SemaphoreType.DMA((halves,)),
             pltpu.SemaphoreType.DMA((3, planes, halves)),
         ],
-        any_out=True, size=size * 6, flops=size * 5,
+        any_outs=(0,), size=size * 6, flops=size * 5,
     )
     return updated
 

time: 54.5 us -> 49.6 us (0.910)
  starting transfers between devices: 18.8 us -> 14.8 us
  waiting for transfers between devices: 25.2 us -> 24 us
    ppermute x10, starting transfers between devices: 18.8 us -> 14.8 us  [the longest x3 7.85 us: exchange(): lax.ppermute(far, 'space', list(enumerate(to_far)))]
    ppermute x10, waiting for transfers between devices: 25.2 us -> 24 us  [the longest x3 13.6 us: exchange(): lax.ppermute(near, 'space', list(enumerate(to_near)))]
  transfers between devices with their start and end apart: 10 -> 10, of which waited for: 8 -> 5; matrix products, arithmetic and copies ran while one was open for 0% -> 0% of each run, Pallas kernels for 9% -> 9%
where the time goes in v2:
time: 49.6 us; the launch traced here: 49.5 us
  waiting for transfers between devices  24 us (48%)
  starting transfers between devices  14.8 us (30%)
  Pallas kernels  8.7 us (18%)
  local copies, waits for them, and re-layouts  1.9 us (4%)
    ppermute x3, waiting for transfers between devices, exchange(): lax.ppermute(near, 'space', list(enumerate(to_near)))  13.6 us
    pallas_call x6, Pallas kernels, call(): pl.pallas_call(kernel, name=name, out_shape=[jax.ShapeDtypeStruct(s, F32)...  8.7 us
    ppermute x3, starting transfers between devices, exchange(): lax.ppermute(far, 'space', list(enumerate(to_far)))  7.85 us
    ppermute x2, waiting for transfers between devices, handed_on(): out.append(lax.ppermute(value, ('tm', 'space'), perm))  7.09 us
    ppermute x3, starting transfers between devices, exchange(): lax.ppermute(near, 'space', list(enumerate(to_near)))  3.42 us
    ppermute x3, waiting for transfers between devices, exchange(): lax.ppermute(far, 'space', list(enumerate(to_far)))  3.27 us
    ppermute x2, starting transfers between devices, swapped(): return lax.ppermute(value, 'tm', [(0, 1), (1, 0)])  3.1 us
    unnamed x4, local copies, waits for them, and re-layouts  1.9 us
  transfers between devices with their start and end apart: 10, of which 5 were waited for; matrix products, arithmetic and copies ran while one was open for 0% of the time, Pallas kernels for 9%

profile of v2, /device:TPU:1, one launch (start us, length us, event | category | flops | bytes accessed | tf_op | source)
XLA Modules:
  0.0 49.5 jit_solution(16960526621901185966)
XLA Ops:
  0.0 1.9 %copy-done = f32[1,3,4,256,256]{4,3,2,1,0:T(8,128)S(1)} copy-done((f32[1,3,4,256,256]{4,3,2,1,0:T(8,128)S(1)}, f32[1,3,4,256,256]{4,3,2,1,0:T(8,128)}, u32[]{:S(2)}) %copy-start) | copy-done | bytes 3145752
  1.9 0.4 edge_mix.1
  2.3 2.1 %collective-permute-start = (f32[2,2,128,128]{3,2,1,0:T(8,128)S(1)}, f32[2,2,128,128]{3,2,1,0:T(8,128)S(1)}, u32[]{:S(2)}, u32[]{:S(2)}) collective-permute-start(f32[2,2,128,128]{3,2,1,0:T(8,128)S(1)} %get-tuple-element.27.own_near), channel_id=1, source_target_pairs={{0,1},{1,0},{2,3},{3,2},{4,5},{5,4},{6,7},{7,6},{8,9},{9,8},{10,11... | collective-permute-start | bytes 786440 | tf_op jit(solution)/shard_map/ppermute | solution.py:419
  4.4 3.3 %collective-permute-start.1 = (f32[2,2,128,128]{3,2,1,0:T(8,128)S(1)}, f32[2,2,128,128]{3,2,1,0:T(8,128)S(1)}, u32[]{:S(2)}, u32[]{:S(2)}) collective-permute-start(f32[2,2,128,128]{3,2,1,0:T(8,128)S(1)} %get-tuple-element.28.own_far), channel_id=1, source_target_pairs={{0,7},{1,2},{2,1},{3,4},{4,3},{5,6},{6,5},{7,0},{8,15},{9,10},{10,... | collective-permute-start | bytes 786440 | tf_op jit(solution)/shard_map/ppermute | solution.py:420
  7.7 2.9 %first_stage.1 = (f32[4,2,2,128,128]{4,3,2,1,0:T(8,128)S(1)}, f32[4,2,2,128,128]{4,3,2,1,0:T(8,128)S(1)}, f32[4,2,2,128,128]{4,3,2,1,0:T(8,128)S(1)}, f32[2,2,12...) custom-call(f32[1,3,4,256,256]{4,3,2,1,0:T(8,128)S(1)} %copy-done), custom_call_target="tpu_custom_call" | custom-call | flops 10485760 | bytes 6291456 | tf_op jit(solution)/shard_map/first_stage/pallas_call | solution.py:397
  10.6 0.1 collective-permute-start.2
  10.7 1.3 %collective-permute-start.3 = (f32[2,2,128,128]{3,2,1,0:T(8,128)S(1)}, f32[2,2,128,128]{3,2,1,0:T(8,128)S(1)}, u32[]{:S(2)}, u32[]{:S(2)}) collective-permute-start(f32[2,2,128,128]{3,2,1,0:T(8,128)S(1)} %get-tuple-element.32), channel_id=1, source_target_pairs={{0,7},{1,2},{2,1},{3,4},{4,3},{5,6},{6,5},{7,0},{8,15},{9,10},{10,... | collective-permute-start | bytes 786440 | tf_op jit(solution)/shard_map/ppermute | solution.py:420
  12.0 8.6 %collective-permute-done.near = f32[2,2,128,128]{3,2,1,0:T(8,128)S(1)} collective-permute-done((f32[2,2,128,128]{3,2,1,0:T(8,128)S(1)}, f32[2,2,128,128]{3,2,1,0:T(8,128)S(1)}, u32[]{:S(2)}, u32[]{:S(2)}) %collective-permute-start) | collective-permute-done | bytes 262176 | tf_op jit(solution)/shard_map/ppermute | solution.py:419
  20.7 0.0 collective-permute-done.1.far
  20.7 1.6 %second_stage.1 = (f32[4,2,2,128,128]{4,3,2,1,0:T(8,128)S(1)}, f32[4,2,2,128,128]{4,3,2,1,0:T(8,128)S(1)}, f32[3,2,128,128]{3,2,1,0:T(8,128)S(1)}) custom-call(f32[4,2,2,128,128]{4,3,2,1,0:T(8,128)S(1)} %get-tuple-element.24.one_in, f32[4,2,2,128,128]{4,3,2,1,0:T(8,128)S(1)} %get-tuple-element.25.slope, f32[4,2,2,128,128]{4,3,2,1,0:T(8,128)S(1)} %get-tuple-element.26.rest, ...), custom_call_target="tpu_custom_call" | custom-call | flops 10485760 | bytes 6291456 | tf_op jit(solution)/shard_map/second_stage/pallas_call | solution.py:397
  22.3 0.0 copy-start.1
  22.3 5.0 %collective-permute-done.2.near = f32[2,2,128,128]{3,2,1,0:T(8,128)S(1)} collective-permute-done((f32[2,2,128,128]{3,2,1,0:T(8,128)S(1)}, f32[2,2,128,128]{3,2,1,0:T(8,128)S(1)}, u32[]{:S(2)}, u32[]{:S(2)}) %collective-permute-start.2) | collective-permute-done | bytes 262176 | tf_op jit(solution)/shard_map/ppermute | solution.py:419
  27.3 0.0 collective-permute-done.3.far
  27.3 1.0 %third_stage.1 = (f32[4,2,2,128,128]{4,3,2,1,0:T(8,128)S(1)}, f32[2,128,128]{2,1,0:T(8,128)S(1)}, f32[2,128,128]{2,1,0:T(8,128)S(1)}, f32[5,2,128,128]{3,2,1,0:T(8,128)S(1)}) custom-call(f32[4,2,2,128,128]{4,3,2,1,0:T(8,128)S(1)} %get-tuple-element.30.two_in, f32[2,2,128,128]{3,2,1,0:T(8,128)S(1)} %collective-permute-done.2.near, ...), custom_call_target="tpu_custom_call" | custom-call | flops 5242880 | bytes 3145728 | tf_op jit(solution)/shard_map/third_stage/pallas_call | solution.py:397
  28.3 1.2 %collective-permute-start.4 = (f32[2,128,128]{2,1,0:T(8,128)S(1)}, f32[2,128,128]{2,1,0:T(8,128)S(1)}, u32[]{:S(2)}, u32[]{:S(2)}) collective-permute-start(f32[2,128,128]{2,1,0:T(8,128)S(1)} %get-tuple-element.36.own_near), channel_id=1, source_target_pairs={{0,1},{1,0},{2,3},{3,2},{4,5},{5,4},{6,7},{7,6},{8,9},{9,8},{10,11... | collective-permute-start | bytes 393224 | tf_op jit(solution)/shard_map/ppermute | solution.py:419
  29.5 3.3 %collective-permute-start.5 = (f32[2,128,128]{2,1,0:T(8,128)S(1)}, f32[2,128,128]{2,1,0:T(8,128)S(1)}, u32[]{:S(2)}, u32[]{:S(2)}) collective-permute-start(f32[2,128,128]{2,1,0:T(8,128)S(1)} %get-tuple-element.37.own_far), channel_id=1, source_target_pairs={{0,7},{1,2},{2,1},{3,4},{4,3},{5,6},{6,5},{7,0},{8,15},{9,10},{10,... | collective-permute-start | bytes 393224 | tf_op jit(solution)/shard_map/ppermute | solution.py:420
  32.8 3.3 %collective-permute-done.5.far = f32[2,128,128]{2,1,0:T(8,128)S(1)} collective-permute-done((f32[2,128,128]{2,1,0:T(8,128)S(1)}, f32[2,128,128]{2,1,0:T(8,128)S(1)}, u32[]{:S(2)}, u32[]{:S(2)}) %collective-permute-start.5) | collective-permute-done | bytes 131104 | tf_op jit(solution)/shard_map/ppermute | solution.py:420
  36.1 0.4 coarse_chain.1
  36.4 3.0 %collective-permute-start.6 = (f32[4,2,2,128,128]{4,3,2,1,0:T(8,128)S(1)}, f32[4,2,2,128,128]{4,3,2,1,0:T(8,128)S(1)}, u32[]{:S(2)}, u32[]{:S(2)}) collective-permute-start(f32[4,2,2,128,128]{4,3,2,1,0:T(8,128)S(1)} %get-tuple-element.39.two), channel_id=1, source_target_pairs={{0,8},{8,0},{1,9},{9,1},{2,10},{10,2},{3,11},{11,3},{4,12},{12,4},... | collective-permute-start | bytes 3145736 | tf_op jit(solution)/shard_map/ppermute | solution.py:425
  39.5 0.1 collective-permute-start.7
  39.5 0.4 collective-permute-start.8
  40.0 4.0 %collective-permute-done.8.ring_near = f32[2,128,128]{2,1,0:T(8,128)S(1)} collective-permute-done((f32[2,128,128]{2,1,0:T(8,128)S(1)}, f32[2,128,128]{2,1,0:T(8,128)S(1)}, u32[]{:S(2)}, u32[]{:S(2)}) %collective-permute-start.8) | collective-permute-done | bytes 131104 | tf_op jit(solution)/shard_map/ppermute | solution.py:433
  43.9 3.1 %collective-permute-done.9.ring_far = f32[2,128,128]{2,1,0:T(8,128)S(1)} collective-permute-done((f32[2,128,128]{2,1,0:T(8,128)S(1)}, f32[2,128,128]{2,1,0:T(8,128)S(1)}, u32[]{:S(2)}, u32[]{:S(2)}) %collective-permute-start.9) | collective-permute-done | bytes 131104 | tf_op jit(solution)/shard_map/ppermute | solution.py:433
  47.1 2.4 %update.1 = f32[1,3,4,256,256]{4,3,2,1,0:T(8,128)} custom-call(f32[1,3,4,256,256]{4,3,2,1,0:T(8,128)S(1)} %copy-done.1, f32[4,2,2,128,128]{4,3,2,1,0:T(8,128)S(1)} %get-tuple-element.29.one, f32[4,2,2,128,128]{4,3,2,1,0:T(8,128)S(1)} %get-tuple-element.39.two, f32[4,2,2,128,128]{4,3,2,1,0:T(8,128)S(1)} %collective-permute-done.6.moved, ...), custom_call_target="tpu_custom_call" | custom-call | flops 5242880 | bytes 6291456 | tf_op jit(solution)/shard_map/update/pallas_call | solution.py:397
  (6 shorter events, 0.0 us)
Async XLA Ops:
  0.0 1.9 %copy-start = (f32[1,3,4,256,256]{4,3,2,1,0:T(8,128)S(1)}, f32[1,3,4,256,256]{4,3,2,1,0:T(8,128)}, u32[]{:S(2)}) copy-start(f32[1,3,4,256,256]{4,3,2,1,0:T(8,128)} %nodes.5) | copy-start | bytes 9437188
  2.3 18.4 %collective-permute-start = (f32[2,2,128,128]{3,2,1,0:T(8,128)S(1)}, f32[2,2,128,128]{3,2,1,0:T(8,128)S(1)}, u32[]{:S(2)}, u32[]{:S(2)}) collective-permute-start(f32[2,2,128,128]{3,2,1,0:T(8,128)S(1)} %get-tuple-element.27.own_near), channel_id=1, source_target_pairs={{0,1},{1,0},{2,3},{3,2},{4,5},{5,4},{6,7},{7,6},{8,9},{9,8},{10,11... | collective-permute-start | bytes 786440 | tf_op jit(solution)/shard_map/ppermute | solution.py:419
  4.4 16.2 %collective-permute-start.1 = (f32[2,2,128,128]{3,2,1,0:T(8,128)S(1)}, f32[2,2,128,128]{3,2,1,0:T(8,128)S(1)}, u32[]{:S(2)}, u32[]{:S(2)}) collective-permute-start(f32[2,2,128,128]{3,2,1,0:T(8,128)S(1)} %get-tuple-element.28.own_far), channel_id=1, source_target_pairs={{0,7},{1,2},{2,1},{3,4},{4,3},{5,6},{6,5},{7,0},{8,15},{9,10},{10,... | collective-permute-start | bytes 786440 | tf_op jit(solution)/shard_map/ppermute | solution.py:420
  10.6 16.7 %collective-permute-start.2 = (f32[2,2,128,128]{3,2,1,0:T(8,128)S(1)}, f32[2,2,128,128]{3,2,1,0:T(8,128)S(1)}, u32[]{:S(2)}, u32[]{:S(2)}) collective-permute-start(f32[2,2,128,128]{3,2,1,0:T(8,128)S(1)} %get-tuple-element.31), channel_id=1, source_target_pairs={{0,1},{1,0},{2,3},{3,2},{4,5},{5,4},{6,7},{7,6},{8,9},{9,8},{10,11... | collective-permute-start | bytes 786440 | tf_op jit(solution)/shard_map/ppermute | solution.py:419
  10.7 16.6 %collective-permute-start.3 = (f32[2,2,128,128]{3,2,1,0:T(8,128)S(1)}, f32[2,2,128,128]{3,2,1,0:T(8,128)S(1)}, u32[]{:S(2)}, u32[]{:S(2)}) collective-permute-start(f32[2,2,128,128]{3,2,1,0:T(8,128)S(1)} %get-tuple-element.32), channel_id=1, source_target_pairs={{0,7},{1,2},{2,1},{3,4},{4,3},{5,6},{6,5},{7,0},{8,15},{9,10},{10,... | collective-permute-start | bytes 786440 | tf_op jit(solution)/shard_map/ppermute | solution.py:420
  22.3 24.8 %copy-start.1 = (f32[1,3,4,256,256]{4,3,2,1,0:T(8,128)S(1)}, f32[1,3,4,256,256]{4,3,2,1,0:T(8,128)}, u32[]{:S(2)}) copy-start(f32[1,3,4,256,256]{4,3,2,1,0:T(8,128)} %nodes.5) | copy-start | bytes 9437188
  28.3 4.5 %collective-permute-start.4 = (f32[2,128,128]{2,1,0:T(8,128)S(1)}, f32[2,128,128]{2,1,0:T(8,128)S(1)}, u32[]{:S(2)}, u32[]{:S(2)}) collective-permute-start(f32[2,128,128]{2,1,0:T(8,128)S(1)} %get-tuple-element.36.own_near), channel_id=1, source_target_pairs={{0,1},{1,0},{2,3},{3,2},{4,5},{5,4},{6,7},{7,6},{8,9},{9,8},{10,11... | collective-permute-start | bytes 393224 | tf_op jit(solution)/shard_map/ppermute | solution.py:419
  29.5 6.5 %collective-permute-start.5 = (f32[2,128,128]{2,1,0:T(8,128)S(1)}, f32[2,128,128]{2,1,0:T(8,128)S(1)}, u32[]{:S(2)}, u32[]{:S(2)}) collective-permute-start(f32[2,128,128]{2,1,0:T(8,128)S(1)} %get-tuple-element.37.own_far), channel_id=1, source_target_pairs={{0,7},{1,2},{2,1},{3,4},{4,3},{5,6},{6,5},{7,0},{8,15},{9,10},{10,... | collective-permute-start | bytes 393224 | tf_op jit(solution)/shard_map/ppermute | solution.py:420
  36.4 10.6 %collective-permute-start.6 = (f32[4,2,2,128,128]{4,3,2,1,0:T(8,128)S(1)}, f32[4,2,2,128,128]{4,3,2,1,0:T(8,128)S(1)}, u32[]{:S(2)}, u32[]{:S(2)}) collective-permute-start(f32[4,2,2,128,128]{4,3,2,1,0:T(8,128)S(1)} %get-tuple-element.39.two), channel_id=1, source_target_pairs={{0,8},{8,0},{1,9},{9,1},{2,10},{10,2},{3,11},{11,3},{4,12},{12,4},... | collective-permute-start | bytes 3145736 | tf_op jit(solution)/shard_map/ppermute | solution.py:425
  39.5 7.6 %collective-permute-start.7 = (f32[2,2,128,128]{3,2,1,0:T(8,128)S(1)}, f32[2,2,128,128]{3,2,1,0:T(8,128)S(1)}, u32[]{:S(2)}, u32[]{:S(2)}) collective-permute-start(f32[2,2,128,128]{3,2,1,0:T(8,128)S(1)} %get-tuple-element.40), channel_id=1, source_target_pairs={{0,8},{8,0},{1,9},{9,1},{2,10},{10,2},{3,11},{11,3},{4,12},{12,4},... | collective-permute-start | bytes 786440 | tf_op jit(solution)/shard_map/ppermute | solution.py:425
  39.5 4.4 %collective-permute-start.8 = (f32[2,128,128]{2,1,0:T(8,128)S(1)}, f32[2,128,128]{2,1,0:T(8,128)S(1)}, u32[]{:S(2)}, u32[]{:S(2)}) collective-permute-start(f32[2,128,128]{2,1,0:T(8,128)S(1)} %get-tuple-element.41), channel_id=1, source_target_pairs={{0,9},{1,8},{2,11},{3,10},{4,13},{5,12},{6,15},{7,14},{8,0},{9,1},... | collective-permute-start | bytes 393224 | tf_op jit(solution)/shard_map/ppermute | solution.py:433
  40.0 7.1 %collective-permute-start.9 = (f32[2,128,128]{2,1,0:T(8,128)S(1)}, f32[2,128,128]{2,1,0:T(8,128)S(1)}, u32[]{:S(2)}, u32[]{:S(2)}) collective-permute-start(f32[2,128,128]{2,1,0:T(8,128)S(1)} %get-tuple-element.42), channel_id=1, source_target_pairs={{0,15},{1,10},{2,9},{3,12},{4,11},{5,14},{6,13},{7,8},{8,0},{9,1},... | collective-permute-start | bytes 393224 | tf_op jit(solution)/shard_map/ppermute | solution.py:433

commit v3 on v2

--- a/solution.py
+++ b/solution.py
@@ -14,6 +14,8 @@
 F32 = jnp.float32
 BF16 = jnp.bfloat16
 VMEM_LIMIT = 32 * 1024 * 1024
+EDGE_LIMIT = 52 * 1024 * 1024
+FIRST_LIMIT = 48 * 1024 * 1024
 
 
 def combine(weights, parts):
@@ -145,61 +147,47 @@
     return (1 - odd) * (planes - 1), odd * (planes - 1)
 
 
-def edge_kernel(nodes, near, far, held, sem):
-    planes, halves = nodes.shape[2], held.shape[2]
-    copies = []
-    for e, p in enumerate(outer_planes(planes)):
-        for m in range(3):
-            for h in range(halves):
-                copies.append(
-                    pltpu.make_async_copy(
-                        nodes.at[0, m, p, :, pl.ds(h * LANES, LANES)],
-                        held.at[e, m, h],
-                        sem.at[e, m, h],
-                    )
-                )
-    for copy in copies:
-        copy.start()
-    for copy in copies:
-        copy.wait()
+def edge_kernel(nodes, near, far, held, work, sem):
+    planes, halves = nodes.shape[2], near.shape[0]
     rows = near.shape[2]
-    for e, out in enumerate((near, far)):
-        for h in range(halves):
-            for q in range(2):
-                parts = [held[e, m, h, pl.ds(q, rows, stride=2), :] for m in range(3)]
-                out[h, q] = combine(WEIGHTS[0], parts)
-
-
-def first_kernel(nodes, one, slope, rest, near, far, coarse, held, start, mix, sem):
-    planes, halves = nodes.shape[2], held.shape[2]
-    rows = one.shape[3]
     copies = [
         [
-            pltpu.make_async_copy(
-                nodes.at[0, m, p, :, pl.ds(h * LANES, LANES)], held.at[m, p, h], sem.at[m, p, h]
-            )
+            pltpu.make_async_copy(nodes.at[0, m, p], held.at[e, m], sem.at[e, m])
             for m in range(3)
-            for h in range(halves)
         ]
-        for p in range(planes)
+        for e, p in enumerate(outer_planes(planes))
     ]
     for group in copies:
         for copy in group:
             copy.start()
-    for p in range(planes):
-        for copy in copies[p]:
+    for e, out in enumerate((near, far)):
+        for copy in copies[e]:
             copy.wait()
         for h in range(halves):
+            lanes = pl.ds(h * LANES, LANES)
+            work[e, h] = combine(WEIGHTS[0], [held[e, m, :, lanes] for m in range(3)])
             for q in range(2):
-                parts = [held[m, p, h, pl.ds(q, rows, stride=2), :] for m in range(3)]
-                cubes = [cube(v) for v in parts]
-                a = combine(WEIGHTS[0], parts)
-                d = combine(SECOND, parts)
-                start[p, h, q] = parts[0]
-                mix[p, h, q] = a
-                slope[p, h, q] = d
-                one[p, h, q] = parts[0] + GROWTH * (a - combine(WEIGHTS[0], cubes))
-                rest[p, h, q] = GROWTH * (d - combine(SECOND, cubes))
+                out[h, q] = work[e, h, pl.ds(q, rows, stride=2), :]
+
+
+def first_kernel(nodes, one, slope, rest, near, far, coarse, work, start, mix):
+    planes, halves = one.shape[0], one.shape[1]
+    rows = one.shape[3]
+    for p in range(planes):
+        for h in range(halves):
+            lanes = pl.ds(h * LANES, LANES)
+            parts = [nodes[0, m, p, :, lanes] for m in range(3)]
+            cubes = [cube(v) for v in parts]
+            a = combine(WEIGHTS[0], parts)
+            d = combine(SECOND, parts)
+            work[0] = parts[0]
+            work[1] = a
+            work[2] = d
+            work[3] = parts[0] + GROWTH * (a - combine(WEIGHTS[0], cubes))
+            work[4] = GROWTH * (d - combine(SECOND, cubes))
+            for q in range(2):
+                for k, out in enumerate((start, mix, slope, one, rest)):
+                    out[p, h, q] = work[k, pl.ds(q, rows, stride=2), :]
     for p in range(planes):
         for h, q, _, laplace in laplace_planes(mix, p, planes, halves):
             one[p, h, q] = one[p, h, q] + DIFFUSE * laplace
@@ -262,6 +250,7 @@
         work[2, p] = means_two[p]
         work[3, p] = sweep_zero[p] - 0.5 * force_zero[p]
         work[4, p] = sweep_one[p] - 0.5 * force_one[p]
+        two[planes, 0, p] = means_two[p]
 
 
 def low_high(near, far):
@@ -274,40 +263,42 @@
     return [v[0] for v in pairs], [v[1] for v in pairs]
 
 
-def coarse_chain(first, first_low, first_high, bend_low, bend_high, work, low, high, own_low, own_high):
+def with_halo(work, low, high, own_low, own_high):
+    half = work.shape[1]
+    one = [work[3, p] for p in range(half)]
+    two = [work[4, p] for p in range(half)]
+    for p, got, own in ((0, low, own_low), (half - 1, high, own_high)):
+        one[p] = one[p] + got[0]
+        two[p] = two[p] + got[1] + (0.5 * COARSE) * own[0]
+    return one, two
+
+
+def coarse_steps(first, ends, bends, sweep_one, sweep_two):
     half = len(first)
     force = coarse_force(first)
-    one = []
-    for p in range(half):
-        v = first[p] + 0.5 * force[p] + work[3, p]
-        if p == 0:
-            v = v + low[0] + first_low
-        if p == half - 1:
-            v = v + high[0] + first_high
-        one.append(v)
+    one = [first[p] + 0.5 * force[p] + sweep_one[p] for p in range(half)]
+    for p, end in zip((0, half - 1), ends):
+        one[p] = one[p] + end
     force = coarse_force(one)
-    two = []
-    for p in range(half):
-        v = one[p] + 0.5 * force[p] + work[4, p]
-        if p == 0:
-            v = v + low[1] + (0.5 * COARSE) * (own_low[0] + bend_low)
-        if p == half - 1:
-            v = v + high[1] + (0.5 * COARSE) * (own_high[0] + bend_high)
-        two.append(v)
+    two = [one[p] + 0.5 * force[p] + sweep_two[p] for p in range(half)]
+    for p, bend in zip((0, half - 1), bends):
+        two[p] = two[p] + (0.5 * COARSE) * bend
     return one, two
 
 
-def fourth_kernel(work, near, far, own_near, own_far, held, partner, send_near, send_far, passed):
-    del held, passed
+def fourth_kernel(work, near, far, own_near, own_far, end, send_near, send_far, swept):
     half = work.shape[1]
     first = [work[0, p] for p in range(half)]
     low, high = sides(near, far)
     own_low, own_high = sides(own_near, own_far)
-    one, two = coarse_chain(first, 0.0, 0.0, 0.0, 0.0, work, low, high, own_low, own_high)
+    sweeps = with_halo(work, low, high, own_low, own_high)
+    _, two = coarse_steps(first, (0.0, 0.0), (0.0, 0.0), *sweeps)
+    for k, parts in enumerate(sweeps):
+        for p in range(half):
+            swept[k, p] = parts[p]
     force = coarse_force(two)
     for p in range(half):
-        partner[0, p] = two[p]
-        partner[1, p] = two[p] - work[2, p]
+        end[p] = two[p]
     send_near[0], send_far[0] = low_high(two[0], two[half - 1])
     send_near[1], send_far[1] = low_high(
         two[0] + 0.5 * force[0], two[half - 1] + 0.5 * force[half - 1]
@@ -315,16 +306,13 @@
 
 
 def last_kernel(
-    nodes, one, two, moved, work, near, far, own_near, own_far, partner, ring_near, ring_far,
+    nodes, ring_far, ring_near, end, one, two, moved, work, swept,
     updated, held, result, load_sem, store_sem,
 ):
     planes, halves = one.shape[0], one.shape[1]
     rows = one.shape[3]
     half = planes // 2
     section = lax.axis_index("tm")
-    low, high = sides(near, far)
-    own_low, own_high = sides(own_near, own_far)
-    ring_low, ring_high = sides(ring_near, ring_far)
     loads = [
         pltpu.make_async_copy(
             nodes.at[0, 0, :, :, pl.ds(h * LANES, LANES)], held.at[:, h], load_sem.at[h]
@@ -333,73 +321,65 @@
     ]
     for copy in loads:
         copy.start()
-    first, change = [], []
-    for p in range(half):
-        first.append(jnp.where(section == 0, work[0, p], partner[0, p]))
-        change.append(jnp.where(section == 0, first[p] - work[0, p], partner[1, p]))
-    scale = 0.5 * COARSE
-    coarse_one, coarse_two = coarse_chain(
-        first,
-        jnp.where(section == 0, 0.0, scale * ring_low[0]),
-        jnp.where(section == 0, 0.0, scale * ring_high[0]),
-        jnp.where(section == 0, 0.0, ring_low[1] + scale * first[0]),
-        jnp.where(section == 0, 0.0, ring_high[1] + scale * first[half - 1]),
-        work, low, high, own_low, own_high,
-    )
     spread = spread_matrix(LANES * halves // 2)
+    first = [jnp.where(section == 0, work[0, p], end[p]) for p in range(half)]
     stores = []
 
-    def put(node, p):
-        for h in range(halves):
-            copy = pltpu.make_async_copy(
-                result.at[node, p, h],
-                updated.at[0, node, p, :, pl.ds(h * LANES, LANES)],
-                store_sem.at[node, p, h],
-            )
-            copy.start()
-            stores.append(copy)
-
-    for node, base in ((1, one), (2, two)):
-        for top in range(half):
-            diff = (coarse_one[top] if node == 1 else coarse_two[top]) - work[node, top]
-            wide = times(diff, spread)
-            for p in (2 * top, 2 * top + 1):
-                for h in range(halves):
-                    for q in range(2):
-                        result[node, p, h, pl.ds(q, rows, stride=2), :] = (
-                            base[p, h, q] + wide[:, h * LANES : (h + 1) * LANES]
-                        )
-                put(node, p)
+    def put(node, top, change, base):
+        wide = times(change, spread)
+        for p in (2 * top, 2 * top + 1):
+            for h in range(halves):
+                for q in range(2):
+                    result[node, p, h, pl.ds(q, rows, stride=2), :] = (
+                        base(p, h, q) + wide[:, h * LANES : (h + 1) * LANES]
+                    )
+                copy = pltpu.make_async_copy(
+                    result.at[node, p, h],
+                    updated.at[0, node, p, :, pl.ds(h * LANES, LANES)],
+                    store_sem.at[node, p, h],
+                )
+                copy.start()
+                stores.append(copy)
+
+    def start(p, h, q):
+        own = held[p, h, pl.ds(q, rows, stride=2), :]
+        return jnp.where(section == 0, own, moved[p, h, q])
+
     for copy in loads:
         copy.wait()
     for top in range(half):
-        wide = times(change[top], spread)
-        for p in (2 * top, 2 * top + 1):
-            for h in range(halves):
-                for q in range(2):
-                    own = held[p, h, pl.ds(q, rows, stride=2), :]
-                    start = jnp.where(section == 0, own, moved[p, h, q])
-                    result[0, p, h, pl.ds(q, rows, stride=2), :] = (
-                        start + wide[:, h * LANES : (h + 1) * LANES]
-                    )
-            put(0, p)
+        mean = jnp.where(section == 0, work[0, top], moved[planes, 0, top])
+        put(0, top, first[top] - mean, start)
+
+    ring_low, ring_high = sides(ring_near, ring_far)
+    scale = 0.5 * COARSE
+    ends = [jnp.where(section == 0, 0.0, scale * v[0]) for v in (ring_low, ring_high)]
+    bends = [
+        jnp.where(section == 0, 0.0, v[1] + scale * first[p])
+        for v, p in ((ring_low, 0), (ring_high, half - 1))
+    ]
+    coarse_one, coarse_two = coarse_steps(
+        first, ends, bends, *[[swept[k, p] for p in range(half)] for k in range(2)]
+    )
+    for top in range(half):
+        put(1, top, coarse_one[top] - work[1, top], lambda p, h, q: one[p, h, q])
+    for top in range(half):
+        put(2, top, coarse_two[top] - work[2, top], lambda p, h, q: two[p, h, q])
     for copy in stores:
         copy.wait()
 
 
 def call(kernel, name, inputs, any_inputs, outs, scratch=(), any_outs=(), limit=VMEM_LIMIT,
          aliases=None, flops=0, size=0):
-    def spec(far, passed):
-        return pl.BlockSpec(
-            memory_space=pl.ANY if passed else pltpu.HBM if far else pltpu.VMEM
-        )
+    def spec(far):
+        return pl.BlockSpec(memory_space=pl.ANY if far else pltpu.VMEM)
 
     return pl.pallas_call(
         kernel,
         name=name,
         out_shape=[jax.ShapeDtypeStruct(s, F32) for s in outs],
-        in_specs=[spec(k in any_inputs, k in (aliases or {})) for k in range(len(inputs))],
-        out_specs=[spec(k in any_outs, k in (aliases or {}).values()) for k in range(len(outs))],
+        in_specs=[spec(k in any_inputs) for k in range(len(inputs))],
+        out_specs=[spec(k in any_outs) for k in range(len(outs))],
         scratch_shapes=list(scratch),
         input_output_aliases=aliases or {},
         compiler_params=pltpu.CompilerParams(vmem_limit_bytes=limit),
@@ -428,7 +408,7 @@
 def handed_on(near, far):
     peers = lax.axis_size("space")
     out = []
-    for value, to in zip((near, far), pairings(peers)):
+    for value, to in zip((far, near), pairings(peers)[::-1]):
         perm = [(i, peers + to[i]) for i in range(peers)] + [(peers + i, i) for i in range(peers)]
         out.append(lax.ppermute(value, ("tm", "space"), perm))
     return out
@@ -446,18 +426,18 @@
 
     a_near, a_far = call(
         edge_kernel, "edge_mix", (nodes,), (0,), [plane, plane],
-        [pltpu.VMEM((2, 3, halves, ny, LANES), F32), pltpu.SemaphoreType.DMA((2, 3, halves))],
-        size=size * 2, flops=size,
+        [
+            pltpu.VMEM((2, 3, ny, nz), F32),
+            pltpu.VMEM((2, halves, ny, LANES), F32),
+            pltpu.SemaphoreType.DMA((2, 3)),
+        ],
+        limit=EDGE_LIMIT, size=size * 2, flops=size,
     )
     got_a_near, got_a_far = exchange(a_near, a_far)
     one_part, slope, rest, b_near, b_far, coarse_zero = call(
-        first_kernel, "first_stage", (nodes,), (0,), [field, field, field, plane, plane, packed],
-        [
-            pltpu.VMEM((3, planes, halves, ny, LANES), F32),
-            pltpu.VMEM(field, F32),
-            pltpu.VMEM(field, F32),
-            pltpu.SemaphoreType.DMA((3, planes, halves)),
-        ],
+        first_kernel, "first_stage", (nodes,), (), [field, field, field, plane, plane, packed],
+        [pltpu.VMEM((5, ny, LANES), F32), pltpu.VMEM(field, F32), pltpu.VMEM(field, F32)],
+        limit=FIRST_LIMIT,
         size=size * 6, flops=size * 10,
     )
     got_b_near, got_b_far = exchange(b_near, b_far)
@@ -469,21 +449,20 @@
     )
     two, h_near, h_far, work = call(
         third_kernel, "third_stage", (two_part, got_b_near, got_b_far, coarse_zero, coarse_mid), (),
-        [field, pair, pair, (5, half) + quarter],
+        [(planes + 1,) + plane, pair, pair, (5, half) + quarter],
         size=size * 3, flops=size * 5,
     )
+    moved = swapped(two)
     got_near, got_far = exchange(h_near, h_far)
-    partner, f_near, f_far, two = call(
-        fourth_kernel, "coarse_chain", (work, got_near, got_far, h_near, h_far, two), (5,),
-        [(2, half) + quarter, pair, pair, field], any_outs=(3,), aliases={5: 3},
-        size=size, flops=size,
-    )
-    ring_near, ring_far = handed_on(f_near, f_far)
-    partner = swapped(partner)
-    moved = swapped(two)
+    end, f_near, f_far, swept = call(
+        fourth_kernel, "coarse_chain", (work, got_near, got_far, h_near, h_far), (),
+        [(half,) + quarter, pair, pair, (2, half) + quarter], size=size, flops=size,
+    )
+    ring_far, ring_near = handed_on(f_near, f_far)
+    end = swapped(end)
     updated, = call(
         last_kernel, "update",
-        (nodes, one, two, moved, work, got_near, got_far, h_near, h_far, partner, ring_near, ring_far),
+        (nodes, ring_far, ring_near, end, one, two, moved, work, swept),
         (0,), [(1, 3, planes, ny, nz)],
         [
             pltpu.VMEM((planes, halves, ny, LANES), F32),

time: 49.6 us -> 47.8 us (0.964)
  waiting for transfers between devices: 24 us -> 19.5 us
  Pallas kernels: 8.7 us -> 11.5 us
  local copies, waits for them, and re-layouts: 1.9 us -> 0.01 us
  starting transfers between devices: 14.8 us -> 16.6 us
    ppermute x2, waiting for transfers between devices: 7.09 us -> 3.43 us  [handed_on(): out.append(lax.ppermute(value, ('tm', 'space'), perm))]
    ppermute x2, starting transfers between devices: 0.43 us -> 3.71 us  [handed_on(): out.append(lax.ppermute(value, ('tm', 'space'), perm))]
    pallas_call x6, Pallas kernels: 8.7 us -> 11.5 us  [call(): pl.pallas_call(kernel, name=name, out_shape=[jax.ShapeDtypeStruct(s, F32)...]
    unnamed x4 -> x2, local copies, waits for them, and re-layouts: 1.9 us -> 0.01 us
    ppermute x2, starting transfers between devices: 3.1 us -> 1.3 us  [swapped(): return lax.ppermute(value, 'tm', [(0, 1), (1, 0)])]
    ppermute x3, waiting for transfers between devices: 3.27 us -> 1.77 us  [exchange(): lax.ppermute(far, 'space', list(enumerate(to_far)))]
    ppermute x3, waiting for transfers between devices: 13.6 us -> 14.3 us  [exchange(): lax.ppermute(near, 'space', list(enumerate(to_near)))]
  transfers between devices with their start and end apart: 10 -> 10, of which waited for: 5 -> 5; matrix products, arithmetic and copies ran while one was open for 0% -> 0% of each run, Pallas kernels for 9% -> 14%
where the time goes in v3:
time: 47.8 us; the launch traced here: 47.6 us
  waiting for transfers between devices  19.5 us (41%)
  starting transfers between devices  16.6 us (35%)
  Pallas kernels  11.5 us (24%)
    ppermute x3, waiting for transfers between devices, exchange(): lax.ppermute(near, 'space', list(enumerate(to_near)))  14.3 us
    pallas_call x6, Pallas kernels, call(): pl.pallas_call(kernel, name=name, out_shape=[jax.ShapeDtypeStruct(s, F32)...  11.5 us
    ppermute x3, starting transfers between devices, exchange(): lax.ppermute(far, 'space', list(enumerate(to_far)))  7.87 us
    ppermute x2, starting transfers between devices, handed_on(): out.append(lax.ppermute(value, ('tm', 'space'), perm))  3.71 us
    ppermute x3, starting transfers between devices, exchange(): lax.ppermute(near, 'space', list(enumerate(to_near)))  3.68 us
    ppermute x2, waiting for transfers between devices, handed_on(): out.append(lax.ppermute(value, ('tm', 'space'), perm))  3.43 us
    ppermute x3, waiting for transfers between devices, exchange(): lax.ppermute(far, 'space', list(enumerate(to_far)))  1.77 us
    ppermute x2, starting transfers between devices, swapped(): return lax.ppermute(value, 'tm', [(0, 1), (1, 0)])  1.3 us
  transfers between devices with their start and end apart: 10, of which 5 were waited for; matrix products, arithmetic and copies ran while one was open for 0% of the time, Pallas kernels for 14%

profile of v3, /device:TPU:1, one launch (start us, length us, event | category | flops | bytes accessed | tf_op | source)
XLA Modules:
  0.0 47.6 jit_solution(2864990874840256553)
XLA Ops:
  0.0 1.5 %edge_mix.1 = (f32[2,2,128,128]{3,2,1,0:T(8,128)S(1)}, f32[2,2,128,128]{3,2,1,0:T(8,128)S(1)}) custom-call(f32[1,3,4,256,256]{4,3,2,1,0:T(8,128)} %nodes.5), custom_call_target="tpu_custom_call" | custom-call | flops 1048576 | bytes 2097152 | tf_op jit(solution)/shard_map/edge_mix/pallas_call | solution.py:377
  1.5 2.1 %collective-permute-start = (f32[2,2,128,128]{3,2,1,0:T(8,128)S(1)}, f32[2,2,128,128]{3,2,1,0:T(8,128)S(1)}, u32[]{:S(2)}, u32[]{:S(2)}) collective-permute-start(f32[2,2,128,128]{3,2,1,0:T(8,128)S(1)} %get-tuple-element.27.own_near), channel_id=1, source_target_pairs={{0,1},{1,0},{2,3},{3,2},{4,5},{5,4},{6,7},{7,6},{8,9},{9,8},{10,11... | collective-permute-start | bytes 786440 | tf_op jit(solution)/shard_map/ppermute | solution.py:399
  3.6 3.3 %collective-permute-start.1 = (f32[2,2,128,128]{3,2,1,0:T(8,128)S(1)}, f32[2,2,128,128]{3,2,1,0:T(8,128)S(1)}, u32[]{:S(2)}, u32[]{:S(2)}) collective-permute-start(f32[2,2,128,128]{3,2,1,0:T(8,128)S(1)} %get-tuple-element.28.own_far), channel_id=1, source_target_pairs={{0,7},{1,2},{2,1},{3,4},{4,3},{5,6},{6,5},{7,0},{8,15},{9,10},{10,... | collective-permute-start | bytes 786440 | tf_op jit(solution)/shard_map/ppermute | solution.py:400
  6.9 4.7 %first_stage.1 = (f32[4,2,2,128,128]{4,3,2,1,0:T(8,128)S(1)}, f32[4,2,2,128,128]{4,3,2,1,0:T(8,128)S(1)}, f32[4,2,2,128,128]{4,3,2,1,0:T(8,128)S(1)}, f32[2,2,12...) custom-call(f32[1,3,4,256,256]{4,3,2,1,0:T(8,128)} %nodes.5), custom_call_target="tpu_custom_call" | custom-call | flops 10485760 | bytes 6291456 | tf_op jit(solution)/shard_map/first_stage/pallas_call | solution.py:377
  11.6 0.1 collective-permute-start.2
  11.7 1.3 %collective-permute-start.3 = (f32[2,2,128,128]{3,2,1,0:T(8,128)S(1)}, f32[2,2,128,128]{3,2,1,0:T(8,128)S(1)}, u32[]{:S(2)}, u32[]{:S(2)}) collective-permute-start(f32[2,2,128,128]{3,2,1,0:T(8,128)S(1)} %get-tuple-element.31), channel_id=1, source_target_pairs={{0,7},{1,2},{2,1},{3,4},{4,3},{5,6},{6,5},{7,0},{8,15},{9,10},{10,... | collective-permute-start | bytes 786440 | tf_op jit(solution)/shard_map/ppermute | solution.py:400
  13.0 2.3 %collective-permute-done.near = f32[2,2,128,128]{3,2,1,0:T(8,128)S(1)} collective-permute-done((f32[2,2,128,128]{3,2,1,0:T(8,128)S(1)}, f32[2,2,128,128]{3,2,1,0:T(8,128)S(1)}, u32[]{:S(2)}, u32[]{:S(2)}) %collective-permute-start) | collective-permute-done | bytes 262176 | tf_op jit(solution)/shard_map/ppermute | solution.py:399
  15.3 0.0 collective-permute-done.1.far
  15.3 1.6 %second_stage.1 = (f32[4,2,2,128,128]{4,3,2,1,0:T(8,128)S(1)}, f32[4,2,2,128,128]{4,3,2,1,0:T(8,128)S(1)}, f32[3,2,128,128]{3,2,1,0:T(8,128)S(1)}) custom-call(f32[4,2,2,128,128]{4,3,2,1,0:T(8,128)S(1)} %get-tuple-element.24.one_in, f32[4,2,2,128,128]{4,3,2,1,0:T(8,128)S(1)} %get-tuple-element.25.slope, f32[4,2,2,128,128]{4,3,2,1,0:T(8,128)S(1)} %get-tuple-element.26.rest, ...), custom_call_target="tpu_custom_call" | custom-call | flops 10485760 | bytes 6291456 | tf_op jit(solution)/shard_map/second_stage/pallas_call | solution.py:377
  16.9 9.6 %collective-permute-done.2.near = f32[2,2,128,128]{3,2,1,0:T(8,128)S(1)} collective-permute-done((f32[2,2,128,128]{3,2,1,0:T(8,128)S(1)}, f32[2,2,128,128]{3,2,1,0:T(8,128)S(1)}, u32[]{:S(2)}, u32[]{:S(2)}) %collective-permute-start.2) | collective-permute-done | bytes 262176 | tf_op jit(solution)/shard_map/ppermute | solution.py:399
  26.5 0.0 collective-permute-done.3.far
  26.5 1.0 %third_stage.1 = (f32[5,2,2,128,128]{4,3,2,1,0:T(8,128)S(1)}, f32[2,128,128]{2,1,0:T(8,128)S(1)}, f32[2,128,128]{2,1,0:T(8,128)S(1)}, f32[5,2,128,128]{3,2,1,0:T(8,128)S(1)}) custom-call(f32[4,2,2,128,128]{4,3,2,1,0:T(8,128)S(1)} %get-tuple-element.29.two_in, f32[2,2,128,128]{3,2,1,0:T(8,128)S(1)} %collective-permute-done.2.near, ...), custom_call_target="tpu_custom_call" | custom-call | flops 5242880 | bytes 3145728 | tf_op jit(solution)/shard_map/third_stage/pallas_call | solution.py:377
  27.5 1.3 %collective-permute-start.9 = (f32[5,2,2,128,128]{4,3,2,1,0:T(8,128)S(1)}, f32[5,2,2,128,128]{4,3,2,1,0:T(8,128)S(1)}, u32[]{:S(2)}, u32[]{:S(2)}) collective-permute-start(f32[5,2,2,128,128]{4,3,2,1,0:T(8,128)S(1)} %get-tuple-element.41.two), channel_id=1, source_target_pairs={{0,8},{8,0},{1,9},{9,1},{2,10},{10,2},{3,11},{11,3},{4,12},{12,4},... | collective-permute-start | bytes 3932168 | tf_op jit(solution)/shard_map/ppermute | solution.py:405
  28.8 1.5 %collective-permute-start.4 = (f32[2,128,128]{2,1,0:T(8,128)S(1)}, f32[2,128,128]{2,1,0:T(8,128)S(1)}, u32[]{:S(2)}, u32[]{:S(2)}) collective-permute-start(f32[2,128,128]{2,1,0:T(8,128)S(1)} %get-tuple-element.35.own_near), channel_id=1, source_target_pairs={{0,1},{1,0},{2,3},{3,2},{4,5},{5,4},{6,7},{7,6},{8,9},{9,8},{10,11... | collective-permute-start | bytes 393224 | tf_op jit(solution)/shard_map/ppermute | solution.py:399
  30.3 3.3 %collective-permute-start.5 = (f32[2,128,128]{2,1,0:T(8,128)S(1)}, f32[2,128,128]{2,1,0:T(8,128)S(1)}, u32[]{:S(2)}, u32[]{:S(2)}) collective-permute-start(f32[2,128,128]{2,1,0:T(8,128)S(1)} %get-tuple-element.36.own_far), channel_id=1, source_target_pairs={{0,7},{1,2},{2,1},{3,4},{4,3},{5,6},{6,5},{7,0},{8,15},{9,10},{10,... | collective-permute-start | bytes 393224 | tf_op jit(solution)/shard_map/ppermute | solution.py:400
  33.6 2.4 %collective-permute-done.4.near = f32[2,128,128]{2,1,0:T(8,128)S(1)} collective-permute-done((f32[2,128,128]{2,1,0:T(8,128)S(1)}, f32[2,128,128]{2,1,0:T(8,128)S(1)}, u32[]{:S(2)}, u32[]{:S(2)}) %collective-permute-start.4) | collective-permute-done | bytes 131104 | tf_op jit(solution)/shard_map/ppermute | solution.py:399
  36.0 1.8 %collective-permute-done.5.far = f32[2,128,128]{2,1,0:T(8,128)S(1)} collective-permute-done((f32[2,128,128]{2,1,0:T(8,128)S(1)}, f32[2,128,128]{2,1,0:T(8,128)S(1)}, u32[]{:S(2)}, u32[]{:S(2)}) %collective-permute-start.5) | collective-permute-done | bytes 131104 | tf_op jit(solution)/shard_map/ppermute | solution.py:400
  37.7 0.4 coarse_chain.1
  38.1 1.2 %collective-permute-start.6 = (f32[2,128,128]{2,1,0:T(8,128)S(1)}, f32[2,128,128]{2,1,0:T(8,128)S(1)}, u32[]{:S(2)}, u32[]{:S(2)}) collective-permute-start(f32[2,128,128]{2,1,0:T(8,128)S(1)} %get-tuple-element.37), channel_id=1, source_target_pairs={{0,15},{1,10},{2,9},{3,12},{4,11},{5,14},{6,13},{7,8},{8,0},{9,1},... | collective-permute-start | bytes 393224 | tf_op jit(solution)/shard_map/ppermute | solution.py:413
  39.3 2.5 %collective-permute-start.7 = (f32[2,128,128]{2,1,0:T(8,128)S(1)}, f32[2,128,128]{2,1,0:T(8,128)S(1)}, u32[]{:S(2)}, u32[]{:S(2)}) collective-permute-start(f32[2,128,128]{2,1,0:T(8,128)S(1)} %get-tuple-element.38), channel_id=1, source_target_pairs={{0,9},{1,8},{2,11},{3,10},{4,13},{5,12},{6,15},{7,14},{8,0},{9,1},... | collective-permute-start | bytes 393224 | tf_op jit(solution)/shard_map/ppermute | solution.py:413
  41.8 0.0 collective-permute-start.8
  41.8 3.4 %collective-permute-done.6.ring_far = f32[2,128,128]{2,1,0:T(8,128)S(1)} collective-permute-done((f32[2,128,128]{2,1,0:T(8,128)S(1)}, f32[2,128,128]{2,1,0:T(8,128)S(1)}, u32[]{:S(2)}, u32[]{:S(2)}) %collective-permute-start.6) | collective-permute-done | bytes 131104 | tf_op jit(solution)/shard_map/ppermute | solution.py:413
  45.2 0.0 collective-permute-done.7.ring_near
  45.3 2.3 %update.1 = f32[1,3,4,256,256]{4,3,2,1,0:T(8,128)} custom-call(f32[1,3,4,256,256]{4,3,2,1,0:T(8,128)S(1)} %copy-done, f32[2,128,128]{2,1,0:T(8,128)S(1)} %collective-permute-done.6.ring_far, f32[2,128,128]{2,1,0:T(8,128)S(1)} %collective-permute-done.7.ring_near, f32[2,128,128]{2,1,0:T(8,128)S(1)} %collective-permute-done.8.end, ...), custom_call_target="tpu_custom_call" | custom-call | flops 5242880 | bytes 6291456 | tf_op jit(solution)/shard_map/update/pallas_call | solution.py:377
  (4 shorter events, 0.0 us)
Async XLA Ops:
  1.5 13.8 %collective-permute-start = (f32[2,2,128,128]{3,2,1,0:T(8,128)S(1)}, f32[2,2,128,128]{3,2,1,0:T(8,128)S(1)}, u32[]{:S(2)}, u32[]{:S(2)}) collective-permute-start(f32[2,2,128,128]{3,2,1,0:T(8,128)S(1)} %get-tuple-element.27.own_near), channel_id=1, source_target_pairs={{0,1},{1,0},{2,3},{3,2},{4,5},{5,4},{6,7},{7,6},{8,9},{9,8},{10,11... | collective-permute-start | bytes 786440 | tf_op jit(solution)/shard_map/ppermute | solution.py:399
  3.6 11.7 %collective-permute-start.1 = (f32[2,2,128,128]{3,2,1,0:T(8,128)S(1)}, f32[2,2,128,128]{3,2,1,0:T(8,128)S(1)}, u32[]{:S(2)}, u32[]{:S(2)}) collective-permute-start(f32[2,2,128,128]{3,2,1,0:T(8,128)S(1)} %get-tuple-element.28.own_far), channel_id=1, source_target_pairs={{0,7},{1,2},{2,1},{3,4},{4,3},{5,6},{6,5},{7,0},{8,15},{9,10},{10,... | collective-permute-start | bytes 786440 | tf_op jit(solution)/shard_map/ppermute | solution.py:400
  11.6 14.9 %collective-permute-start.2 = (f32[2,2,128,128]{3,2,1,0:T(8,128)S(1)}, f32[2,2,128,128]{3,2,1,0:T(8,128)S(1)}, u32[]{:S(2)}, u32[]{:S(2)}) collective-permute-start(f32[2,2,128,128]{3,2,1,0:T(8,128)S(1)} %get-tuple-element.30), channel_id=1, source_target_pairs={{0,1},{1,0},{2,3},{3,2},{4,5},{5,4},{6,7},{7,6},{8,9},{9,8},{10,11... | collective-permute-start | bytes 786440 | tf_op jit(solution)/shard_map/ppermute | solution.py:399
  11.7 14.9 %collective-permute-start.3 = (f32[2,2,128,128]{3,2,1,0:T(8,128)S(1)}, f32[2,2,128,128]{3,2,1,0:T(8,128)S(1)}, u32[]{:S(2)}, u32[]{:S(2)}) collective-permute-start(f32[2,2,128,128]{3,2,1,0:T(8,128)S(1)} %get-tuple-element.31), channel_id=1, source_target_pairs={{0,7},{1,2},{2,1},{3,4},{4,3},{5,6},{6,5},{7,0},{8,15},{9,10},{10,... | collective-permute-start | bytes 786440 | tf_op jit(solution)/shard_map/ppermute | solution.py:400
  15.3 30.0 %copy-start = (f32[1,3,4,256,256]{4,3,2,1,0:T(8,128)S(1)}, f32[1,3,4,256,256]{4,3,2,1,0:T(8,128)}, u32[]{:S(2)}) copy-start(f32[1,3,4,256,256]{4,3,2,1,0:T(8,128)} %nodes.5) | copy-start | bytes 9437188
  27.5 17.7 %collective-permute-start.9 = (f32[5,2,2,128,128]{4,3,2,1,0:T(8,128)S(1)}, f32[5,2,2,128,128]{4,3,2,1,0:T(8,128)S(1)}, u32[]{:S(2)}, u32[]{:S(2)}) collective-permute-start(f32[5,2,2,128,128]{4,3,2,1,0:T(8,128)S(1)} %get-tuple-element.41.two), channel_id=1, source_target_pairs={{0,8},{8,0},{1,9},{9,1},{2,10},{10,2},{3,11},{11,3},{4,12},{12,4},... | collective-permute-start | bytes 3932168 | tf_op jit(solution)/shard_map/ppermute | solution.py:405
  28.8 7.1 %collective-permute-start.4 = (f32[2,128,128]{2,1,0:T(8,128)S(1)}, f32[2,128,128]{2,1,0:T(8,128)S(1)}, u32[]{:S(2)}, u32[]{:S(2)}) collective-permute-start(f32[2,128,128]{2,1,0:T(8,128)S(1)} %get-tuple-element.35.own_near), channel_id=1, source_target_pairs={{0,1},{1,0},{2,3},{3,2},{4,5},{5,4},{6,7},{7,6},{8,9},{9,8},{10,11... | collective-permute-start | bytes 393224 | tf_op jit(solution)/shard_map/ppermute | solution.py:399
  30.3 7.4 %collective-permute-start.5 = (f32[2,128,128]{2,1,0:T(8,128)S(1)}, f32[2,128,128]{2,1,0:T(8,128)S(1)}, u32[]{:S(2)}, u32[]{:S(2)}) collective-permute-start(f32[2,128,128]{2,1,0:T(8,128)S(1)} %get-tuple-element.36.own_far), channel_id=1, source_target_pairs={{0,7},{1,2},{2,1},{3,4},{4,3},{5,6},{6,5},{7,0},{8,15},{9,10},{10,... | collective-permute-start | bytes 393224 | tf_op jit(solution)/shard_map/ppermute | solution.py:400
  38.1 7.1 %collective-permute-start.6 = (f32[2,128,128]{2,1,0:T(8,128)S(1)}, f32[2,128,128]{2,1,0:T(8,128)S(1)}, u32[]{:S(2)}, u32[]{:S(2)}) collective-permute-start(f32[2,128,128]{2,1,0:T(8,128)S(1)} %get-tuple-element.37), channel_id=1, source_target_pairs={{0,15},{1,10},{2,9},{3,12},{4,11},{5,14},{6,13},{7,8},{8,0},{9,1},... | collective-permute-start | bytes 393224 | tf_op jit(solution)/shard_map/ppermute | solution.py:413
  39.3 5.9 %collective-permute-start.7 = (f32[2,128,128]{2,1,0:T(8,128)S(1)}, f32[2,128,128]{2,1,0:T(8,128)S(1)}, u32[]{:S(2)}, u32[]{:S(2)}) collective-permute-start(f32[2,128,128]{2,1,0:T(8,128)S(1)} %get-tuple-element.38), channel_id=1, source_target_pairs={{0,9},{1,8},{2,11},{3,10},{4,13},{5,12},{6,15},{7,14},{8,0},{9,1},... | collective-permute-start | bytes 393224 | tf_op jit(solution)/shard_map/ppermute | solution.py:413
  41.8 3.4 %collective-permute-start.8 = (f32[2,128,128]{2,1,0:T(8,128)S(1)}, f32[2,128,128]{2,1,0:T(8,128)S(1)}, u32[]{:S(2)}, u32[]{:S(2)}) collective-permute-start(f32[2,128,128]{2,1,0:T(8,128)S(1)} %get-tuple-element.39), channel_id=1, source_target_pairs={{0,8},{8,0},{1,9},{9,1},{2,10},{10,2},{3,11},{11,3},{4,12},{12,4},... | collective-permute-start | bytes 393224 | tf_op jit(solution)/shard_map/ppermute | solution.py:405

commit v4 on v3

--- a/solution.py
+++ b/solution.py
@@ -1,5 +1,6 @@
 import jax
 import jax.numpy as jnp
+import numpy as np
 from jax import lax
 from jax.experimental import pallas as pl
 from jax.experimental.pallas import tpu as pltpu
@@ -80,20 +81,18 @@
 
 
 def pair_matrix(size):
-    row = lax.broadcasted_iota(jnp.int32, (size, size // 2), 0)
-    col = lax.broadcasted_iota(jnp.int32, (size, size // 2), 1)
-    offset = lax.rem(row - 2 * col + size, size)
-    inner = offset < 2
-    outer = (offset == 2) | (offset == size - 1)
-    sums = jnp.where(inner, 1.0, 0.0).astype(F32)
-    bends = jnp.where(outer, 1.0, 0.0).astype(F32) - sums
-    return sums.astype(BF16), bends.astype(BF16)
+    out = np.zeros((size, size), np.float32)
+    for k in range(size // 2):
+        for offset in (0, 1):
+            out[2 * k + offset, k] = 1.0
+            out[2 * k + offset, size // 2 + k] = -1.0
+        for offset in (-1, 2):
+            out[(2 * k + offset) % size, size // 2 + k] = 1.0
+    return jnp.asarray(out, BF16)
 
 
 def spread_matrix(size):
-    row = lax.broadcasted_iota(jnp.int32, (size, 2 * size), 0)
-    col = lax.broadcasted_iota(jnp.int32, (size, 2 * size), 1)
-    return jnp.where((col == 2 * row) | (col == 2 * row + 1), 1.0, 0.0).astype(F32).astype(BF16)
+    return jnp.asarray(np.repeat(np.eye(size, dtype=np.float32), 2, axis=1), BF16)
 
 
 def times(v, matrix):
@@ -103,9 +102,8 @@
     )
 
 
-def restrict_field(ref, planes, halves):
-    size = halves * LANES
-    sums, bends = pair_matrix(size)
+def restrict_field(ref, pairs, planes, halves):
+    sums, bends = pairs[:, : halves * LANES // 2], pairs[:, halves * LANES // 2 :]
 
     def y_sum(p):
         return [ref[p, h, 0] + ref[p, h, 1] for h in range(halves)]
@@ -170,7 +168,7 @@
                 out[h, q] = work[e, h, pl.ds(q, rows, stride=2), :]
 
 
-def first_kernel(nodes, one, slope, rest, near, far, coarse, work, start, mix):
+def first_kernel(nodes, pairs, one, slope, rest, near, far, coarse, work, start, mix):
     planes, halves = one.shape[0], one.shape[1]
     rows = one.shape[3]
     for p in range(planes):
@@ -193,10 +191,12 @@
             one[p, h, q] = one[p, h, q] + DIFFUSE * laplace
     for p, out in zip(outer_planes(planes), (near, far)):
         out[...] = 0.5 * one[p] + slope[p]
-    store_coarse(coarse, *restrict_field(start, planes, halves))
-
-
-def second_kernel(one_in, slope, rest, near, far, own_near, own_far, one, two, coarse, mix):
+    store_coarse(coarse, *restrict_field(start, pairs, planes, halves))
+
+
+def second_kernel(
+    one_in, slope, rest, near, far, own_near, own_far, pairs, one, two, coarse, inner, mix
+):
     planes, halves = one_in.shape[0], one_in.shape[1]
     outer = outer_planes(planes)
     for p in range(1, planes - 1):
@@ -213,17 +213,53 @@
             )
     for p, own in zip(outer, (own_near, own_far)):
         two[p] = two[p] + (0.5 * DIFFUSE * DIFFUSE) * own[...]
-    store_coarse(coarse, *restrict_field(one, planes, halves))
-
-
-def third_kernel(two_in, near, far, coarse_zero, coarse_one, two, send_near, send_far, work):
-    planes, halves = two_in.shape[0], two_in.shape[1]
+    for k, p in enumerate((1, planes - 2)):
+        for h in range(halves):
+            even, odd = two[p, h, 0], two[p, h, 1]
+            inner[k, 0, h] = even
+            inner[k, 1, h] = odd
+            inner[k, 2, h] = GROWTH * (even + odd - cube(even) - cube(odd))
+    store_coarse(coarse, *restrict_field(one, pairs, planes, halves))
+
+
+def third_kernel(
+    two_in, near, far, inner, coarse_zero, coarse_one, pairs, two, send_near, send_far, work, outer
+):
+    planes, halves = two_in.shape[0] - 1, two_in.shape[1]
     later = lax.axis_index("tm").astype(F32)
-    for p in range(1, planes - 1):
-        two[p] = two_in[p]
     for p, halo in zip(outer_planes(planes), (near, far)):
-        two[p] = two_in[p] + DIFFUSE * halo[...]
-    means_two, forces_two, edges_two = restrict_field(two, planes, halves)
+        outer[p // (planes - 1)] = two_in[p] + DIFFUSE * halo[...]
+    totals, rests, flats = [], [], []
+    other_flats = [[inner[k, 0, h] + inner[k, 1, h] for h in range(halves)] for k in range(2)]
+    for k in range(2):
+        two[k * (planes - 1)] = outer[k]
+        total, rest, flat = [], [], []
+        for h in range(halves):
+            own = outer[k, h, 0], outer[k, h, 1]
+            even, odd = own[0] + inner[k, 0, h], own[1] + inner[k, 1, h]
+            line = own[0] + own[1]
+            full = line + other_flats[k][h]
+            rows = full.shape[0]
+            flux = pltpu.roll(odd, 1, 0) + pltpu.roll(even, rows - 1, 0) - 2.0 * full
+            flux = flux + other_flats[1 - k][h]
+            total.append(full)
+            flat.append(line)
+            rest.append(
+                DIFFUSE * flux + (GROWTH * (line - cube(own[0]) - cube(own[1])) + inner[k, 2, h])
+            )
+        totals.append(jnp.concatenate(total, axis=1))
+        rests.append(jnp.concatenate(rest, axis=1))
+        flats.append(jnp.concatenate(flat, axis=1))
+    wide = times(jnp.concatenate(totals + flats, axis=0), pairs[...])
+    tall = times(jnp.concatenate(rests, axis=0), pairs[:, : halves * LANES // 2])
+    rows, lanes = tall.shape[0] // 2, tall.shape[1]
+    means_two = [0.125 * wide[k * rows : (k + 1) * rows, :lanes] for k in range(2)]
+    edges_two = [wide[k * rows : (k + 1) * rows, :lanes] for k in (2, 3)]
+    forces_two = [
+        0.125
+        * (tall[k * rows : (k + 1) * rows] + DIFFUSE * wide[k * rows : (k + 1) * rows, lanes:])
+        for k in range(2)
+    ]
     half = planes // 2
     zero = [coarse_zero[0, p] for p in range(half)]
     mean_one = [coarse_one[0, p] for p in range(half)]
@@ -273,41 +309,68 @@
     return one, two
 
 
-def coarse_steps(first, ends, bends, sweep_one, sweep_two):
+def coarse_steps(first, sweep_one, sweep_two):
     half = len(first)
     force = coarse_force(first)
     one = [first[p] + 0.5 * force[p] + sweep_one[p] for p in range(half)]
-    for p, end in zip((0, half - 1), ends):
-        one[p] = one[p] + end
     force = coarse_force(one)
-    two = [one[p] + 0.5 * force[p] + sweep_two[p] for p in range(half)]
-    for p, bend in zip((0, half - 1), bends):
-        two[p] = two[p] + (0.5 * COARSE) * bend
-    return one, two
+    return [one[p] + 0.5 * force[p] + sweep_two[p] for p in range(half)]
 
 
 def fourth_kernel(work, near, far, own_near, own_far, end, send_near, send_far, swept):
     half = work.shape[1]
-    first = [work[0, p] for p in range(half)]
     low, high = sides(near, far)
     own_low, own_high = sides(own_near, own_far)
-    sweeps = with_halo(work, low, high, own_low, own_high)
-    _, two = coarse_steps(first, (0.0, 0.0), (0.0, 0.0), *sweeps)
-    for k, parts in enumerate(sweeps):
+    for k, parts in enumerate(with_halo(work, low, high, own_low, own_high)):
         for p in range(half):
             swept[k, p] = parts[p]
-    force = coarse_force(two)
-    for p in range(half):
-        end[p] = two[p]
-    send_near[0], send_far[0] = low_high(two[0], two[half - 1])
-    send_near[1], send_far[1] = low_high(
-        two[0] + 0.5 * force[0], two[half - 1] + 0.5 * force[half - 1]
-    )
+
+    @pl.when(lax.axis_index("tm") == 0)
+    def _():
+        first = [work[0, p] for p in range(half)]
+        two = coarse_steps(first, *[[swept[k, p] for p in range(half)] for k in range(2)])
+        force = coarse_force(two)
+        for p in range(half):
+            end[p] = two[p]
+        send_near[0], send_far[0] = low_high(two[0], two[half - 1])
+        send_near[1], send_far[1] = low_high(
+            two[0] + 0.5 * force[0], two[half - 1] + 0.5 * force[half - 1]
+        )
+
+
+class Planes:
+    def __init__(self, spread, updated, parts, result, sem):
+        self.updated, self.parts, self.result, self.sem = updated, parts, result, sem
+        self.rows = parts.shape[2] // 2
+        self.halves = parts.shape[1]
+        self.spread = spread[...]
+        self.copies = []
+
+    def put(self, node, top, change, base):
+        wide = times(change, self.spread)
+        for p in (2 * top, 2 * top + 1):
+            slot = len(self.copies)
+            for h in range(self.halves):
+                lanes = slice(h * LANES, (h + 1) * LANES)
+                for q in range(2):
+                    self.parts[slot, h, pl.ds(q, self.rows, stride=2), :] = (
+                        base(p, h, q) + wide[:, lanes]
+                    )
+                self.result[slot, :, lanes] = self.parts[slot, h]
+            copy = pltpu.make_async_copy(
+                self.result.at[slot], self.updated.at[0, node, p], self.sem.at[slot]
+            )
+            copy.start()
+            self.copies.append(copy)
+
+    def finish(self):
+        for copy in self.copies:
+            copy.wait()
 
 
 def last_kernel(
-    nodes, ring_far, ring_near, end, one, two, moved, work, swept,
-    updated, held, result, load_sem, store_sem,
+    nodes, ring_far, ring_near, end, one, two, moved, work, swept, spread,
+    updated, held, parts, result, load_sem, sem,
 ):
     planes, halves = one.shape[0], one.shape[1]
     rows = one.shape[3]
@@ -319,54 +382,39 @@
         )
         for h in range(halves)
     ]
-    for copy in loads:
-        copy.start()
-    spread = spread_matrix(LANES * halves // 2)
+
+
+    @pl.when(section == 0)
+    def _():
+        for copy in loads:
+            copy.start()
+        for copy in loads:
+            copy.wait()
+
+    def start(p, h, q):
+        return jnp.where(section == 0, held[p, h, pl.ds(q, rows, stride=2), :], moved[p, h, q])
+
+    out = Planes(spread, updated, parts, result, sem)
     first = [jnp.where(section == 0, work[0, p], end[p]) for p in range(half)]
-    stores = []
-
-    def put(node, top, change, base):
-        wide = times(change, spread)
-        for p in (2 * top, 2 * top + 1):
-            for h in range(halves):
-                for q in range(2):
-                    result[node, p, h, pl.ds(q, rows, stride=2), :] = (
-                        base(p, h, q) + wide[:, h * LANES : (h + 1) * LANES]
-                    )
-                copy = pltpu.make_async_copy(
-                    result.at[node, p, h],
-                    updated.at[0, node, p, :, pl.ds(h * LANES, LANES)],
-                    store_sem.at[node, p, h],
-                )
-                copy.start()
-                stores.append(copy)
-
-    def start(p, h, q):
-        own = held[p, h, pl.ds(q, rows, stride=2), :]
-        return jnp.where(section == 0, own, moved[p, h, q])
-
-    for copy in loads:
-        copy.wait()
     for top in range(half):
         mean = jnp.where(section == 0, work[0, top], moved[planes, 0, top])
-        put(0, top, first[top] - mean, start)
-
+        out.put(0, top, first[top] - mean, start)
     ring_low, ring_high = sides(ring_near, ring_far)
     scale = 0.5 * COARSE
-    ends = [jnp.where(section == 0, 0.0, scale * v[0]) for v in (ring_low, ring_high)]
-    bends = [
-        jnp.where(section == 0, 0.0, v[1] + scale * first[p])
-        for v, p in ((ring_low, 0), (ring_high, half - 1))
-    ]
-    coarse_one, coarse_two = coarse_steps(
-        first, ends, bends, *[[swept[k, p] for p in range(half)] for k in range(2)]
-    )
+    force = coarse_force(first)
+    coarse_one = [first[p] + 0.5 * force[p] + swept[0, p] for p in range(half)]
+    for p, v in ((0, ring_low), (half - 1, ring_high)):
+        coarse_one[p] = coarse_one[p] + jnp.where(section == 0, 0.0, scale * v[0])
     for top in range(half):
-        put(1, top, coarse_one[top] - work[1, top], lambda p, h, q: one[p, h, q])
+        out.put(1, top, coarse_one[top] - work[1, top], lambda p, h, q: one[p, h, q])
+    force = coarse_force(coarse_one)
+    coarse_two = [coarse_one[p] + 0.5 * force[p] + swept[1, p] for p in range(half)]
+    for p, v in ((0, ring_low), (half - 1, ring_high)):
+        bend = jnp.where(section == 0, 0.0, v[1] + scale * first[p])
+        coarse_two[p] = coarse_two[p] + scale * bend
     for top in range(half):
-        put(2, top, coarse_two[top] - work[2, top], lambda p, h, q: two[p, h, q])
-    for copy in stores:
-        copy.wait()
+        out.put(2, top, coarse_two[top] - work[2, top], lambda p, h, q: two[p, h, q])
+    out.finish()
 
 
 def call(kernel, name, inputs, any_inputs, outs, scratch=(), any_outs=(), limit=VMEM_LIMIT,
@@ -424,6 +472,7 @@
     packed = (3, half) + quarter
     size = planes * ny * nz * 4
 
+    pairs, spread = pair_matrix(nz), spread_matrix(nz // 2)
     a_near, a_far = call(
         edge_kernel, "edge_mix", (nodes,), (0,), [plane, plane],
         [
@@ -435,22 +484,24 @@
     )
     got_a_near, got_a_far = exchange(a_near, a_far)
     one_part, slope, rest, b_near, b_far, coarse_zero = call(
-        first_kernel, "first_stage", (nodes,), (), [field, field, field, plane, plane, packed],
+        first_kernel, "first_stage", (nodes, pairs), (), [field, field, field, plane, plane, packed],
         [pltpu.VMEM((5, ny, LANES), F32), pltpu.VMEM(field, F32), pltpu.VMEM(field, F32)],
         limit=FIRST_LIMIT,
         size=size * 6, flops=size * 10,
     )
     got_b_near, got_b_far = exchange(b_near, b_far)
-    one, two_part, coarse_mid = call(
+    one, two_part, coarse_mid, inner = call(
         second_kernel, "second_stage",
-        (one_part, slope, rest, got_a_near, got_a_far, a_near, a_far), (),
-        [field, field, packed], [pltpu.VMEM(field, F32)],
+        (one_part, slope, rest, got_a_near, got_a_far, a_near, a_far, pairs), (),
+        [field, (planes + 1,) + plane, packed, (2, 3, halves, rows, LANES)],
+        [pltpu.VMEM(field, F32)],
         size=size * 6, flops=size * 10,
     )
     two, h_near, h_far, work = call(
-        third_kernel, "third_stage", (two_part, got_b_near, got_b_far, coarse_zero, coarse_mid), (),
-        [(planes + 1,) + plane, pair, pair, (5, half) + quarter],
-        size=size * 3, flops=size * 5,
+        third_kernel, "third_stage",
+        (two_part, got_b_near, got_b_far, inner, coarse_zero, coarse_mid, pairs), (),
+        [(planes + 1,) + plane, pair, pair, (5, half) + quarter], [pltpu.VMEM((2,) + plane, F32)],
+        aliases={0: 0}, size=size * 3, flops=size * 5,
     )
     moved = swapped(two)
     got_near, got_far = exchange(h_near, h_far)
@@ -462,13 +513,14 @@
     end = swapped(end)
     updated, = call(
         last_kernel, "update",
-        (nodes, ring_far, ring_near, end, one, two, moved, work, swept),
-        (0,), [(1, 3, planes, ny, nz)],
+        (nodes, ring_far, ring_near, end, one, two, moved, work, swept, spread), (0,),
+        [(1, 3, planes, ny, nz)],
         [
             pltpu.VMEM((planes, halves, ny, LANES), F32),
-            pltpu.VMEM((3, planes, halves, ny, LANES), F32),
+            pltpu.VMEM((3 * planes, halves, ny, LANES), F32),
+            pltpu.VMEM((3 * planes, ny, nz), F32),
             pltpu.SemaphoreType.DMA((halves,)),
-            pltpu.SemaphoreType.DMA((3, planes, halves)),
+            pltpu.SemaphoreType.DMA((3 * planes,)),
         ],
         any_outs=(0,), size=size * 6, flops=size * 5,
     )

time: 47.8 us -> 47.4 us (level)
  Pallas kernels: 11.5 us -> 10.7 us
    pallas_call x6, Pallas kernels: 11.5 us -> 10.7 us  [call(): pl.pallas_call(kernel, name=name, out_shape=[jax.ShapeDtypeStruct(s, F32)...]
  transfers between devices with their start and end apart: 10 -> 10, of which waited for: 5 -> 5; matrix products, arithmetic and copies ran while one was open for 0% -> 0% of each run, Pallas kernels for 14% -> 13%
where the time goes in v4:
time: 47.4 us; the launch traced here: 47.2 us
  waiting for transfers between devices  19.8 us (42%)
  starting transfers between devices  16.6 us (35%)
  Pallas kernels  10.7 us (23%)
    ppermute x3, waiting for transfers between devices, exchange(): lax.ppermute(near, 'space', list(enumerate(to_near)))  14.4 us
    pallas_call x6, Pallas kernels, call(): pl.pallas_call(kernel, name=name, out_shape=[jax.ShapeDtypeStruct(s, F32)...  10.7 us
    ppermute x3, starting transfers between devices, exchange(): lax.ppermute(far, 'space', list(enumerate(to_far)))  7.87 us
    ppermute x2, starting transfers between devices, handed_on(): out.append(lax.ppermute(value, ('tm', 'space'), perm))  3.71 us
    ppermute x3, starting transfers between devices, exchange(): lax.ppermute(near, 'space', list(enumerate(to_near)))  3.68 us
    ppermute x2, waiting for transfers between devices, handed_on(): out.append(lax.ppermute(value, ('tm', 'space'), perm))  3.67 us
    ppermute x3, waiting for transfers between devices, exchange(): lax.ppermute(far, 'space', list(enumerate(to_far)))  1.77 us
    ppermute x2, starting transfers between devices, swapped(): return lax.ppermute(value, 'tm', [(0, 1), (1, 0)])  1.3 us
  transfers between devices with their start and end apart: 10, of which 5 were waited for; matrix products, arithmetic and copies ran while one was open for 0% of the time, Pallas kernels for 13%

profile of v4, /device:TPU:1, one launch (start us, length us, event | category | flops | bytes accessed | tf_op | source)
XLA Modules:
  0.0 47.2 jit_solution(17599168800305602118)
XLA Ops:
  0.0 1.5 %edge_mix.1 = (f32[2,2,128,128]{3,2,1,0:T(8,128)S(1)}, f32[2,2,128,128]{3,2,1,0:T(8,128)S(1)}) custom-call(f32[1,3,4,256,256]{4,3,2,1,0:T(8,128)} %nodes.5), custom_call_target="tpu_custom_call" | custom-call | flops 1048576 | bytes 2097152 | tf_op jit(solution)/shard_map/edge_mix/pallas_call | solution.py:425
  1.5 2.1 %collective-permute-start = (f32[2,2,128,128]{3,2,1,0:T(8,128)S(1)}, f32[2,2,128,128]{3,2,1,0:T(8,128)S(1)}, u32[]{:S(2)}, u32[]{:S(2)}) collective-permute-start(f32[2,2,128,128]{3,2,1,0:T(8,128)S(1)} %get-tuple-element.28.own_near), channel_id=1, source_target_pairs={{0,1},{1,0},{2,3},{3,2},{4,5},{5,4},{6,7},{7,6},{8,9},{9,8},{10,11... | collective-permute-start | bytes 786440 | tf_op jit(solution)/shard_map/ppermute | solution.py:447
  3.7 3.3 %collective-permute-start.1 = (f32[2,2,128,128]{3,2,1,0:T(8,128)S(1)}, f32[2,2,128,128]{3,2,1,0:T(8,128)S(1)}, u32[]{:S(2)}, u32[]{:S(2)}) collective-permute-start(f32[2,2,128,128]{3,2,1,0:T(8,128)S(1)} %get-tuple-element.29.own_far), channel_id=1, source_target_pairs={{0,7},{1,2},{2,1},{3,4},{4,3},{5,6},{6,5},{7,0},{8,15},{9,10},{10,... | collective-permute-start | bytes 786440 | tf_op jit(solution)/shard_map/ppermute | solution.py:448
  6.9 4.6 %first_stage.1 = (f32[4,2,2,128,128]{4,3,2,1,0:T(8,128)S(1)}, f32[4,2,2,128,128]{4,3,2,1,0:T(8,128)S(1)}, f32[4,2,2,128,128]{4,3,2,1,0:T(8,128)S(1)}, f32[2,2,12...) custom-call(f32[1,3,4,256,256]{4,3,2,1,0:T(8,128)} %nodes.5, ...), custom_call_target="tpu_custom_call" | custom-call | flops 10485760 | bytes 6291456 | tf_op jit(solution)/shard_map/first_stage/pallas_call | solution.py:425
  11.5 0.1 collective-permute-start.2
  11.6 1.3 %collective-permute-start.3 = (f32[2,2,128,128]{3,2,1,0:T(8,128)S(1)}, f32[2,2,128,128]{3,2,1,0:T(8,128)S(1)}, u32[]{:S(2)}, u32[]{:S(2)}) collective-permute-start(f32[2,2,128,128]{3,2,1,0:T(8,128)S(1)} %get-tuple-element.32), channel_id=1, source_target_pairs={{0,7},{1,2},{2,1},{3,4},{4,3},{5,6},{6,5},{7,0},{8,15},{9,10},{10,... | collective-permute-start | bytes 786440 | tf_op jit(solution)/shard_map/ppermute | solution.py:448
  12.9 2.4 %collective-permute-done.near = f32[2,2,128,128]{3,2,1,0:T(8,128)S(1)} collective-permute-done((f32[2,2,128,128]{3,2,1,0:T(8,128)S(1)}, f32[2,2,128,128]{3,2,1,0:T(8,128)S(1)}, u32[]{:S(2)}, u32[]{:S(2)}) %collective-permute-start) | collective-permute-done | bytes 262176 | tf_op jit(solution)/shard_map/ppermute | solution.py:447
  15.3 1.6 %second_stage.1 = (f32[4,2,2,128,128]{4,3,2,1,0:T(8,128)S(1)}, f32[5,2,2,128,128]{4,3,2,1,0:T(8,128)S(1)}, f32[3,2,128,128]{3,2,1,0:T(8,128)S(1)}, f32[2,3,2,128,128]{4,3,2,1,0:T(8,128)S(1)}) custom-call(f32[4,2,2,128,128]{4,3,2,1,0:T(8,128)S(1)} %get-tuple-element.25.one_in, f32[4,2,2,128,128]{4,3,2,1,0:T(8,128)S(1)} %get-tuple-element.26.slope, ...), custom_call_target="tpu_custom_call" | custom-call | flops 10485760 | bytes 6291456 | tf_op jit(solution)/shard_map/second_stage/pallas_call | solution.py:425
  17.0 9.6 %collective-permute-done.2.near = f32[2,2,128,128]{3,2,1,0:T(8,128)S(1)} collective-permute-done((f32[2,2,128,128]{3,2,1,0:T(8,128)S(1)}, f32[2,2,128,128]{3,2,1,0:T(8,128)S(1)}, u32[]{:S(2)}, u32[]{:S(2)}) %collective-permute-start.2) | collective-permute-done | bytes 262176 | tf_op jit(solution)/shard_map/ppermute | solution.py:447
  26.6 0.0 collective-permute-done.3.far
  26.6 0.7 %third_stage.1 = (f32[5,2,2,128,128]{4,3,2,1,0:T(8,128)S(1)}, f32[2,128,128]{2,1,0:T(8,128)S(1)}, f32[2,128,128]{2,1,0:T(8,128)S(1)}, f32[5,2,128,128]{3,2,1,0:T(8,128)S(1)}) custom-call(f32[5,2,2,128,128]{4,3,2,1,0:T(8,128)S(1)} %get-tuple-element.30.two_in, f32[2,2,128,128]{3,2,1,0:T(8,128)S(1)} %collective-permute-done.2.near, ...), custom_call_target="tpu_custom_call", output_to_operand_aliasing={{0}: (0, {})} | custom-call | flops 5242880 | bytes 3145728 | tf_op jit(solution)/shard_map/third_stage/pallas_call | solution.py:425
  27.3 1.3 %collective-permute-start.9 = (f32[5,2,2,128,128]{4,3,2,1,0:T(8,128)S(1)}, f32[5,2,2,128,128]{4,3,2,1,0:T(8,128)S(1)}, u32[]{:S(2)}, u32[]{:S(2)}) collective-permute-start(f32[5,2,2,128,128]{4,3,2,1,0:T(8,128)S(1)} %get-tuple-element.43.two), channel_id=1, source_target_pairs={{0,8},{8,0},{1,9},{9,1},{2,10},{10,2},{3,11},{11,3},{4,12},{12,4},... | collective-permute-start | bytes 3932168 | tf_op jit(solution)/shard_map/ppermute | solution.py:453
  28.6 1.5 %collective-permute-start.4 = (f32[2,128,128]{2,1,0:T(8,128)S(1)}, f32[2,128,128]{2,1,0:T(8,128)S(1)}, u32[]{:S(2)}, u32[]{:S(2)}) collective-permute-start(f32[2,128,128]{2,1,0:T(8,128)S(1)} %get-tuple-element.37.own_near), channel_id=1, source_target_pairs={{0,1},{1,0},{2,3},{3,2},{4,5},{5,4},{6,7},{7,6},{8,9},{9,8},{10,11... | collective-permute-start | bytes 393224 | tf_op jit(solution)/shard_map/ppermute | solution.py:447
  30.1 3.3 %collective-permute-start.5 = (f32[2,128,128]{2,1,0:T(8,128)S(1)}, f32[2,128,128]{2,1,0:T(8,128)S(1)}, u32[]{:S(2)}, u32[]{:S(2)}) collective-permute-start(f32[2,128,128]{2,1,0:T(8,128)S(1)} %get-tuple-element.38.own_far), channel_id=1, source_target_pairs={{0,7},{1,2},{2,1},{3,4},{4,3},{5,6},{6,5},{7,0},{8,15},{9,10},{10,... | collective-permute-start | bytes 393224 | tf_op jit(solution)/shard_map/ppermute | solution.py:448
  33.3 2.4 %collective-permute-done.4.near = f32[2,128,128]{2,1,0:T(8,128)S(1)} collective-permute-done((f32[2,128,128]{2,1,0:T(8,128)S(1)}, f32[2,128,128]{2,1,0:T(8,128)S(1)}, u32[]{:S(2)}, u32[]{:S(2)}) %collective-permute-start.4) | collective-permute-done | bytes 131104 | tf_op jit(solution)/shard_map/ppermute | solution.py:447
  35.8 1.8 %collective-permute-done.5.far = f32[2,128,128]{2,1,0:T(8,128)S(1)} collective-permute-done((f32[2,128,128]{2,1,0:T(8,128)S(1)}, f32[2,128,128]{2,1,0:T(8,128)S(1)}, u32[]{:S(2)}, u32[]{:S(2)}) %collective-permute-start.5) | collective-permute-done | bytes 131104 | tf_op jit(solution)/shard_map/ppermute | solution.py:448
  37.6 1.6 %collective-permute-start.6 = (f32[2,128,128]{2,1,0:T(8,128)S(1)}, f32[2,128,128]{2,1,0:T(8,128)S(1)}, u32[]{:S(2)}, u32[]{:S(2)}) collective-permute-start(f32[2,128,128]{2,1,0:T(8,128)S(1)} %get-tuple-element.39), channel_id=1, source_target_pairs={{0,15},{1,10},{2,9},{3,12},{4,11},{5,14},{6,13},{7,8},{8,0},{9,1},... | collective-permute-start | bytes 393224 | tf_op jit(solution)/shard_map/ppermute | solution.py:461
  39.2 2.1 %collective-permute-start.7 = (f32[2,128,128]{2,1,0:T(8,128)S(1)}, f32[2,128,128]{2,1,0:T(8,128)S(1)}, u32[]{:S(2)}, u32[]{:S(2)}) collective-permute-start(f32[2,128,128]{2,1,0:T(8,128)S(1)} %get-tuple-element.40), channel_id=1, source_target_pairs={{0,9},{1,8},{2,11},{3,10},{4,13},{5,12},{6,15},{7,14},{8,0},{9,1},... | collective-permute-start | bytes 393224 | tf_op jit(solution)/shard_map/ppermute | solution.py:461
  41.3 0.0 collective-permute-start.8
  41.3 3.7 %collective-permute-done.6.ring_far = f32[2,128,128]{2,1,0:T(8,128)S(1)} collective-permute-done((f32[2,128,128]{2,1,0:T(8,128)S(1)}, f32[2,128,128]{2,1,0:T(8,128)S(1)}, u32[]{:S(2)}, u32[]{:S(2)}) %collective-permute-start.6) | collective-permute-done | bytes 131104 | tf_op jit(solution)/shard_map/ppermute | solution.py:461
  45.0 0.0 collective-permute-done.7.ring_near
  45.0 0.0 collective-permute-done.8.end
  45.0 0.0 collective-permute-done.9.moved
  45.0 2.2 %update.1 = f32[1,3,4,256,256]{4,3,2,1,0:T(8,128)} custom-call(f32[1,3,4,256,256]{4,3,2,1,0:T(8,128)S(1)} %copy-done, f32[2,128,128]{2,1,0:T(8,128)S(1)} %collective-permute-done.6.ring_far, f32[2,128,128]{2,1,0:T(8,128)S(1)} %collective-permute-done.7.ring_near, f32[2,128,128]{2,1,0:T(8,128)S(1)} %collective-permute-done.8.end, ...), custom_call_target="tpu_custom_call" | custom-call | flops 5242880 | bytes 6291456 | tf_op jit(solution)/shard_map/update/pallas_call | solution.py:425
  (8 shorter events, 0.1 us)
Async XLA Ops:
  0.0 6.9 %copy-start.1 = (bf16[256,256]{1,0:T(8,128)(2,1)S(1)}, bf16[256,256]{1,0:T(8,128)(2,1)}, u32[]{:S(2)}) copy-start(bf16[256,256]{1,0:T(8,128)(2,1)} %constant.4.clone.pairs) | copy-start | bytes 393220
  1.5 13.8 %collective-permute-start = (f32[2,2,128,128]{3,2,1,0:T(8,128)S(1)}, f32[2,2,128,128]{3,2,1,0:T(8,128)S(1)}, u32[]{:S(2)}, u32[]{:S(2)}) collective-permute-start(f32[2,2,128,128]{3,2,1,0:T(8,128)S(1)} %get-tuple-element.28.own_near), channel_id=1, source_target_pairs={{0,1},{1,0},{2,3},{3,2},{4,5},{5,4},{6,7},{7,6},{8,9},{9,8},{10,11... | collective-permute-start | bytes 786440 | tf_op jit(solution)/shard_map/ppermute | solution.py:447
  3.7 11.7 %collective-permute-start.1 = (f32[2,2,128,128]{3,2,1,0:T(8,128)S(1)}, f32[2,2,128,128]{3,2,1,0:T(8,128)S(1)}, u32[]{:S(2)}, u32[]{:S(2)}) collective-permute-start(f32[2,2,128,128]{3,2,1,0:T(8,128)S(1)} %get-tuple-element.29.own_far), channel_id=1, source_target_pairs={{0,7},{1,2},{2,1},{3,4},{4,3},{5,6},{6,5},{7,0},{8,15},{9,10},{10,... | collective-permute-start | bytes 786440 | tf_op jit(solution)/shard_map/ppermute | solution.py:448
  11.5 15.0 %collective-permute-start.2 = (f32[2,2,128,128]{3,2,1,0:T(8,128)S(1)}, f32[2,2,128,128]{3,2,1,0:T(8,128)S(1)}, u32[]{:S(2)}, u32[]{:S(2)}) collective-permute-start(f32[2,2,128,128]{3,2,1,0:T(8,128)S(1)} %get-tuple-element.31), channel_id=1, source_target_pairs={{0,1},{1,0},{2,3},{3,2},{4,5},{5,4},{6,7},{7,6},{8,9},{9,8},{10,11... | collective-permute-start | bytes 786440 | tf_op jit(solution)/shard_map/ppermute | solution.py:447
  11.6 15.0 %collective-permute-start.3 = (f32[2,2,128,128]{3,2,1,0:T(8,128)S(1)}, f32[2,2,128,128]{3,2,1,0:T(8,128)S(1)}, u32[]{:S(2)}, u32[]{:S(2)}) collective-permute-start(f32[2,2,128,128]{3,2,1,0:T(8,128)S(1)} %get-tuple-element.32), channel_id=1, source_target_pairs={{0,7},{1,2},{2,1},{3,4},{4,3},{5,6},{6,5},{7,0},{8,15},{9,10},{10,... | collective-permute-start | bytes 786440 | tf_op jit(solution)/shard_map/ppermute | solution.py:448
  26.6 18.4 %copy-start = (f32[1,3,4,256,256]{4,3,2,1,0:T(8,128)S(1)}, f32[1,3,4,256,256]{4,3,2,1,0:T(8,128)}, u32[]{:S(2)}) copy-start(f32[1,3,4,256,256]{4,3,2,1,0:T(8,128)} %nodes.5) | copy-start | bytes 9437188
  26.6 18.4 %copy-start.2 = (bf16[128,256]{1,0:T(8,128)(2,1)S(1)}, bf16[128,256]{1,0:T(8,128)(2,1)}, u32[]{:S(2)}) copy-start(bf16[128,256]{1,0:T(8,128)(2,1)} %constant.5.clone.spread) | copy-start | bytes 196612
  27.3 17.6 %collective-permute-start.9 = (f32[5,2,2,128,128]{4,3,2,1,0:T(8,128)S(1)}, f32[5,2,2,128,128]{4,3,2,1,0:T(8,128)S(1)}, u32[]{:S(2)}, u32[]{:S(2)}) collective-permute-start(f32[5,2,2,128,128]{4,3,2,1,0:T(8,128)S(1)} %get-tuple-element.43.two), channel_id=1, source_target_pairs={{0,8},{8,0},{1,9},{9,1},{2,10},{10,2},{3,11},{11,3},{4,12},{12,4},... | collective-permute-start | bytes 3932168 | tf_op jit(solution)/shard_map/ppermute | solution.py:453
  28.6 7.1 %collective-permute-start.4 = (f32[2,128,128]{2,1,0:T(8,128)S(1)}, f32[2,128,128]{2,1,0:T(8,128)S(1)}, u32[]{:S(2)}, u32[]{:S(2)}) collective-permute-start(f32[2,128,128]{2,1,0:T(8,128)S(1)} %get-tuple-element.37.own_near), channel_id=1, source_target_pairs={{0,1},{1,0},{2,3},{3,2},{4,5},{5,4},{6,7},{7,6},{8,9},{9,8},{10,11... | collective-permute-start | bytes 393224 | tf_op jit(solution)/shard_map/ppermute | solution.py:447
  30.1 7.4 %collective-permute-start.5 = (f32[2,128,128]{2,1,0:T(8,128)S(1)}, f32[2,128,128]{2,1,0:T(8,128)S(1)}, u32[]{:S(2)}, u32[]{:S(2)}) collective-permute-start(f32[2,128,128]{2,1,0:T(8,128)S(1)} %get-tuple-element.38.own_far), channel_id=1, source_target_pairs={{0,7},{1,2},{2,1},{3,4},{4,3},{5,6},{6,5},{7,0},{8,15},{9,10},{10,... | collective-permute-start | bytes 393224 | tf_op jit(solution)/shard_map/ppermute | solution.py:448
  37.6 7.4 %collective-permute-start.6 = (f32[2,128,128]{2,1,0:T(8,128)S(1)}, f32[2,128,128]{2,1,0:T(8,128)S(1)}, u32[]{:S(2)}, u32[]{:S(2)}) collective-permute-start(f32[2,128,128]{2,1,0:T(8,128)S(1)} %get-tuple-element.39), channel_id=1, source_target_pairs={{0,15},{1,10},{2,9},{3,12},{4,11},{5,14},{6,13},{7,8},{8,0},{9,1},... | collective-permute-start | bytes 393224 | tf_op jit(solution)/shard_map/ppermute | solution.py:461
  39.2 5.8 %collective-permute-start.7 = (f32[2,128,128]{2,1,0:T(8,128)S(1)}, f32[2,128,128]{2,1,0:T(8,128)S(1)}, u32[]{:S(2)}, u32[]{:S(2)}) collective-permute-start(f32[2,128,128]{2,1,0:T(8,128)S(1)} %get-tuple-element.40), channel_id=1, source_target_pairs={{0,9},{1,8},{2,11},{3,10},{4,13},{5,12},{6,15},{7,14},{8,0},{9,1},... | collective-permute-start | bytes 393224 | tf_op jit(solution)/shard_map/ppermute | solution.py:461
  41.3 3.7 %collective-permute-start.8 = (f32[2,128,128]{2,1,0:T(8,128)S(1)}, f32[2,128,128]{2,1,0:T(8,128)S(1)}, u32[]{:S(2)}, u32[]{:S(2)}) collective-permute-start(f32[2,128,128]{2,1,0:T(8,128)S(1)} %get-tuple-element.41), channel_id=1, source_target_pairs={{0,8},{8,0},{1,9},{9,1},{2,10},{10,2},{3,11},{11,3},{4,12},{12,4},... | collective-permute-start | bytes 393224 | tf_op jit(solution)/shard_map/ppermute | solution.py:453

commit v5 on v4

--- a/solution.py
+++ b/solution.py
@@ -195,7 +195,7 @@
 
 
 def second_kernel(
-    one_in, slope, rest, near, far, own_near, own_far, pairs, one, two, coarse, inner, mix
+    one_in, slope, rest, near, far, own_near, own_far, pairs, coarse_zero, one, two, coarse, inner, coarse_forces, mix
 ):
     planes, halves = one_in.shape[0], one_in.shape[1]
     outer = outer_planes(planes)
@@ -219,11 +219,15 @@
             inner[k, 0, h] = even
             inner[k, 1, h] = odd
             inner[k, 2, h] = GROWTH * (even + odd - cube(even) - cube(odd))
-    store_coarse(coarse, *restrict_field(one, pairs, planes, halves))
+    means, forces, edges = restrict_field(one, pairs, planes, halves)
+    store_coarse(coarse, means, forces, edges)
+    for k, field in enumerate(([coarse_zero[0, p] for p in range(planes // 2)], means)):
+        for p, v in enumerate(coarse_force(field)):
+            coarse_forces[k, p] = v
 
 
 def third_kernel(
-    two_in, near, far, inner, coarse_zero, coarse_one, pairs, two, send_near, send_far, work, outer
+    two_in, near, far, inner, coarse_zero, coarse_one, coarse_forces, pairs, two, send_near, send_far, work, outer
 ):
     planes, halves = two_in.shape[0] - 1, two_in.shape[1]
     later = lax.axis_index("tm").astype(F32)
@@ -263,8 +267,8 @@
     half = planes // 2
     zero = [coarse_zero[0, p] for p in range(half)]
     mean_one = [coarse_one[0, p] for p in range(half)]
-    force_zero = coarse_force(zero)
-    force_one = coarse_force(mean_one)
+    force_zero = [coarse_forces[0, p] for p in range(half)]
+    force_one = [coarse_forces[1, p] for p in range(half)]
     sweep_zero, sweep_one = [], []
     for p in range(half):
         parts = (coarse_zero[1, p], coarse_one[1, p], forces_two[p])
@@ -309,15 +313,14 @@
     return one, two
 
 
-def coarse_steps(first, sweep_one, sweep_two):
+def coarse_steps(first, force, sweep_one, sweep_two):
     half = len(first)
-    force = coarse_force(first)
     one = [first[p] + 0.5 * force[p] + sweep_one[p] for p in range(half)]
     force = coarse_force(one)
     return [one[p] + 0.5 * force[p] + sweep_two[p] for p in range(half)]
 
 
-def fourth_kernel(work, near, far, own_near, own_far, end, send_near, send_far, swept):
+def fourth_kernel(work, near, far, own_near, own_far, coarse_forces, end, send_near, send_far, swept):
     half = work.shape[1]
     low, high = sides(near, far)
     own_low, own_high = sides(own_near, own_far)
@@ -328,7 +331,8 @@
     @pl.when(lax.axis_index("tm") == 0)
     def _():
         first = [work[0, p] for p in range(half)]
-        two = coarse_steps(first, *[[swept[k, p] for p in range(half)] for k in range(2)])
+        start = [coarse_forces[0, p] for p in range(half)]
+        two = coarse_steps(first, start, *[[swept[k, p] for p in range(half)] for k in range(2)])
         force = coarse_force(two)
         for p in range(half):
             end[p] = two[p]
@@ -490,23 +494,23 @@
         size=size * 6, flops=size * 10,
     )
     got_b_near, got_b_far = exchange(b_near, b_far)
-    one, two_part, coarse_mid, inner = call(
+    one, two_part, coarse_mid, inner, coarse_forces = call(
         second_kernel, "second_stage",
-        (one_part, slope, rest, got_a_near, got_a_far, a_near, a_far, pairs), (),
-        [field, (planes + 1,) + plane, packed, (2, 3, halves, rows, LANES)],
+        (one_part, slope, rest, got_a_near, got_a_far, a_near, a_far, pairs, coarse_zero), (),
+        [field, (planes + 1,) + plane, packed, (2, 3, halves, rows, LANES), (2, half) + quarter],
         [pltpu.VMEM(field, F32)],
         size=size * 6, flops=size * 10,
     )
     two, h_near, h_far, work = call(
         third_kernel, "third_stage",
-        (two_part, got_b_near, got_b_far, inner, coarse_zero, coarse_mid, pairs), (),
+        (two_part, got_b_near, got_b_far, inner, coarse_zero, coarse_mid, coarse_forces, pairs), (),
         [(planes + 1,) + plane, pair, pair, (5, half) + quarter], [pltpu.VMEM((2,) + plane, F32)],
         aliases={0: 0}, size=size * 3, flops=size * 5,
     )
     moved = swapped(two)
     got_near, got_far = exchange(h_near, h_far)
     end, f_near, f_far, swept = call(
-        fourth_kernel, "coarse_chain", (work, got_near, got_far, h_near, h_far), (),
+        fourth_kernel, "coarse_chain", (work, got_near, got_far, h_near, h_far, coarse_forces), (),
         [(half,) + quarter, pair, pair, (2, half) + quarter], size=size, flops=size,
     )
     ring_far, ring_near = handed_on(f_near, f_far)

time: 47.4 us -> 47.2 us (level)
  transfers between devices with their start and end apart: 10 -> 10, of which waited for: 5 -> 5; matrix products, arithmetic and copies ran while one was open for 0% -> 0% of each run, Pallas kernels for 13% -> 14%
where the time goes in v5:
time: 47.2 us; the launch traced here: 47 us
  waiting for transfers between devices  19.6 us (42%)
  starting transfers between devices  16.6 us (35%)
  Pallas kernels  10.8 us (23%)
    ppermute x3, waiting for transfers between devices, exchange(): lax.ppermute(near, 'space', list(enumerate(to_near)))  14.2 us
    pallas_call x6, Pallas kernels, call(): pl.pallas_call(kernel, name=name, out_shape=[jax.ShapeDtypeStruct(s, F32)...  10.8 us
    ppermute x3, starting transfers between devices, exchange(): lax.ppermute(far, 'space', list(enumerate(to_far)))  7.87 us
    ppermute x2, starting transfers between devices, handed_on(): out.append(lax.ppermute(value, ('tm', 'space'), perm))  3.71 us
    ppermute x3, starting transfers between devices, exchange(): lax.ppermute(near, 'space', list(enumerate(to_near)))  3.68 us
    ppermute x2, waiting for transfers between devices, handed_on(): out.append(lax.ppermute(value, ('tm', 'space'), perm))  3.57 us
    ppermute x3, waiting for transfers between devices, exchange(): lax.ppermute(far, 'space', list(enumerate(to_far)))  1.77 us
    ppermute x2, starting transfers between devices, swapped(): return lax.ppermute(value, 'tm', [(0, 1), (1, 0)])  1.3 us
  transfers between devices with their start and end apart: 10, of which 5 were waited for; matrix products, arithmetic and copies ran while one was open for 0% of the time, Pallas kernels for 14%

profile of v5, /device:TPU:1, one launch (start us, length us, event | category | flops | bytes accessed | tf_op | source)
XLA Modules:
  0.0 47.0 jit_solution(2973848034576754234)
XLA Ops:
  0.0 1.5 %edge_mix.1 = (f32[2,2,128,128]{3,2,1,0:T(8,128)S(1)}, f32[2,2,128,128]{3,2,1,0:T(8,128)S(1)}) custom-call(f32[1,3,4,256,256]{4,3,2,1,0:T(8,128)} %nodes.5), custom_call_target="tpu_custom_call" | custom-call | flops 1048576 | bytes 2097152 | tf_op jit(solution)/shard_map/edge_mix/pallas_call | solution.py:429
  1.5 2.1 %collective-permute-start = (f32[2,2,128,128]{3,2,1,0:T(8,128)S(1)}, f32[2,2,128,128]{3,2,1,0:T(8,128)S(1)}, u32[]{:S(2)}, u32[]{:S(2)}) collective-permute-start(f32[2,2,128,128]{3,2,1,0:T(8,128)S(1)} %get-tuple-element.29.own_near), channel_id=1, source_target_pairs={{0,1},{1,0},{2,3},{3,2},{4,5},{5,4},{6,7},{7,6},{8,9},{9,8},{10,11... | collective-permute-start | bytes 786440 | tf_op jit(solution)/shard_map/ppermute | solution.py:451
  3.7 3.3 %collective-permute-start.1 = (f32[2,2,128,128]{3,2,1,0:T(8,128)S(1)}, f32[2,2,128,128]{3,2,1,0:T(8,128)S(1)}, u32[]{:S(2)}, u32[]{:S(2)}) collective-permute-start(f32[2,2,128,128]{3,2,1,0:T(8,128)S(1)} %get-tuple-element.30.own_far), channel_id=1, source_target_pairs={{0,7},{1,2},{2,1},{3,4},{4,3},{5,6},{6,5},{7,0},{8,15},{9,10},{10,... | collective-permute-start | bytes 786440 | tf_op jit(solution)/shard_map/ppermute | solution.py:452
  6.9 4.6 %first_stage.1 = (f32[4,2,2,128,128]{4,3,2,1,0:T(8,128)S(1)}, f32[4,2,2,128,128]{4,3,2,1,0:T(8,128)S(1)}, f32[4,2,2,128,128]{4,3,2,1,0:T(8,128)S(1)}, f32[2,2,12...) custom-call(f32[1,3,4,256,256]{4,3,2,1,0:T(8,128)} %nodes.5, ...), custom_call_target="tpu_custom_call" | custom-call | flops 10485760 | bytes 6291456 | tf_op jit(solution)/shard_map/first_stage/pallas_call | solution.py:429
  11.5 0.1 collective-permute-start.2
  11.6 1.3 %collective-permute-start.3 = (f32[2,2,128,128]{3,2,1,0:T(8,128)S(1)}, f32[2,2,128,128]{3,2,1,0:T(8,128)S(1)}, u32[]{:S(2)}, u32[]{:S(2)}) collective-permute-start(f32[2,2,128,128]{3,2,1,0:T(8,128)S(1)} %get-tuple-element.34), channel_id=1, source_target_pairs={{0,7},{1,2},{2,1},{3,4},{4,3},{5,6},{6,5},{7,0},{8,15},{9,10},{10,... | collective-permute-start | bytes 786440 | tf_op jit(solution)/shard_map/ppermute | solution.py:452
  12.9 2.4 %collective-permute-done.near = f32[2,2,128,128]{3,2,1,0:T(8,128)S(1)} collective-permute-done((f32[2,2,128,128]{3,2,1,0:T(8,128)S(1)}, f32[2,2,128,128]{3,2,1,0:T(8,128)S(1)}, u32[]{:S(2)}, u32[]{:S(2)}) %collective-permute-start) | collective-permute-done | bytes 262176 | tf_op jit(solution)/shard_map/ppermute | solution.py:451
  15.3 1.8 %second_stage.1 = (f32[4,2,2,128,128]{4,3,2,1,0:T(8,128)S(1)}, f32[5,2,2,128,128]{4,3,2,1,0:T(8,128)S(1)}, f32[3,2,128,128]{3,2,1,0:T(8,128)S(1)}, f32[2,3,2,128...) custom-call(f32[4,2,2,128,128]{4,3,2,1,0:T(8,128)S(1)} %get-tuple-element.26.one_in, ...), custom_call_target="tpu_custom_call" | custom-call | flops 10485760 | bytes 6291456 | tf_op jit(solution)/shard_map/second_stage/pallas_call | solution.py:429
  17.1 9.4 %collective-permute-done.2.near = f32[2,2,128,128]{3,2,1,0:T(8,128)S(1)} collective-permute-done((f32[2,2,128,128]{3,2,1,0:T(8,128)S(1)}, f32[2,2,128,128]{3,2,1,0:T(8,128)S(1)}, u32[]{:S(2)}, u32[]{:S(2)}) %collective-permute-start.2) | collective-permute-done | bytes 262176 | tf_op jit(solution)/shard_map/ppermute | solution.py:451
  26.6 0.0 collective-permute-done.3.far
  26.6 0.7 %third_stage.1 = (f32[5,2,2,128,128]{4,3,2,1,0:T(8,128)S(1)}, f32[2,128,128]{2,1,0:T(8,128)S(1)}, f32[2,128,128]{2,1,0:T(8,128)S(1)}, f32[5,2,128,128]{3,2,1,0:T(8,128)S(1)}) custom-call(f32[5,2,2,128,128]{4,3,2,1,0:T(8,128)S(1)} %get-tuple-element.32.two_in, f32[2,2,128,128]{3,2,1,0:T(8,128)S(1)} %collective-permute-done.2.near, ...), custom_call_target="tpu_custom_call", output_to_operand_aliasing={{0}: (0, {})} | custom-call | flops 5242880 | bytes 3145728 | tf_op jit(solution)/shard_map/third_stage/pallas_call | solution.py:429
  27.2 0.0 copy-start.2
  27.3 1.3 %collective-permute-start.9 = (f32[5,2,2,128,128]{4,3,2,1,0:T(8,128)S(1)}, f32[5,2,2,128,128]{4,3,2,1,0:T(8,128)S(1)}, u32[]{:S(2)}, u32[]{:S(2)}) collective-permute-start(f32[5,2,2,128,128]{4,3,2,1,0:T(8,128)S(1)} %get-tuple-element.45.two), channel_id=1, source_target_pairs={{0,8},{8,0},{1,9},{9,1},{2,10},{10,2},{3,11},{11,3},{4,12},{12,4},... | collective-permute-start | bytes 3932168 | tf_op jit(solution)/shard_map/ppermute | solution.py:457
  28.5 1.5 %collective-permute-start.4 = (f32[2,128,128]{2,1,0:T(8,128)S(1)}, f32[2,128,128]{2,1,0:T(8,128)S(1)}, u32[]{:S(2)}, u32[]{:S(2)}) collective-permute-start(f32[2,128,128]{2,1,0:T(8,128)S(1)} %get-tuple-element.39.own_near), channel_id=1, source_target_pairs={{0,1},{1,0},{2,3},{3,2},{4,5},{5,4},{6,7},{7,6},{8,9},{9,8},{10,11... | collective-permute-start | bytes 393224 | tf_op jit(solution)/shard_map/ppermute | solution.py:451
  30.0 3.3 %collective-permute-start.5 = (f32[2,128,128]{2,1,0:T(8,128)S(1)}, f32[2,128,128]{2,1,0:T(8,128)S(1)}, u32[]{:S(2)}, u32[]{:S(2)}) collective-permute-start(f32[2,128,128]{2,1,0:T(8,128)S(1)} %get-tuple-element.40.own_far), channel_id=1, source_target_pairs={{0,7},{1,2},{2,1},{3,4},{4,3},{5,6},{6,5},{7,0},{8,15},{9,10},{10,... | collective-permute-start | bytes 393224 | tf_op jit(solution)/shard_map/ppermute | solution.py:452
  33.3 2.4 %collective-permute-done.4.near = f32[2,128,128]{2,1,0:T(8,128)S(1)} collective-permute-done((f32[2,128,128]{2,1,0:T(8,128)S(1)}, f32[2,128,128]{2,1,0:T(8,128)S(1)}, u32[]{:S(2)}, u32[]{:S(2)}) %collective-permute-start.4) | collective-permute-done | bytes 131104 | tf_op jit(solution)/shard_map/ppermute | solution.py:451
  35.7 1.8 %collective-permute-done.5.far = f32[2,128,128]{2,1,0:T(8,128)S(1)} collective-permute-done((f32[2,128,128]{2,1,0:T(8,128)S(1)}, f32[2,128,128]{2,1,0:T(8,128)S(1)}, u32[]{:S(2)}, u32[]{:S(2)}) %collective-permute-start.5) | collective-permute-done | bytes 131104 | tf_op jit(solution)/shard_map/ppermute | solution.py:452
  37.5 1.5 %collective-permute-start.6 = (f32[2,128,128]{2,1,0:T(8,128)S(1)}, f32[2,128,128]{2,1,0:T(8,128)S(1)}, u32[]{:S(2)}, u32[]{:S(2)}) collective-permute-start(f32[2,128,128]{2,1,0:T(8,128)S(1)} %get-tuple-element.41), channel_id=1, source_target_pairs={{0,15},{1,10},{2,9},{3,12},{4,11},{5,14},{6,13},{7,8},{8,0},{9,1},... | collective-permute-start | bytes 393224 | tf_op jit(solution)/shard_map/ppermute | solution.py:465
  39.0 2.2 %collective-permute-start.7 = (f32[2,128,128]{2,1,0:T(8,128)S(1)}, f32[2,128,128]{2,1,0:T(8,128)S(1)}, u32[]{:S(2)}, u32[]{:S(2)}) collective-permute-start(f32[2,128,128]{2,1,0:T(8,128)S(1)} %get-tuple-element.42), channel_id=1, source_target_pairs={{0,9},{1,8},{2,11},{3,10},{4,13},{5,12},{6,15},{7,14},{8,0},{9,1},... | collective-permute-start | bytes 393224 | tf_op jit(solution)/shard_map/ppermute | solution.py:465
  41.2 0.0 collective-permute-start.8
  41.2 3.6 %collective-permute-done.6.ring_far = f32[2,128,128]{2,1,0:T(8,128)S(1)} collective-permute-done((f32[2,128,128]{2,1,0:T(8,128)S(1)}, f32[2,128,128]{2,1,0:T(8,128)S(1)}, u32[]{:S(2)}, u32[]{:S(2)}) %collective-permute-start.6) | collective-permute-done | bytes 131104 | tf_op jit(solution)/shard_map/ppermute | solution.py:465
  44.8 0.0 collective-permute-done.7.ring_near
  44.8 0.0 collective-permute-done.8.end
  44.8 2.2 %update.1 = f32[1,3,4,256,256]{4,3,2,1,0:T(8,128)} custom-call(f32[1,3,4,256,256]{4,3,2,1,0:T(8,128)S(1)} %copy-done, f32[2,128,128]{2,1,0:T(8,128)S(1)} %collective-permute-done.6.ring_far, f32[2,128,128]{2,1,0:T(8,128)S(1)} %collective-permute-done.7.ring_near, f32[2,128,128]{2,1,0:T(8,128)S(1)} %collective-permute-done.8.end, ...), custom_call_target="tpu_custom_call" | custom-call | flops 5242880 | bytes 6291456 | tf_op jit(solution)/shard_map/update/pallas_call | solution.py:429
  (8 shorter events, 0.1 us)
Async XLA Ops:
  0.0 6.9 %copy-start.1 = (bf16[256,256]{1,0:T(8,128)(2,1)S(1)}, bf16[256,256]{1,0:T(8,128)(2,1)}, u32[]{:S(2)}) copy-start(bf16[256,256]{1,0:T(8,128)(2,1)} %constant.4.clone.pairs) | copy-start | bytes 393220
  1.5 13.8 %collective-permute-start = (f32[2,2,128,128]{3,2,1,0:T(8,128)S(1)}, f32[2,2,128,128]{3,2,1,0:T(8,128)S(1)}, u32[]{:S(2)}, u32[]{:S(2)}) collective-permute-start(f32[2,2,128,128]{3,2,1,0:T(8,128)S(1)} %get-tuple-element.29.own_near), channel_id=1, source_target_pairs={{0,1},{1,0},{2,3},{3,2},{4,5},{5,4},{6,7},{7,6},{8,9},{9,8},{10,11... | collective-permute-start | bytes 786440 | tf_op jit(solution)/shard_map/ppermute | solution.py:451
  3.7 11.7 %collective-permute-start.1 = (f32[2,2,128,128]{3,2,1,0:T(8,128)S(1)}, f32[2,2,128,128]{3,2,1,0:T(8,128)S(1)}, u32[]{:S(2)}, u32[]{:S(2)}) collective-permute-start(f32[2,2,128,128]{3,2,1,0:T(8,128)S(1)} %get-tuple-element.30.own_far), channel_id=1, source_target_pairs={{0,7},{1,2},{2,1},{3,4},{4,3},{5,6},{6,5},{7,0},{8,15},{9,10},{10,... | collective-permute-start | bytes 786440 | tf_op jit(solution)/shard_map/ppermute | solution.py:452
  11.5 15.0 %collective-permute-start.2 = (f32[2,2,128,128]{3,2,1,0:T(8,128)S(1)}, f32[2,2,128,128]{3,2,1,0:T(8,128)S(1)}, u32[]{:S(2)}, u32[]{:S(2)}) collective-permute-start(f32[2,2,128,128]{3,2,1,0:T(8,128)S(1)} %get-tuple-element.33), channel_id=1, source_target_pairs={{0,1},{1,0},{2,3},{3,2},{4,5},{5,4},{6,7},{7,6},{8,9},{9,8},{10,11... | collective-permute-start | bytes 786440 | tf_op jit(solution)/shard_map/ppermute | solution.py:451
  11.6 15.0 %collective-permute-start.3 = (f32[2,2,128,128]{3,2,1,0:T(8,128)S(1)}, f32[2,2,128,128]{3,2,1,0:T(8,128)S(1)}, u32[]{:S(2)}, u32[]{:S(2)}) collective-permute-start(f32[2,2,128,128]{3,2,1,0:T(8,128)S(1)} %get-tuple-element.34), channel_id=1, source_target_pairs={{0,7},{1,2},{2,1},{3,4},{4,3},{5,6},{6,5},{7,0},{8,15},{9,10},{10,... | collective-permute-start | bytes 786440 | tf_op jit(solution)/shard_map/ppermute | solution.py:452
  26.6 18.2 %copy-start = (f32[1,3,4,256,256]{4,3,2,1,0:T(8,128)S(1)}, f32[1,3,4,256,256]{4,3,2,1,0:T(8,128)}, u32[]{:S(2)}) copy-start(f32[1,3,4,256,256]{4,3,2,1,0:T(8,128)} %nodes.5) | copy-start | bytes 9437188
  27.2 17.6 %copy-start.2 = (bf16[128,256]{1,0:T(8,128)(2,1)S(1)}, bf16[128,256]{1,0:T(8,128)(2,1)}, u32[]{:S(2)}) copy-start(bf16[128,256]{1,0:T(8,128)(2,1)} %constant.5.clone.spread) | copy-start | bytes 196612
  27.3 17.6 %collective-permute-start.9 = (f32[5,2,2,128,128]{4,3,2,1,0:T(8,128)S(1)}, f32[5,2,2,128,128]{4,3,2,1,0:T(8,128)S(1)}, u32[]{:S(2)}, u32[]{:S(2)}) collective-permute-start(f32[5,2,2,128,128]{4,3,2,1,0:T(8,128)S(1)} %get-tuple-element.45.two), channel_id=1, source_target_pairs={{0,8},{8,0},{1,9},{9,1},{2,10},{10,2},{3,11},{11,3},{4,12},{12,4},... | collective-permute-start | bytes 3932168 | tf_op jit(solution)/shard_map/ppermute | solution.py:457
  28.5 7.1 %collective-permute-start.4 = (f32[2,128,128]{2,1,0:T(8,128)S(1)}, f32[2,128,128]{2,1,0:T(8,128)S(1)}, u32[]{:S(2)}, u32[]{:S(2)}) collective-permute-start(f32[2,128,128]{2,1,0:T(8,128)S(1)} %get-tuple-element.39.own_near), channel_id=1, source_target_pairs={{0,1},{1,0},{2,3},{3,2},{4,5},{5,4},{6,7},{7,6},{8,9},{9,8},{10,11... | collective-permute-start | bytes 393224 | tf_op jit(solution)/shard_map/ppermute | solution.py:451
  30.0 7.4 %collective-permute-start.5 = (f32[2,128,128]{2,1,0:T(8,128)S(1)}, f32[2,128,128]{2,1,0:T(8,128)S(1)}, u32[]{:S(2)}, u32[]{:S(2)}) collective-permute-start(f32[2,128,128]{2,1,0:T(8,128)S(1)} %get-tuple-element.40.own_far), channel_id=1, source_target_pairs={{0,7},{1,2},{2,1},{3,4},{4,3},{5,6},{6,5},{7,0},{8,15},{9,10},{10,... | collective-permute-start | bytes 393224 | tf_op jit(solution)/shard_map/ppermute | solution.py:452
  37.5 7.3 %collective-permute-start.6 = (f32[2,128,128]{2,1,0:T(8,128)S(1)}, f32[2,128,128]{2,1,0:T(8,128)S(1)}, u32[]{:S(2)}, u32[]{:S(2)}) collective-permute-start(f32[2,128,128]{2,1,0:T(8,128)S(1)} %get-tuple-element.41), channel_id=1, source_target_pairs={{0,15},{1,10},{2,9},{3,12},{4,11},{5,14},{6,13},{7,8},{8,0},{9,1},... | collective-permute-start | bytes 393224 | tf_op jit(solution)/shard_map/ppermute | solution.py:465
  39.0 5.8 %collective-permute-start.7 = (f32[2,128,128]{2,1,0:T(8,128)S(1)}, f32[2,128,128]{2,1,0:T(8,128)S(1)}, u32[]{:S(2)}, u32[]{:S(2)}) collective-permute-start(f32[2,128,128]{2,1,0:T(8,128)S(1)} %get-tuple-element.42), channel_id=1, source_target_pairs={{0,9},{1,8},{2,11},{3,10},{4,13},{5,12},{6,15},{7,14},{8,0},{9,1},... | collective-permute-start | bytes 393224 | tf_op jit(solution)/shard_map/ppermute | solution.py:465
  41.2 3.6 %collective-permute-start.8 = (f32[2,128,128]{2,1,0:T(8,128)S(1)}, f32[2,128,128]{2,1,0:T(8,128)S(1)}, u32[]{:S(2)}, u32[]{:S(2)}) collective-permute-start(f32[2,128,128]{2,1,0:T(8,128)S(1)} %get-tuple-element.43), channel_id=1, source_target_pairs={{0,8},{8,0},{1,9},{9,1},{2,10},{10,2},{3,11},{11,3},{4,12},{12,4},... | collective-permute-start | bytes 393224 | tf_op jit(solution)/shard_map/ppermute | solution.py:457

commit v6 on v5

--- a/solution.py
+++ b/solution.py
@@ -92,7 +92,9 @@
 
 
 def spread_matrix(size):
-    return jnp.asarray(np.repeat(np.eye(size, dtype=np.float32), 2, axis=1), BF16)
+    row = lax.broadcasted_iota(jnp.int32, (size, 2 * size), 0)
+    col = lax.broadcasted_iota(jnp.int32, (size, 2 * size), 1)
+    return jnp.where((col == 2 * row) | (col == 2 * row + 1), 1.0, 0.0).astype(F32).astype(BF16)
 
 
 def times(v, matrix):
@@ -168,7 +170,7 @@
                 out[h, q] = work[e, h, pl.ds(q, rows, stride=2), :]
 
 
-def first_kernel(nodes, pairs, one, slope, rest, near, far, coarse, work, start, mix):
+def first_kernel(nodes, pairs, one, slope, rest, near, far, coarse, start, work, mix):
     planes, halves = one.shape[0], one.shape[1]
     rows = one.shape[3]
     for p in range(planes):
@@ -320,7 +322,10 @@
     return [one[p] + 0.5 * force[p] + sweep_two[p] for p in range(half)]
 
 
-def fourth_kernel(work, near, far, own_near, own_far, coarse_forces, end, send_near, send_far, swept):
+def fourth_kernel(
+    work, near, far, own_near, own_far, coarse_forces, held, end, send_near, send_far, swept, passed
+):
+    del held, passed
     half = work.shape[1]
     low, high = sides(near, far)
     own_low, own_high = sides(own_near, own_far)
@@ -343,11 +348,11 @@
 
 
 class Planes:
-    def __init__(self, spread, updated, parts, result, sem):
+    def __init__(self, updated, parts, result, sem):
         self.updated, self.parts, self.result, self.sem = updated, parts, result, sem
         self.rows = parts.shape[2] // 2
         self.halves = parts.shape[1]
-        self.spread = spread[...]
+        self.spread = spread_matrix(LANES * self.halves // 2)
         self.copies = []
 
     def put(self, node, top, change, base):
@@ -372,52 +377,43 @@
             copy.wait()
 
 
+def step_kernel(ring_far, ring_near, end, work, swept, first, change):
+    half = work.shape[1]
+    section = lax.axis_index("tm")
+    ring_low, ring_high = sides(ring_near, ring_far)
+    scale = 0.5 * COARSE
+    start = [jnp.where(section == 0, work[0, p], end[p]) for p in range(half)]
+    force = coarse_force(start)
+    one = [start[p] + 0.5 * force[p] + swept[0, p] for p in range(half)]
+    for p, v in ((0, ring_low), (half - 1, ring_high)):
+        one[p] = one[p] + jnp.where(section == 0, 0.0, scale * v[0])
+    force = coarse_force(one)
+    two = [one[p] + 0.5 * force[p] + swept[1, p] for p in range(half)]
+    for p, v in ((0, ring_low), (half - 1, ring_high)):
+        two[p] = two[p] + scale * jnp.where(section == 0, 0.0, v[1] + scale * start[p])
+    for p in range(half):
+        first[p] = start[p]
+        change[0, p] = one[p] - work[1, p]
+        change[1, p] = two[p] - work[2, p]
+
+
 def last_kernel(
-    nodes, ring_far, ring_near, end, one, two, moved, work, swept, spread,
-    updated, held, parts, result, load_sem, sem,
+    own, first, change, moved, one, two, work, updated, parts, result, sem
 ):
-    planes, halves = one.shape[0], one.shape[1]
-    rows = one.shape[3]
-    half = planes // 2
+    planes, half = one.shape[0], one.shape[0] // 2
     section = lax.axis_index("tm")
-    loads = [
-        pltpu.make_async_copy(
-            nodes.at[0, 0, :, :, pl.ds(h * LANES, LANES)], held.at[:, h], load_sem.at[h]
-        )
-        for h in range(halves)
-    ]
-
-
-    @pl.when(section == 0)
-    def _():
-        for copy in loads:
-            copy.start()
-        for copy in loads:
-            copy.wait()
+    out = Planes(updated, parts, result, sem)
+    for top in range(half):
+        out.put(1, top, change[0, top], lambda p, h, q: one[p, h, q])
+    for top in range(half):
+        out.put(2, top, change[1, top], lambda p, h, q: two[p, h, q])
 
     def start(p, h, q):
-        return jnp.where(section == 0, held[p, h, pl.ds(q, rows, stride=2), :], moved[p, h, q])
-
-    out = Planes(spread, updated, parts, result, sem)
-    first = [jnp.where(section == 0, work[0, p], end[p]) for p in range(half)]
+        return jnp.where(section == 0, own[p, h, q], moved[p, h, q])
+
     for top in range(half):
         mean = jnp.where(section == 0, work[0, top], moved[planes, 0, top])
         out.put(0, top, first[top] - mean, start)
-    ring_low, ring_high = sides(ring_near, ring_far)
-    scale = 0.5 * COARSE
-    force = coarse_force(first)
-    coarse_one = [first[p] + 0.5 * force[p] + swept[0, p] for p in range(half)]
-    for p, v in ((0, ring_low), (half - 1, ring_high)):
-        coarse_one[p] = coarse_one[p] + jnp.where(section == 0, 0.0, scale * v[0])
-    for top in range(half):
-        out.put(1, top, coarse_one[top] - work[1, top], lambda p, h, q: one[p, h, q])
-    force = coarse_force(coarse_one)
-    coarse_two = [coarse_one[p] + 0.5 * force[p] + swept[1, p] for p in range(half)]
-    for p, v in ((0, ring_low), (half - 1, ring_high)):
-        bend = jnp.where(section == 0, 0.0, v[1] + scale * first[p])
-        coarse_two[p] = coarse_two[p] + scale * bend
-    for top in range(half):
-        out.put(2, top, coarse_two[top] - work[2, top], lambda p, h, q: two[p, h, q])
     out.finish()
 
 
@@ -476,7 +472,7 @@
     packed = (3, half) + quarter
     size = planes * ny * nz * 4
 
-    pairs, spread = pair_matrix(nz), spread_matrix(nz // 2)
+    pairs = pair_matrix(nz)
     a_near, a_far = call(
         edge_kernel, "edge_mix", (nodes,), (0,), [plane, plane],
         [
@@ -487,9 +483,9 @@
         limit=EDGE_LIMIT, size=size * 2, flops=size,
     )
     got_a_near, got_a_far = exchange(a_near, a_far)
-    one_part, slope, rest, b_near, b_far, coarse_zero = call(
-        first_kernel, "first_stage", (nodes, pairs), (), [field, field, field, plane, plane, packed],
-        [pltpu.VMEM((5, ny, LANES), F32), pltpu.VMEM(field, F32), pltpu.VMEM(field, F32)],
+    one_part, slope, rest, b_near, b_far, coarse_zero, start = call(
+        first_kernel, "first_stage", (nodes, pairs), (), [field, field, field, plane, plane, packed, field],
+        [pltpu.VMEM((5, ny, LANES), F32), pltpu.VMEM(field, F32)],
         limit=FIRST_LIMIT,
         size=size * 6, flops=size * 10,
     )
@@ -507,23 +503,26 @@
         [(planes + 1,) + plane, pair, pair, (5, half) + quarter], [pltpu.VMEM((2,) + plane, F32)],
         aliases={0: 0}, size=size * 3, flops=size * 5,
     )
-    moved = swapped(two)
     got_near, got_far = exchange(h_near, h_far)
-    end, f_near, f_far, swept = call(
-        fourth_kernel, "coarse_chain", (work, got_near, got_far, h_near, h_far, coarse_forces), (),
-        [(half,) + quarter, pair, pair, (2, half) + quarter], size=size, flops=size,
+    end, f_near, f_far, swept, two = call(
+        fourth_kernel, "coarse_chain", (work, got_near, got_far, h_near, h_far, coarse_forces, two), (6,),
+        [(half,) + quarter, pair, pair, (2, half) + quarter, (planes + 1,) + plane],
+        any_outs=(4,), aliases={6: 4}, size=size, flops=size,
     )
     ring_far, ring_near = handed_on(f_near, f_far)
     end = swapped(end)
+    moved = swapped(two)
+    first, change = call(
+        step_kernel, "coarse_steps", (ring_far, ring_near, end, work, swept), (),
+        [(half,) + quarter, (2, half) + quarter], size=size, flops=size * 50000,
+    )
     updated, = call(
         last_kernel, "update",
-        (nodes, ring_far, ring_near, end, one, two, moved, work, swept, spread), (0,),
+        (start, first, change, moved, one, two, work), (),
         [(1, 3, planes, ny, nz)],
         [
-            pltpu.VMEM((planes, halves, ny, LANES), F32),
             pltpu.VMEM((3 * planes, halves, ny, LANES), F32),
             pltpu.VMEM((3 * planes, ny, nz), F32),
-            pltpu.SemaphoreType.DMA((halves,)),
             pltpu.SemaphoreType.DMA((3 * planes,)),
         ],
         any_outs=(0,), size=size * 6, flops=size * 5,

time: 47.2 us -> 46.6 us (0.987)
  starting transfers between devices: 16.6 us -> 15.6 us
    ppermute x3, waiting for transfers between devices: 14.2 us -> 11.8 us  [exchange(): lax.ppermute(near, 'space', list(enumerate(to_near)))]
    ppermute x3, waiting for transfers between devices: 1.77 us -> 3.27 us  [exchange(): lax.ppermute(far, 'space', list(enumerate(to_far)))]
    ppermute x2, waiting for transfers between devices: 3.57 us -> 4.76 us  [handed_on(): out.append(lax.ppermute(value, ('tm', 'space'), perm))]
    ppermute x2, starting transfers between devices: 1.3 us -> 0.51 us  [swapped(): return lax.ppermute(value, 'tm', [(0, 1), (1, 0)])]
    pallas_call x6 -> x7, Pallas kernels: 10.8 us -> 11 us  [call(): pl.pallas_call(kernel, name=name, out_shape=[jax.ShapeDtypeStruct(s, F32)...]
  transfers between devices with their start and end apart: 10 -> 10, of which waited for: 5 -> 4; matrix products, arithmetic and copies ran while one was open for 0% -> 0% of each run, Pallas kernels for 14% -> 14%
where the time goes in v6:
time: 46.6 us; the launch traced here: 46.5 us
  waiting for transfers between devices  19.8 us (42%)
  starting transfers between devices  15.6 us (33%)
  Pallas kernels  11 us (24%)
    ppermute x3, waiting for transfers between devices, exchange(): lax.ppermute(near, 'space', list(enumerate(to_near)))  11.8 us
    pallas_call x7, Pallas kernels, call(): pl.pallas_call(kernel, name=name, out_shape=[jax.ShapeDtypeStruct(s, F32)...  11 us
    ppermute x3, starting transfers between devices, exchange(): lax.ppermute(far, 'space', list(enumerate(to_far)))  7.85 us
    ppermute x2, waiting for transfers between devices, handed_on(): out.append(lax.ppermute(value, ('tm', 'space'), perm))  4.76 us
    ppermute x2, starting transfers between devices, handed_on(): out.append(lax.ppermute(value, ('tm', 'space'), perm))  3.8 us
    ppermute x3, starting transfers between devices, exchange(): lax.ppermute(near, 'space', list(enumerate(to_near)))  3.43 us
    ppermute x3, waiting for transfers between devices, exchange(): lax.ppermute(far, 'space', list(enumerate(to_far)))  3.27 us
  transfers between devices with their start and end apart: 10, of which 4 were waited for; matrix products, arithmetic and copies ran while one was open for 0% of the time, Pallas kernels for 14%

profile of v6, /device:TPU:1, one launch (start us, length us, event | category | flops | bytes accessed | tf_op | source)
XLA Modules:
  0.0 46.5 jit_solution(7626116289467714614)
XLA Ops:
  0.0 1.5 %edge_mix.1 = (f32[2,2,128,128]{3,2,1,0:T(8,128)S(1)}, f32[2,2,128,128]{3,2,1,0:T(8,128)S(1)}) custom-call(f32[1,3,4,256,256]{4,3,2,1,0:T(8,128)} %nodes.3), custom_call_target="tpu_custom_call" | custom-call | flops 1048576 | bytes 2097152 | tf_op jit(solution)/shard_map/edge_mix/pallas_call | solution.py:425
  1.5 2.1 %collective-permute-start = (f32[2,2,128,128]{3,2,1,0:T(8,128)S(1)}, f32[2,2,128,128]{3,2,1,0:T(8,128)S(1)}, u32[]{:S(2)}, u32[]{:S(2)}) collective-permute-start(f32[2,2,128,128]{3,2,1,0:T(8,128)S(1)} %get-tuple-element.34.own_near), channel_id=1, source_target_pairs={{0,1},{1,0},{2,3},{3,2},{4,5},{5,4},{6,7},{7,6},{8,9},{9,8},{10,11... | collective-permute-start | bytes 786440 | tf_op jit(solution)/shard_map/ppermute | solution.py:447
  3.7 3.3 %collective-permute-start.1 = (f32[2,2,128,128]{3,2,1,0:T(8,128)S(1)}, f32[2,2,128,128]{3,2,1,0:T(8,128)S(1)}, u32[]{:S(2)}, u32[]{:S(2)}) collective-permute-start(f32[2,2,128,128]{3,2,1,0:T(8,128)S(1)} %get-tuple-element.35.own_far), channel_id=1, source_target_pairs={{0,7},{1,2},{2,1},{3,4},{4,3},{5,6},{6,5},{7,0},{8,15},{9,10},{10,... | collective-permute-start | bytes 786440 | tf_op jit(solution)/shard_map/ppermute | solution.py:448
  6.9 4.6 %first_stage.1 = (f32[4,2,2,128,128]{4,3,2,1,0:T(8,128)S(1)}, f32[4,2,2,128,128]{4,3,2,1,0:T(8,128)S(1)}, f32[4,2,2,128,128]{4,3,2,1,0:T(8,128)S(1)}, f32[2,2,12...) custom-call(f32[1,3,4,256,256]{4,3,2,1,0:T(8,128)} %nodes.3, ...), custom_call_target="tpu_custom_call" | custom-call | flops 10485760 | bytes 6291456 | tf_op jit(solution)/shard_map/first_stage/pallas_call | solution.py:425
  11.6 0.1 collective-permute-start.2
  11.7 1.3 %collective-permute-start.3 = (f32[2,2,128,128]{3,2,1,0:T(8,128)S(1)}, f32[2,2,128,128]{3,2,1,0:T(8,128)S(1)}, u32[]{:S(2)}, u32[]{:S(2)}) collective-permute-start(f32[2,2,128,128]{3,2,1,0:T(8,128)S(1)} %get-tuple-element.39), channel_id=1, source_target_pairs={{0,7},{1,2},{2,1},{3,4},{4,3},{5,6},{6,5},{7,0},{8,15},{9,10},{10,... | collective-permute-start | bytes 786440 | tf_op jit(solution)/shard_map/ppermute | solution.py:448
  13.0 2.3 %collective-permute-done.near = f32[2,2,128,128]{3,2,1,0:T(8,128)S(1)} collective-permute-done((f32[2,2,128,128]{3,2,1,0:T(8,128)S(1)}, f32[2,2,128,128]{3,2,1,0:T(8,128)S(1)}, u32[]{:S(2)}, u32[]{:S(2)}) %collective-permute-start) | collective-permute-done | bytes 262176 | tf_op jit(solution)/shard_map/ppermute | solution.py:447
  15.3 1.8 %second_stage.1 = (f32[4,2,2,128,128]{4,3,2,1,0:T(8,128)S(1)}, f32[5,2,2,128,128]{4,3,2,1,0:T(8,128)S(1)}, f32[3,2,128,128]{3,2,1,0:T(8,128)S(1)}, f32[2,3,2,128...) custom-call(f32[4,2,2,128,128]{4,3,2,1,0:T(8,128)S(1)} %get-tuple-element.31.one_in, ...), custom_call_target="tpu_custom_call" | custom-call | flops 10485760 | bytes 6291456 | tf_op jit(solution)/shard_map/second_stage/pallas_call | solution.py:425
  17.1 9.4 %collective-permute-done.2.near = f32[2,2,128,128]{3,2,1,0:T(8,128)S(1)} collective-permute-done((f32[2,2,128,128]{3,2,1,0:T(8,128)S(1)}, f32[2,2,128,128]{3,2,1,0:T(8,128)S(1)}, u32[]{:S(2)}, u32[]{:S(2)}) %collective-permute-start.2) | collective-permute-done | bytes 262176 | tf_op jit(solution)/shard_map/ppermute | solution.py:447
  26.6 0.0 collective-permute-done.3.far
  26.6 0.7 %third_stage.1 = (f32[5,2,2,128,128]{4,3,2,1,0:T(8,128)S(1)}, f32[2,128,128]{2,1,0:T(8,128)S(1)}, f32[2,128,128]{2,1,0:T(8,128)S(1)}, f32[5,2,128,128]{3,2,1,0:T(8,128)S(1)}) custom-call(f32[5,2,2,128,128]{4,3,2,1,0:T(8,128)S(1)} %get-tuple-element.37.two_in, f32[2,2,128,128]{3,2,1,0:T(8,128)S(1)} %collective-permute-done.2.near, ...), custom_call_target="tpu_custom_call", output_to_operand_aliasing={{0}: (0, {})} | custom-call | flops 5242880 | bytes 3145728 | tf_op jit(solution)/shard_map/third_stage/pallas_call | solution.py:425
  27.2 1.2 %collective-permute-start.4 = (f32[2,128,128]{2,1,0:T(8,128)S(1)}, f32[2,128,128]{2,1,0:T(8,128)S(1)}, u32[]{:S(2)}, u32[]{:S(2)}) collective-permute-start(f32[2,128,128]{2,1,0:T(8,128)S(1)} %get-tuple-element.44.own_near), channel_id=1, source_target_pairs={{0,1},{1,0},{2,3},{3,2},{4,5},{5,4},{6,7},{7,6},{8,9},{9,8},{10,11... | collective-permute-start | bytes 393224 | tf_op jit(solution)/shard_map/ppermute | solution.py:447
  28.5 3.2 %collective-permute-start.5 = (f32[2,128,128]{2,1,0:T(8,128)S(1)}, f32[2,128,128]{2,1,0:T(8,128)S(1)}, u32[]{:S(2)}, u32[]{:S(2)}) collective-permute-start(f32[2,128,128]{2,1,0:T(8,128)S(1)} %get-tuple-element.45.own_far), channel_id=1, source_target_pairs={{0,7},{1,2},{2,1},{3,4},{4,3},{5,6},{6,5},{7,0},{8,15},{9,10},{10,... | collective-permute-start | bytes 393224 | tf_op jit(solution)/shard_map/ppermute | solution.py:448
  31.7 0.0 collective-permute-done.4.near
  31.7 3.3 %collective-permute-done.5.far = f32[2,128,128]{2,1,0:T(8,128)S(1)} collective-permute-done((f32[2,128,128]{2,1,0:T(8,128)S(1)}, f32[2,128,128]{2,1,0:T(8,128)S(1)}, u32[]{:S(2)}, u32[]{:S(2)}) %collective-permute-start.5) | collective-permute-done | bytes 131104 | tf_op jit(solution)/shard_map/ppermute | solution.py:448
  35.0 3.3 %collective-permute-start.6 = (f32[2,128,128]{2,1,0:T(8,128)S(1)}, f32[2,128,128]{2,1,0:T(8,128)S(1)}, u32[]{:S(2)}, u32[]{:S(2)}) collective-permute-start(f32[2,128,128]{2,1,0:T(8,128)S(1)} %get-tuple-element.47), channel_id=1, source_target_pairs={{0,15},{1,10},{2,9},{3,12},{4,11},{5,14},{6,13},{7,8},{8,0},{9,1},... | collective-permute-start | bytes 393224 | tf_op jit(solution)/shard_map/ppermute | solution.py:461
  38.3 0.5 %collective-permute-start.7 = (f32[2,128,128]{2,1,0:T(8,128)S(1)}, f32[2,128,128]{2,1,0:T(8,128)S(1)}, u32[]{:S(2)}, u32[]{:S(2)}) collective-permute-start(f32[2,128,128]{2,1,0:T(8,128)S(1)} %get-tuple-element.48), channel_id=1, source_target_pairs={{0,9},{1,8},{2,11},{3,10},{4,13},{5,12},{6,15},{7,14},{8,0},{9,1},... | collective-permute-start | bytes 393224 | tf_op jit(solution)/shard_map/ppermute | solution.py:461
  38.8 0.0 collective-permute-start.8
  38.8 0.5 %collective-permute-start.9 = (f32[5,2,2,128,128]{4,3,2,1,0:T(8,128)S(1)}, f32[5,2,2,128,128]{4,3,2,1,0:T(8,128)S(1)}, u32[]{:S(2)}, u32[]{:S(2)}) collective-permute-start(f32[5,2,2,128,128]{4,3,2,1,0:T(8,128)S(1)} %get-tuple-element.53.two), channel_id=1, source_target_pairs={{0,8},{8,0},{1,9},{9,1},{2,10},{10,2},{3,11},{11,3},{4,12},{12,4},... | collective-permute-start | bytes 3932168 | tf_op jit(solution)/shard_map/ppermute | solution.py:453
  39.3 4.8 %collective-permute-done.6.ring_far = f32[2,128,128]{2,1,0:T(8,128)S(1)} collective-permute-done((f32[2,128,128]{2,1,0:T(8,128)S(1)}, f32[2,128,128]{2,1,0:T(8,128)S(1)}, u32[]{:S(2)}, u32[]{:S(2)}) %collective-permute-start.6) | collective-permute-done | bytes 131104 | tf_op jit(solution)/shard_map/ppermute | solution.py:461
  44.1 0.0 collective-permute-done.7.ring_near
  44.1 0.3 coarse_steps.1
  44.4 0.0 collective-permute-done.9.moved
  44.4 2.1 %update.1 = f32[1,3,4,256,256]{4,3,2,1,0:T(8,128)} custom-call(f32[4,2,2,128,128]{4,3,2,1,0:T(8,128)S(1)} %get-tuple-element.30.own, f32[2,128,128]{2,1,0:T(8,128)S(1)} %get-tuple-element.51.first, f32[2,2,128,128]{3,2,1,0:T(8,128)S(1)} %get-tuple-element.52.change, f32[5,2,2,128,128]{4,3,2,1,0:T(8,128)S(1)} %collective-permute-done.9.moved, ...), custom_call_target="tpu_custom_call" | custom-call | flops 5242880 | bytes 6291456 | tf_op jit(solution)/shard_map/update/pallas_call | solution.py:425
  (5 shorter events, 0.1 us)
Async XLA Ops:
  0.0 6.9 %copy-start = (bf16[256,256]{1,0:T(8,128)(2,1)S(1)}, bf16[256,256]{1,0:T(8,128)(2,1)}, u32[]{:S(2)}) copy-start(bf16[256,256]{1,0:T(8,128)(2,1)} %constant.2.clone.pairs) | copy-start | bytes 393220
  1.5 13.8 %collective-permute-start = (f32[2,2,128,128]{3,2,1,0:T(8,128)S(1)}, f32[2,2,128,128]{3,2,1,0:T(8,128)S(1)}, u32[]{:S(2)}, u32[]{:S(2)}) collective-permute-start(f32[2,2,128,128]{3,2,1,0:T(8,128)S(1)} %get-tuple-element.34.own_near), channel_id=1, source_target_pairs={{0,1},{1,0},{2,3},{3,2},{4,5},{5,4},{6,7},{7,6},{8,9},{9,8},{10,11... | collective-permute-start | bytes 786440 | tf_op jit(solution)/shard_map/ppermute | solution.py:447
  3.7 11.7 %collective-permute-start.1 = (f32[2,2,128,128]{3,2,1,0:T(8,128)S(1)}, f32[2,2,128,128]{3,2,1,0:T(8,128)S(1)}, u32[]{:S(2)}, u32[]{:S(2)}) collective-permute-start(f32[2,2,128,128]{3,2,1,0:T(8,128)S(1)} %get-tuple-element.35.own_far), channel_id=1, source_target_pairs={{0,7},{1,2},{2,1},{3,4},{4,3},{5,6},{6,5},{7,0},{8,15},{9,10},{10,... | collective-permute-start | bytes 786440 | tf_op jit(solution)/shard_map/ppermute | solution.py:448
  11.6 15.0 %collective-permute-start.2 = (f32[2,2,128,128]{3,2,1,0:T(8,128)S(1)}, f32[2,2,128,128]{3,2,1,0:T(8,128)S(1)}, u32[]{:S(2)}, u32[]{:S(2)}) collective-permute-start(f32[2,2,128,128]{3,2,1,0:T(8,128)S(1)} %get-tuple-element.38), channel_id=1, source_target_pairs={{0,1},{1,0},{2,3},{3,2},{4,5},{5,4},{6,7},{7,6},{8,9},{9,8},{10,11... | collective-permute-start | bytes 786440 | tf_op jit(solution)/shard_map/ppermute | solution.py:447
  11.7 14.9 %collective-permute-start.3 = (f32[2,2,128,128]{3,2,1,0:T(8,128)S(1)}, f32[2,2,128,128]{3,2,1,0:T(8,128)S(1)}, u32[]{:S(2)}, u32[]{:S(2)}) collective-permute-start(f32[2,2,128,128]{3,2,1,0:T(8,128)S(1)} %get-tuple-element.39), channel_id=1, source_target_pairs={{0,7},{1,2},{2,1},{3,4},{4,3},{5,6},{6,5},{7,0},{8,15},{9,10},{10,... | collective-permute-start | bytes 786440 | tf_op jit(solution)/shard_map/ppermute | solution.py:448
  27.2 4.5 %collective-permute-start.4 = (f32[2,128,128]{2,1,0:T(8,128)S(1)}, f32[2,128,128]{2,1,0:T(8,128)S(1)}, u32[]{:S(2)}, u32[]{:S(2)}) collective-permute-start(f32[2,128,128]{2,1,0:T(8,128)S(1)} %get-tuple-element.44.own_near), channel_id=1, source_target_pairs={{0,1},{1,0},{2,3},{3,2},{4,5},{5,4},{6,7},{7,6},{8,9},{9,8},{10,11... | collective-permute-start | bytes 393224 | tf_op jit(solution)/shard_map/ppermute | solution.py:447
  28.5 6.5 %collective-permute-start.5 = (f32[2,128,128]{2,1,0:T(8,128)S(1)}, f32[2,128,128]{2,1,0:T(8,128)S(1)}, u32[]{:S(2)}, u32[]{:S(2)}) collective-permute-start(f32[2,128,128]{2,1,0:T(8,128)S(1)} %get-tuple-element.45.own_far), channel_id=1, source_target_pairs={{0,7},{1,2},{2,1},{3,4},{4,3},{5,6},{6,5},{7,0},{8,15},{9,10},{10,... | collective-permute-start | bytes 393224 | tf_op jit(solution)/shard_map/ppermute | solution.py:448
  35.0 9.1 %collective-permute-start.6 = (f32[2,128,128]{2,1,0:T(8,128)S(1)}, f32[2,128,128]{2,1,0:T(8,128)S(1)}, u32[]{:S(2)}, u32[]{:S(2)}) collective-permute-start(f32[2,128,128]{2,1,0:T(8,128)S(1)} %get-tuple-element.47), channel_id=1, source_target_pairs={{0,15},{1,10},{2,9},{3,12},{4,11},{5,14},{6,13},{7,8},{8,0},{9,1},... | collective-permute-start | bytes 393224 | tf_op jit(solution)/shard_map/ppermute | solution.py:461
  38.3 5.8 %collective-permute-start.7 = (f32[2,128,128]{2,1,0:T(8,128)S(1)}, f32[2,128,128]{2,1,0:T(8,128)S(1)}, u32[]{:S(2)}, u32[]{:S(2)}) collective-permute-start(f32[2,128,128]{2,1,0:T(8,128)S(1)} %get-tuple-element.48), channel_id=1, source_target_pairs={{0,9},{1,8},{2,11},{3,10},{4,13},{5,12},{6,15},{7,14},{8,0},{9,1},... | collective-permute-start | bytes 393224 | tf_op jit(solution)/shard_map/ppermute | solution.py:461
  38.8 5.3 %collective-permute-start.8 = (f32[2,128,128]{2,1,0:T(8,128)S(1)}, f32[2,128,128]{2,1,0:T(8,128)S(1)}, u32[]{:S(2)}, u32[]{:S(2)}) collective-permute-start(f32[2,128,128]{2,1,0:T(8,128)S(1)} %get-tuple-element.49), channel_id=1, source_target_pairs={{0,8},{8,0},{1,9},{9,1},{2,10},{10,2},{3,11},{11,3},{4,12},{12,4},... | collective-permute-start | bytes 393224 | tf_op jit(solution)/shard_map/ppermute | solution.py:453
  38.8 5.6 %collective-permute-start.9 = (f32[5,2,2,128,128]{4,3,2,1,0:T(8,128)S(1)}, f32[5,2,2,128,128]{4,3,2,1,0:T(8,128)S(1)}, u32[]{:S(2)}, u32[]{:S(2)}) collective-permute-start(f32[5,2,2,128,128]{4,3,2,1,0:T(8,128)S(1)} %get-tuple-element.53.two), channel_id=1, source_target_pairs={{0,8},{8,0},{1,9},{9,1},{2,10},{10,2},{3,11},{11,3},{4,12},{12,4},... | collective-permute-start | bytes 3932168 | tf_op jit(solution)/shard_map/ppermute | solution.py:453

commit v7 on v6

--- a/solution.py
+++ b/solution.py
@@ -377,36 +377,17 @@
             copy.wait()
 
 
-def step_kernel(ring_far, ring_near, end, work, swept, first, change):
-    half = work.shape[1]
-    section = lax.axis_index("tm")
-    ring_low, ring_high = sides(ring_near, ring_far)
-    scale = 0.5 * COARSE
-    start = [jnp.where(section == 0, work[0, p], end[p]) for p in range(half)]
-    force = coarse_force(start)
-    one = [start[p] + 0.5 * force[p] + swept[0, p] for p in range(half)]
-    for p, v in ((0, ring_low), (half - 1, ring_high)):
-        one[p] = one[p] + jnp.where(section == 0, 0.0, scale * v[0])
-    force = coarse_force(one)
-    two = [one[p] + 0.5 * force[p] + swept[1, p] for p in range(half)]
-    for p, v in ((0, ring_low), (half - 1, ring_high)):
-        two[p] = two[p] + scale * jnp.where(section == 0, 0.0, v[1] + scale * start[p])
-    for p in range(half):
-        first[p] = start[p]
-        change[0, p] = one[p] - work[1, p]
-        change[1, p] = two[p] - work[2, p]
+def arrived_kernel(*refs):
+    del refs
 
 
 def last_kernel(
-    own, first, change, moved, one, two, work, updated, parts, result, sem
+    own, ring_far, ring_near, end, moved, one, two, work, swept, updated, parts, result, sem
 ):
     planes, half = one.shape[0], one.shape[0] // 2
     section = lax.axis_index("tm")
     out = Planes(updated, parts, result, sem)
-    for top in range(half):
-        out.put(1, top, change[0, top], lambda p, h, q: one[p, h, q])
-    for top in range(half):
-        out.put(2, top, change[1, top], lambda p, h, q: two[p, h, q])
+    first = [jnp.where(section == 0, work[0, p], end[p]) for p in range(half)]
 
     def start(p, h, q):
         return jnp.where(section == 0, own[p, h, q], moved[p, h, q])
@@ -414,6 +395,20 @@
     for top in range(half):
         mean = jnp.where(section == 0, work[0, top], moved[planes, 0, top])
         out.put(0, top, first[top] - mean, start)
+    ring_low, ring_high = sides(ring_near, ring_far)
+    scale = 0.5 * COARSE
+    force = coarse_force(first)
+    step_one = [first[p] + 0.5 * force[p] + swept[0, p] for p in range(half)]
+    for p, v in ((0, ring_low), (half - 1, ring_high)):
+        step_one[p] = step_one[p] + jnp.where(section == 0, 0.0, scale * v[0])
+    for top in range(half):
+        out.put(1, top, step_one[top] - work[1, top], lambda p, h, q: one[p, h, q])
+    force = coarse_force(step_one)
+    step_two = [step_one[p] + 0.5 * force[p] + swept[1, p] for p in range(half)]
+    for p, v in ((0, ring_low), (half - 1, ring_high)):
+        step_two[p] = step_two[p] + scale * jnp.where(section == 0, 0.0, v[1] + scale * first[p])
+    for top in range(half):
+        out.put(2, top, step_two[top] - work[2, top], lambda p, h, q: two[p, h, q])
     out.finish()
 
 
@@ -512,13 +507,14 @@
     ring_far, ring_near = handed_on(f_near, f_far)
     end = swapped(end)
     moved = swapped(two)
-    first, change = call(
-        step_kernel, "coarse_steps", (ring_far, ring_near, end, work, swept), (),
-        [(half,) + quarter, (2, half) + quarter], size=size, flops=size * 50000,
+    ring_far, ring_near, end = call(
+        arrived_kernel, "arrived", (ring_far, ring_near, end), (0, 1, 2),
+        [pair, pair, (half,) + quarter], any_outs=(0, 1, 2), aliases={0: 0, 1: 1, 2: 2},
+        size=size, flops=size * 50000,
     )
     updated, = call(
         last_kernel, "update",
-        (start, first, change, moved, one, two, work), (),
+        (start, ring_far, ring_near, end, moved, one, two, work, swept), (),
         [(1, 3, planes, ny, nz)],
         [
             pltpu.VMEM((3 * planes, halves, ny, LANES), F32),

time: 46.6 us -> 46.5 us (level)
  no operation moved by 1% of the time
where the time goes in v7:
time: 46.5 us; the launch traced here: 46.3 us
  waiting for transfers between devices  19.8 us (43%)
  starting transfers between devices  15.6 us (34%)
  Pallas kernels  10.8 us (23%)
    ppermute x3, waiting for transfers between devices, exchange(): lax.ppermute(near, 'space', list(enumerate(to_near)))  11.8 us
    pallas_call x7, Pallas kernels, call(): pl.pallas_call(kernel, name=name, out_shape=[jax.ShapeDtypeStruct(s, F32)...  10.8 us
    ppermute x3, starting transfers between devices, exchange(): lax.ppermute(far, 'space', list(enumerate(to_far)))  7.85 us
    ppermute x2, waiting for transfers between devices, handed_on(): out.append(lax.ppermute(value, ('tm', 'space'), perm))  4.76 us
    ppermute x2, starting transfers between devices, handed_on(): out.append(lax.ppermute(value, ('tm', 'space'), perm))  3.8 us
    ppermute x3, starting transfers between devices, exchange(): lax.ppermute(near, 'space', list(enumerate(to_near)))  3.43 us
    ppermute x3, waiting for transfers between devices, exchange(): lax.ppermute(far, 'space', list(enumerate(to_far)))  3.27 us
  transfers between devices with their start and end apart: 10, of which 4 were waited for; matrix products, arithmetic and copies ran while one was open for 0% of the time, Pallas kernels for 14%

profile of v7, /device:TPU:1, one launch (start us, length us, event | category | flops | bytes accessed | tf_op | source)
XLA Modules:
  0.0 46.3 jit_solution(4098300148052908887)
XLA Ops:
  0.0 1.5 %edge_mix.1 = (f32[2,2,128,128]{3,2,1,0:T(8,128)S(1)}, f32[2,2,128,128]{3,2,1,0:T(8,128)S(1)}) custom-call(f32[1,3,4,256,256]{4,3,2,1,0:T(8,128)} %nodes.3), custom_call_target="tpu_custom_call" | custom-call | flops 1048576 | bytes 2097152 | tf_op jit(solution)/shard_map/edge_mix/pallas_call | solution.py:420
  1.5 2.1 %collective-permute-start = (f32[2,2,128,128]{3,2,1,0:T(8,128)S(1)}, f32[2,2,128,128]{3,2,1,0:T(8,128)S(1)}, u32[]{:S(2)}, u32[]{:S(2)}) collective-permute-start(f32[2,2,128,128]{3,2,1,0:T(8,128)S(1)} %get-tuple-element.35.own_near), channel_id=1, source_target_pairs={{0,1},{1,0},{2,3},{3,2},{4,5},{5,4},{6,7},{7,6},{8,9},{9,8},{10,11... | collective-permute-start | bytes 786440 | tf_op jit(solution)/shard_map/ppermute | solution.py:442
  3.7 3.3 %collective-permute-start.1 = (f32[2,2,128,128]{3,2,1,0:T(8,128)S(1)}, f32[2,2,128,128]{3,2,1,0:T(8,128)S(1)}, u32[]{:S(2)}, u32[]{:S(2)}) collective-permute-start(f32[2,2,128,128]{3,2,1,0:T(8,128)S(1)} %get-tuple-element.36.own_far), channel_id=1, source_target_pairs={{0,7},{1,2},{2,1},{3,4},{4,3},{5,6},{6,5},{7,0},{8,15},{9,10},{10,... | collective-permute-start | bytes 786440 | tf_op jit(solution)/shard_map/ppermute | solution.py:443
  6.9 4.6 %first_stage.1 = (f32[4,2,2,128,128]{4,3,2,1,0:T(8,128)S(1)}, f32[4,2,2,128,128]{4,3,2,1,0:T(8,128)S(1)}, f32[4,2,2,128,128]{4,3,2,1,0:T(8,128)S(1)}, f32[2,2,12...) custom-call(f32[1,3,4,256,256]{4,3,2,1,0:T(8,128)} %nodes.3, ...), custom_call_target="tpu_custom_call" | custom-call | flops 10485760 | bytes 6291456 | tf_op jit(solution)/shard_map/first_stage/pallas_call | solution.py:420
  11.6 0.1 collective-permute-start.2
  11.7 1.3 %collective-permute-start.3 = (f32[2,2,128,128]{3,2,1,0:T(8,128)S(1)}, f32[2,2,128,128]{3,2,1,0:T(8,128)S(1)}, u32[]{:S(2)}, u32[]{:S(2)}) collective-permute-start(f32[2,2,128,128]{3,2,1,0:T(8,128)S(1)} %get-tuple-element.40), channel_id=1, source_target_pairs={{0,7},{1,2},{2,1},{3,4},{4,3},{5,6},{6,5},{7,0},{8,15},{9,10},{10,... | collective-permute-start | bytes 786440 | tf_op jit(solution)/shard_map/ppermute | solution.py:443
  13.0 2.3 %collective-permute-done.near = f32[2,2,128,128]{3,2,1,0:T(8,128)S(1)} collective-permute-done((f32[2,2,128,128]{3,2,1,0:T(8,128)S(1)}, f32[2,2,128,128]{3,2,1,0:T(8,128)S(1)}, u32[]{:S(2)}, u32[]{:S(2)}) %collective-permute-start) | collective-permute-done | bytes 262176 | tf_op jit(solution)/shard_map/ppermute | solution.py:442
  15.3 0.0 collective-permute-done.1.far
  15.3 1.8 %second_stage.1 = (f32[4,2,2,128,128]{4,3,2,1,0:T(8,128)S(1)}, f32[5,2,2,128,128]{4,3,2,1,0:T(8,128)S(1)}, f32[3,2,128,128]{3,2,1,0:T(8,128)S(1)}, f32[2,3,2,128...) custom-call(f32[4,2,2,128,128]{4,3,2,1,0:T(8,128)S(1)} %get-tuple-element.32.one_in, ...), custom_call_target="tpu_custom_call" | custom-call | flops 10485760 | bytes 6291456 | tf_op jit(solution)/shard_map/second_stage/pallas_call | solution.py:420
  17.1 9.4 %collective-permute-done.2.near = f32[2,2,128,128]{3,2,1,0:T(8,128)S(1)} collective-permute-done((f32[2,2,128,128]{3,2,1,0:T(8,128)S(1)}, f32[2,2,128,128]{3,2,1,0:T(8,128)S(1)}, u32[]{:S(2)}, u32[]{:S(2)}) %collective-permute-start.2) | collective-permute-done | bytes 262176 | tf_op jit(solution)/shard_map/ppermute | solution.py:442
  26.6 0.0 collective-permute-done.3.far
  26.6 0.7 %third_stage.1 = (f32[5,2,2,128,128]{4,3,2,1,0:T(8,128)S(1)}, f32[2,128,128]{2,1,0:T(8,128)S(1)}, f32[2,128,128]{2,1,0:T(8,128)S(1)}, f32[5,2,128,128]{3,2,1,0:T(8,128)S(1)}) custom-call(f32[5,2,2,128,128]{4,3,2,1,0:T(8,128)S(1)} %get-tuple-element.38.two_in, f32[2,2,128,128]{3,2,1,0:T(8,128)S(1)} %collective-permute-done.2.near, ...), custom_call_target="tpu_custom_call", output_to_operand_aliasing={{0}: (0, {})} | custom-call | flops 5242880 | bytes 3145728 | tf_op jit(solution)/shard_map/third_stage/pallas_call | solution.py:420
  27.2 1.2 %collective-permute-start.4 = (f32[2,128,128]{2,1,0:T(8,128)S(1)}, f32[2,128,128]{2,1,0:T(8,128)S(1)}, u32[]{:S(2)}, u32[]{:S(2)}) collective-permute-start(f32[2,128,128]{2,1,0:T(8,128)S(1)} %get-tuple-element.45.own_near), channel_id=1, source_target_pairs={{0,1},{1,0},{2,3},{3,2},{4,5},{5,4},{6,7},{7,6},{8,9},{9,8},{10,11... | collective-permute-start | bytes 393224 | tf_op jit(solution)/shard_map/ppermute | solution.py:442
  28.5 3.2 %collective-permute-start.5 = (f32[2,128,128]{2,1,0:T(8,128)S(1)}, f32[2,128,128]{2,1,0:T(8,128)S(1)}, u32[]{:S(2)}, u32[]{:S(2)}) collective-permute-start(f32[2,128,128]{2,1,0:T(8,128)S(1)} %get-tuple-element.46.own_far), channel_id=1, source_target_pairs={{0,7},{1,2},{2,1},{3,4},{4,3},{5,6},{6,5},{7,0},{8,15},{9,10},{10,... | collective-permute-start | bytes 393224 | tf_op jit(solution)/shard_map/ppermute | solution.py:443
  31.7 0.0 collective-permute-done.4.near
  31.7 3.3 %collective-permute-done.5.far = f32[2,128,128]{2,1,0:T(8,128)S(1)} collective-permute-done((f32[2,128,128]{2,1,0:T(8,128)S(1)}, f32[2,128,128]{2,1,0:T(8,128)S(1)}, u32[]{:S(2)}, u32[]{:S(2)}) %collective-permute-start.5) | collective-permute-done | bytes 131104 | tf_op jit(solution)/shard_map/ppermute | solution.py:443
  35.0 3.3 %collective-permute-start.6 = (f32[2,128,128]{2,1,0:T(8,128)S(1)}, f32[2,128,128]{2,1,0:T(8,128)S(1)}, u32[]{:S(2)}, u32[]{:S(2)}) collective-permute-start(f32[2,128,128]{2,1,0:T(8,128)S(1)} %get-tuple-element.48), channel_id=1, source_target_pairs={{0,15},{1,10},{2,9},{3,12},{4,11},{5,14},{6,13},{7,8},{8,0},{9,1},... | collective-permute-start | bytes 393224 | tf_op jit(solution)/shard_map/ppermute | solution.py:456
  38.3 0.5 %collective-permute-start.7 = (f32[2,128,128]{2,1,0:T(8,128)S(1)}, f32[2,128,128]{2,1,0:T(8,128)S(1)}, u32[]{:S(2)}, u32[]{:S(2)}) collective-permute-start(f32[2,128,128]{2,1,0:T(8,128)S(1)} %get-tuple-element.49), channel_id=1, source_target_pairs={{0,9},{1,8},{2,11},{3,10},{4,13},{5,12},{6,15},{7,14},{8,0},{9,1},... | collective-permute-start | bytes 393224 | tf_op jit(solution)/shard_map/ppermute | solution.py:456
  38.8 0.0 collective-permute-start.8
  38.8 0.5 %collective-permute-start.9 = (f32[5,2,2,128,128]{4,3,2,1,0:T(8,128)S(1)}, f32[5,2,2,128,128]{4,3,2,1,0:T(8,128)S(1)}, u32[]{:S(2)}, u32[]{:S(2)}) collective-permute-start(f32[5,2,2,128,128]{4,3,2,1,0:T(8,128)S(1)} %get-tuple-element.54.two), channel_id=1, source_target_pairs={{0,8},{8,0},{1,9},{9,1},{2,10},{10,2},{3,11},{11,3},{4,12},{12,4},... | collective-permute-start | bytes 3932168 | tf_op jit(solution)/shard_map/ppermute | solution.py:448
  39.3 4.8 %collective-permute-done.6.refs_0_ = f32[2,128,128]{2,1,0:T(8,128)S(1)} collective-permute-done((f32[2,128,128]{2,1,0:T(8,128)S(1)}, f32[2,128,128]{2,1,0:T(8,128)S(1)}, u32[]{:S(2)}, u32[]{:S(2)}) %collective-permute-start.6) | collective-permute-done | bytes 131104 | tf_op jit(solution)/shard_map/ppermute | solution.py:456
  44.1 0.0 collective-permute-done.7.refs_1_
  44.1 0.0 collective-permute-done.8.refs_2_
  44.1 2.2 %update.1 = f32[1,3,4,256,256]{4,3,2,1,0:T(8,128)} custom-call(f32[4,2,2,128,128]{4,3,2,1,0:T(8,128)S(1)} %get-tuple-element.31.own, f32[2,128,128]{2,1,0:T(8,128)S(1)} %get-tuple-element.51.ring_far, f32[2,128,128]{2,1,0:T(8,128)S(1)} %get-tuple-element.52.ring_near, f32[2,128,128]{2,1,0:T(8,128)S(1)} %get-tuple-element.53.end, ...), custom_call_target="tpu_custom_call" | custom-call | flops 5242880 | bytes 6291456 | tf_op jit(solution)/shard_map/update/pallas_call | solution.py:420
  (5 shorter events, 0.1 us)
Async XLA Ops:
  0.0 6.9 %copy-start = (bf16[256,256]{1,0:T(8,128)(2,1)S(1)}, bf16[256,256]{1,0:T(8,128)(2,1)}, u32[]{:S(2)}) copy-start(bf16[256,256]{1,0:T(8,128)(2,1)} %constant.2.clone.pairs) | copy-start | bytes 393220
  1.5 13.8 %collective-permute-start = (f32[2,2,128,128]{3,2,1,0:T(8,128)S(1)}, f32[2,2,128,128]{3,2,1,0:T(8,128)S(1)}, u32[]{:S(2)}, u32[]{:S(2)}) collective-permute-start(f32[2,2,128,128]{3,2,1,0:T(8,128)S(1)} %get-tuple-element.35.own_near), channel_id=1, source_target_pairs={{0,1},{1,0},{2,3},{3,2},{4,5},{5,4},{6,7},{7,6},{8,9},{9,8},{10,11... | collective-permute-start | bytes 786440 | tf_op jit(solution)/shard_map/ppermute | solution.py:442
  3.7 11.7 %collective-permute-start.1 = (f32[2,2,128,128]{3,2,1,0:T(8,128)S(1)}, f32[2,2,128,128]{3,2,1,0:T(8,128)S(1)}, u32[]{:S(2)}, u32[]{:S(2)}) collective-permute-start(f32[2,2,128,128]{3,2,1,0:T(8,128)S(1)} %get-tuple-element.36.own_far), channel_id=1, source_target_pairs={{0,7},{1,2},{2,1},{3,4},{4,3},{5,6},{6,5},{7,0},{8,15},{9,10},{10,... | collective-permute-start | bytes 786440 | tf_op jit(solution)/shard_map/ppermute | solution.py:443
  11.6 15.0 %collective-permute-start.2 = (f32[2,2,128,128]{3,2,1,0:T(8,128)S(1)}, f32[2,2,128,128]{3,2,1,0:T(8,128)S(1)}, u32[]{:S(2)}, u32[]{:S(2)}) collective-permute-start(f32[2,2,128,128]{3,2,1,0:T(8,128)S(1)} %get-tuple-element.39), channel_id=1, source_target_pairs={{0,1},{1,0},{2,3},{3,2},{4,5},{5,4},{6,7},{7,6},{8,9},{9,8},{10,11... | collective-permute-start | bytes 786440 | tf_op jit(solution)/shard_map/ppermute | solution.py:442
  11.7 14.9 %collective-permute-start.3 = (f32[2,2,128,128]{3,2,1,0:T(8,128)S(1)}, f32[2,2,128,128]{3,2,1,0:T(8,128)S(1)}, u32[]{:S(2)}, u32[]{:S(2)}) collective-permute-start(f32[2,2,128,128]{3,2,1,0:T(8,128)S(1)} %get-tuple-element.40), channel_id=1, source_target_pairs={{0,7},{1,2},{2,1},{3,4},{4,3},{5,6},{6,5},{7,0},{8,15},{9,10},{10,... | collective-permute-start | bytes 786440 | tf_op jit(solution)/shard_map/ppermute | solution.py:443
  27.2 4.5 %collective-permute-start.4 = (f32[2,128,128]{2,1,0:T(8,128)S(1)}, f32[2,128,128]{2,1,0:T(8,128)S(1)}, u32[]{:S(2)}, u32[]{:S(2)}) collective-permute-start(f32[2,128,128]{2,1,0:T(8,128)S(1)} %get-tuple-element.45.own_near), channel_id=1, source_target_pairs={{0,1},{1,0},{2,3},{3,2},{4,5},{5,4},{6,7},{7,6},{8,9},{9,8},{10,11... | collective-permute-start | bytes 393224 | tf_op jit(solution)/shard_map/ppermute | solution.py:442
  28.5 6.5 %collective-permute-start.5 = (f32[2,128,128]{2,1,0:T(8,128)S(1)}, f32[2,128,128]{2,1,0:T(8,128)S(1)}, u32[]{:S(2)}, u32[]{:S(2)}) collective-permute-start(f32[2,128,128]{2,1,0:T(8,128)S(1)} %get-tuple-element.46.own_far), channel_id=1, source_target_pairs={{0,7},{1,2},{2,1},{3,4},{4,3},{5,6},{6,5},{7,0},{8,15},{9,10},{10,... | collective-permute-start | bytes 393224 | tf_op jit(solution)/shard_map/ppermute | solution.py:443
  35.0 9.1 %collective-permute-start.6 = (f32[2,128,128]{2,1,0:T(8,128)S(1)}, f32[2,128,128]{2,1,0:T(8,128)S(1)}, u32[]{:S(2)}, u32[]{:S(2)}) collective-permute-start(f32[2,128,128]{2,1,0:T(8,128)S(1)} %get-tuple-element.48), channel_id=1, source_target_pairs={{0,15},{1,10},{2,9},{3,12},{4,11},{5,14},{6,13},{7,8},{8,0},{9,1},... | collective-permute-start | bytes 393224 | tf_op jit(solution)/shard_map/ppermute | solution.py:456
  38.3 5.8 %collective-permute-start.7 = (f32[2,128,128]{2,1,0:T(8,128)S(1)}, f32[2,128,128]{2,1,0:T(8,128)S(1)}, u32[]{:S(2)}, u32[]{:S(2)}) collective-permute-start(f32[2,128,128]{2,1,0:T(8,128)S(1)} %get-tuple-element.49), channel_id=1, source_target_pairs={{0,9},{1,8},{2,11},{3,10},{4,13},{5,12},{6,15},{7,14},{8,0},{9,1},... | collective-permute-start | bytes 393224 | tf_op jit(solution)/shard_map/ppermute | solution.py:456
  38.8 5.3 %collective-permute-start.8 = (f32[2,128,128]{2,1,0:T(8,128)S(1)}, f32[2,128,128]{2,1,0:T(8,128)S(1)}, u32[]{:S(2)}, u32[]{:S(2)}) collective-permute-start(f32[2,128,128]{2,1,0:T(8,128)S(1)} %get-tuple-element.50), channel_id=1, source_target_pairs={{0,8},{8,0},{1,9},{9,1},{2,10},{10,2},{3,11},{11,3},{4,12},{12,4},... | collective-permute-start | bytes 393224 | tf_op jit(solution)/shard_map/ppermute | solution.py:448
  38.8 5.3 %collective-permute-start.9 = (f32[5,2,2,128,128]{4,3,2,1,0:T(8,128)S(1)}, f32[5,2,2,128,128]{4,3,2,1,0:T(8,128)S(1)}, u32[]{:S(2)}, u32[]{:S(2)}) collective-permute-start(f32[5,2,2,128,128]{4,3,2,1,0:T(8,128)S(1)} %get-tuple-element.54.two), channel_id=1, source_target_pairs={{0,8},{8,0},{1,9},{9,1},{2,10},{10,2},{3,11},{11,3},{4,12},{12,4},... | collective-permute-start | bytes 3932168 | tf_op jit(solution)/shard_map/ppermute | solution.py:448

commit v8 on v6

--- a/solution.py
+++ b/solution.py
@@ -403,17 +403,16 @@
     planes, half = one.shape[0], one.shape[0] // 2
     section = lax.axis_index("tm")
     out = Planes(updated, parts, result, sem)
+    def start(p, h, q):
+        return jnp.where(section == 0, own[p, h, q], moved[p, h, q])
+
+    for top in range(half):
+        mean = jnp.where(section == 0, work[0, top], moved[planes, 0, top])
+        out.put(0, top, first[top] - mean, start)
     for top in range(half):
         out.put(1, top, change[0, top], lambda p, h, q: one[p, h, q])
     for top in range(half):
         out.put(2, top, change[1, top], lambda p, h, q: two[p, h, q])
-
-    def start(p, h, q):
-        return jnp.where(section == 0, own[p, h, q], moved[p, h, q])
-
-    for top in range(half):
-        mean = jnp.where(section == 0, work[0, top], moved[planes, 0, top])
-        out.put(0, top, first[top] - mean, start)
     out.finish()
 
 

time: 46.6 us -> 46.7 us (level)
  no operation moved by 1% of the time
where the time goes in v8:
time: 46.7 us; the launch traced here: 46.6 us
  waiting for transfers between devices  19.8 us (42%)
  starting transfers between devices  15.6 us (33%)
  Pallas kernels  11.1 us (24%)
    ppermute x3, waiting for transfers between devices, exchange(): lax.ppermute(near, 'space', list(enumerate(to_near)))  11.8 us
    pallas_call x7, Pallas kernels, call(): pl.pallas_call(kernel, name=name, out_shape=[jax.ShapeDtypeStruct(s, F32)...  11.1 us
    ppermute x3, starting transfers between devices, exchange(): lax.ppermute(far, 'space', list(enumerate(to_far)))  7.85 us
    ppermute x2, waiting for transfers between devices, handed_on(): out.append(lax.ppermute(value, ('tm', 'space'), perm))  4.76 us
    ppermute x2, starting transfers between devices, handed_on(): out.append(lax.ppermute(value, ('tm', 'space'), perm))  3.8 us
    ppermute x3, starting transfers between devices, exchange(): lax.ppermute(near, 'space', list(enumerate(to_near)))  3.43 us
    ppermute x3, waiting for transfers between devices, exchange(): lax.ppermute(far, 'space', list(enumerate(to_far)))  3.27 us
  transfers between devices with their start and end apart: 10, of which 4 were waited for; matrix products, arithmetic and copies ran while one was open for 0% of the time, Pallas kernels for 14%

profile of v8, /device:TPU:1, one launch (start us, length us, event | category | flops | bytes accessed | tf_op | source)
XLA Modules:
  0.0 46.6 jit_solution(3650863756030389924)
XLA Ops:
  0.0 1.5 %edge_mix.1 = (f32[2,2,128,128]{3,2,1,0:T(8,128)S(1)}, f32[2,2,128,128]{3,2,1,0:T(8,128)S(1)}) custom-call(f32[1,3,4,256,256]{4,3,2,1,0:T(8,128)} %nodes.3), custom_call_target="tpu_custom_call" | custom-call | flops 1048576 | bytes 2097152 | tf_op jit(solution)/shard_map/edge_mix/pallas_call | solution.py:424
  1.5 2.1 %collective-permute-start = (f32[2,2,128,128]{3,2,1,0:T(8,128)S(1)}, f32[2,2,128,128]{3,2,1,0:T(8,128)S(1)}, u32[]{:S(2)}, u32[]{:S(2)}) collective-permute-start(f32[2,2,128,128]{3,2,1,0:T(8,128)S(1)} %get-tuple-element.34.own_near), channel_id=1, source_target_pairs={{0,1},{1,0},{2,3},{3,2},{4,5},{5,4},{6,7},{7,6},{8,9},{9,8},{10,11... | collective-permute-start | bytes 786440 | tf_op jit(solution)/shard_map/ppermute | solution.py:446
  3.7 3.3 %collective-permute-start.1 = (f32[2,2,128,128]{3,2,1,0:T(8,128)S(1)}, f32[2,2,128,128]{3,2,1,0:T(8,128)S(1)}, u32[]{:S(2)}, u32[]{:S(2)}) collective-permute-start(f32[2,2,128,128]{3,2,1,0:T(8,128)S(1)} %get-tuple-element.35.own_far), channel_id=1, source_target_pairs={{0,7},{1,2},{2,1},{3,4},{4,3},{5,6},{6,5},{7,0},{8,15},{9,10},{10,... | collective-permute-start | bytes 786440 | tf_op jit(solution)/shard_map/ppermute | solution.py:447
  6.9 4.6 %first_stage.1 = (f32[4,2,2,128,128]{4,3,2,1,0:T(8,128)S(1)}, f32[4,2,2,128,128]{4,3,2,1,0:T(8,128)S(1)}, f32[4,2,2,128,128]{4,3,2,1,0:T(8,128)S(1)}, f32[2,2,12...) custom-call(f32[1,3,4,256,256]{4,3,2,1,0:T(8,128)} %nodes.3, ...), custom_call_target="tpu_custom_call" | custom-call | flops 10485760 | bytes 6291456 | tf_op jit(solution)/shard_map/first_stage/pallas_call | solution.py:424
  11.6 0.1 collective-permute-start.2
  11.7 1.3 %collective-permute-start.3 = (f32[2,2,128,128]{3,2,1,0:T(8,128)S(1)}, f32[2,2,128,128]{3,2,1,0:T(8,128)S(1)}, u32[]{:S(2)}, u32[]{:S(2)}) collective-permute-start(f32[2,2,128,128]{3,2,1,0:T(8,128)S(1)} %get-tuple-element.39), channel_id=1, source_target_pairs={{0,7},{1,2},{2,1},{3,4},{4,3},{5,6},{6,5},{7,0},{8,15},{9,10},{10,... | collective-permute-start | bytes 786440 | tf_op jit(solution)/shard_map/ppermute | solution.py:447
  13.0 2.3 %collective-permute-done.near = f32[2,2,128,128]{3,2,1,0:T(8,128)S(1)} collective-permute-done((f32[2,2,128,128]{3,2,1,0:T(8,128)S(1)}, f32[2,2,128,128]{3,2,1,0:T(8,128)S(1)}, u32[]{:S(2)}, u32[]{:S(2)}) %collective-permute-start) | collective-permute-done | bytes 262176 | tf_op jit(solution)/shard_map/ppermute | solution.py:446
  15.3 0.0 collective-permute-done.1.far
  15.3 1.8 %second_stage.1 = (f32[4,2,2,128,128]{4,3,2,1,0:T(8,128)S(1)}, f32[5,2,2,128,128]{4,3,2,1,0:T(8,128)S(1)}, f32[3,2,128,128]{3,2,1,0:T(8,128)S(1)}, f32[2,3,2,128...) custom-call(f32[4,2,2,128,128]{4,3,2,1,0:T(8,128)S(1)} %get-tuple-element.31.one_in, ...), custom_call_target="tpu_custom_call" | custom-call | flops 10485760 | bytes 6291456 | tf_op jit(solution)/shard_map/second_stage/pallas_call | solution.py:424
  17.1 9.4 %collective-permute-done.2.near = f32[2,2,128,128]{3,2,1,0:T(8,128)S(1)} collective-permute-done((f32[2,2,128,128]{3,2,1,0:T(8,128)S(1)}, f32[2,2,128,128]{3,2,1,0:T(8,128)S(1)}, u32[]{:S(2)}, u32[]{:S(2)}) %collective-permute-start.2) | collective-permute-done | bytes 262176 | tf_op jit(solution)/shard_map/ppermute | solution.py:446
  26.6 0.7 %third_stage.1 = (f32[5,2,2,128,128]{4,3,2,1,0:T(8,128)S(1)}, f32[2,128,128]{2,1,0:T(8,128)S(1)}, f32[2,128,128]{2,1,0:T(8,128)S(1)}, f32[5,2,128,128]{3,2,1,0:T(8,128)S(1)}) custom-call(f32[5,2,2,128,128]{4,3,2,1,0:T(8,128)S(1)} %get-tuple-element.37.two_in, f32[2,2,128,128]{3,2,1,0:T(8,128)S(1)} %collective-permute-done.2.near, ...), custom_call_target="tpu_custom_call", output_to_operand_aliasing={{0}: (0, {})} | custom-call | flops 5242880 | bytes 3145728 | tf_op jit(solution)/shard_map/third_stage/pallas_call | solution.py:424
  27.2 1.2 %collective-permute-start.4 = (f32[2,128,128]{2,1,0:T(8,128)S(1)}, f32[2,128,128]{2,1,0:T(8,128)S(1)}, u32[]{:S(2)}, u32[]{:S(2)}) collective-permute-start(f32[2,128,128]{2,1,0:T(8,128)S(1)} %get-tuple-element.44.own_near), channel_id=1, source_target_pairs={{0,1},{1,0},{2,3},{3,2},{4,5},{5,4},{6,7},{7,6},{8,9},{9,8},{10,11... | collective-permute-start | bytes 393224 | tf_op jit(solution)/shard_map/ppermute | solution.py:446
  28.5 3.2 %collective-permute-start.5 = (f32[2,128,128]{2,1,0:T(8,128)S(1)}, f32[2,128,128]{2,1,0:T(8,128)S(1)}, u32[]{:S(2)}, u32[]{:S(2)}) collective-permute-start(f32[2,128,128]{2,1,0:T(8,128)S(1)} %get-tuple-element.45.own_far), channel_id=1, source_target_pairs={{0,7},{1,2},{2,1},{3,4},{4,3},{5,6},{6,5},{7,0},{8,15},{9,10},{10,... | collective-permute-start | bytes 393224 | tf_op jit(solution)/shard_map/ppermute | solution.py:447
  31.7 0.0 collective-permute-done.4.near
  31.7 3.3 %collective-permute-done.5.far = f32[2,128,128]{2,1,0:T(8,128)S(1)} collective-permute-done((f32[2,128,128]{2,1,0:T(8,128)S(1)}, f32[2,128,128]{2,1,0:T(8,128)S(1)}, u32[]{:S(2)}, u32[]{:S(2)}) %collective-permute-start.5) | collective-permute-done | bytes 131104 | tf_op jit(solution)/shard_map/ppermute | solution.py:447
  35.0 3.3 %collective-permute-start.6 = (f32[2,128,128]{2,1,0:T(8,128)S(1)}, f32[2,128,128]{2,1,0:T(8,128)S(1)}, u32[]{:S(2)}, u32[]{:S(2)}) collective-permute-start(f32[2,128,128]{2,1,0:T(8,128)S(1)} %get-tuple-element.47), channel_id=1, source_target_pairs={{0,15},{1,10},{2,9},{3,12},{4,11},{5,14},{6,13},{7,8},{8,0},{9,1},... | collective-permute-start | bytes 393224 | tf_op jit(solution)/shard_map/ppermute | solution.py:460
  38.3 0.5 %collective-permute-start.7 = (f32[2,128,128]{2,1,0:T(8,128)S(1)}, f32[2,128,128]{2,1,0:T(8,128)S(1)}, u32[]{:S(2)}, u32[]{:S(2)}) collective-permute-start(f32[2,128,128]{2,1,0:T(8,128)S(1)} %get-tuple-element.48), channel_id=1, source_target_pairs={{0,9},{1,8},{2,11},{3,10},{4,13},{5,12},{6,15},{7,14},{8,0},{9,1},... | collective-permute-start | bytes 393224 | tf_op jit(solution)/shard_map/ppermute | solution.py:460
  38.8 0.0 collective-permute-start.8
  38.8 0.5 %collective-permute-start.9 = (f32[5,2,2,128,128]{4,3,2,1,0:T(8,128)S(1)}, f32[5,2,2,128,128]{4,3,2,1,0:T(8,128)S(1)}, u32[]{:S(2)}, u32[]{:S(2)}) collective-permute-start(f32[5,2,2,128,128]{4,3,2,1,0:T(8,128)S(1)} %get-tuple-element.53.two), channel_id=1, source_target_pairs={{0,8},{8,0},{1,9},{9,1},{2,10},{10,2},{3,11},{11,3},{4,12},{12,4},... | collective-permute-start | bytes 3932168 | tf_op jit(solution)/shard_map/ppermute | solution.py:452
  39.3 4.8 %collective-permute-done.6.ring_far = f32[2,128,128]{2,1,0:T(8,128)S(1)} collective-permute-done((f32[2,128,128]{2,1,0:T(8,128)S(1)}, f32[2,128,128]{2,1,0:T(8,128)S(1)}, u32[]{:S(2)}, u32[]{:S(2)}) %collective-permute-start.6) | collective-permute-done | bytes 131104 | tf_op jit(solution)/shard_map/ppermute | solution.py:460
  44.1 0.0 collective-permute-done.7.ring_near
  44.1 0.0 collective-permute-done.8.end
  44.1 0.3 coarse_steps.1
  44.4 2.2 %update.1 = f32[1,3,4,256,256]{4,3,2,1,0:T(8,128)} custom-call(f32[4,2,2,128,128]{4,3,2,1,0:T(8,128)S(1)} %get-tuple-element.30.own, f32[2,128,128]{2,1,0:T(8,128)S(1)} %get-tuple-element.51.first, f32[2,2,128,128]{3,2,1,0:T(8,128)S(1)} %get-tuple-element.52.change, f32[5,2,2,128,128]{4,3,2,1,0:T(8,128)S(1)} %collective-permute-done.9.moved, ...), custom_call_target="tpu_custom_call" | custom-call | flops 5242880 | bytes 6291456 | tf_op jit(solution)/shard_map/update/pallas_call | solution.py:424
  (5 shorter events, 0.1 us)
Async XLA Ops:
  0.0 6.9 %copy-start = (bf16[256,256]{1,0:T(8,128)(2,1)S(1)}, bf16[256,256]{1,0:T(8,128)(2,1)}, u32[]{:S(2)}) copy-start(bf16[256,256]{1,0:T(8,128)(2,1)} %constant.2.clone.pairs) | copy-start | bytes 393220
  1.5 13.8 %collective-permute-start = (f32[2,2,128,128]{3,2,1,0:T(8,128)S(1)}, f32[2,2,128,128]{3,2,1,0:T(8,128)S(1)}, u32[]{:S(2)}, u32[]{:S(2)}) collective-permute-start(f32[2,2,128,128]{3,2,1,0:T(8,128)S(1)} %get-tuple-element.34.own_near), channel_id=1, source_target_pairs={{0,1},{1,0},{2,3},{3,2},{4,5},{5,4},{6,7},{7,6},{8,9},{9,8},{10,11... | collective-permute-start | bytes 786440 | tf_op jit(solution)/shard_map/ppermute | solution.py:446
  3.7 11.7 %collective-permute-start.1 = (f32[2,2,128,128]{3,2,1,0:T(8,128)S(1)}, f32[2,2,128,128]{3,2,1,0:T(8,128)S(1)}, u32[]{:S(2)}, u32[]{:S(2)}) collective-permute-start(f32[2,2,128,128]{3,2,1,0:T(8,128)S(1)} %get-tuple-element.35.own_far), channel_id=1, source_target_pairs={{0,7},{1,2},{2,1},{3,4},{4,3},{5,6},{6,5},{7,0},{8,15},{9,10},{10,... | collective-permute-start | bytes 786440 | tf_op jit(solution)/shard_map/ppermute | solution.py:447
  11.6 15.0 %collective-permute-start.2 = (f32[2,2,128,128]{3,2,1,0:T(8,128)S(1)}, f32[2,2,128,128]{3,2,1,0:T(8,128)S(1)}, u32[]{:S(2)}, u32[]{:S(2)}) collective-permute-start(f32[2,2,128,128]{3,2,1,0:T(8,128)S(1)} %get-tuple-element.38), channel_id=1, source_target_pairs={{0,1},{1,0},{2,3},{3,2},{4,5},{5,4},{6,7},{7,6},{8,9},{9,8},{10,11... | collective-permute-start | bytes 786440 | tf_op jit(solution)/shard_map/ppermute | solution.py:446
  11.7 14.9 %collective-permute-start.3 = (f32[2,2,128,128]{3,2,1,0:T(8,128)S(1)}, f32[2,2,128,128]{3,2,1,0:T(8,128)S(1)}, u32[]{:S(2)}, u32[]{:S(2)}) collective-permute-start(f32[2,2,128,128]{3,2,1,0:T(8,128)S(1)} %get-tuple-element.39), channel_id=1, source_target_pairs={{0,7},{1,2},{2,1},{3,4},{4,3},{5,6},{6,5},{7,0},{8,15},{9,10},{10,... | collective-permute-start | bytes 786440 | tf_op jit(solution)/shard_map/ppermute | solution.py:447
  27.2 4.5 %collective-permute-start.4 = (f32[2,128,128]{2,1,0:T(8,128)S(1)}, f32[2,128,128]{2,1,0:T(8,128)S(1)}, u32[]{:S(2)}, u32[]{:S(2)}) collective-permute-start(f32[2,128,128]{2,1,0:T(8,128)S(1)} %get-tuple-element.44.own_near), channel_id=1, source_target_pairs={{0,1},{1,0},{2,3},{3,2},{4,5},{5,4},{6,7},{7,6},{8,9},{9,8},{10,11... | collective-permute-start | bytes 393224 | tf_op jit(solution)/shard_map/ppermute | solution.py:446
  28.5 6.5 %collective-permute-start.5 = (f32[2,128,128]{2,1,0:T(8,128)S(1)}, f32[2,128,128]{2,1,0:T(8,128)S(1)}, u32[]{:S(2)}, u32[]{:S(2)}) collective-permute-start(f32[2,128,128]{2,1,0:T(8,128)S(1)} %get-tuple-element.45.own_far), channel_id=1, source_target_pairs={{0,7},{1,2},{2,1},{3,4},{4,3},{5,6},{6,5},{7,0},{8,15},{9,10},{10,... | collective-permute-start | bytes 393224 | tf_op jit(solution)/shard_map/ppermute | solution.py:447
  35.0 9.1 %collective-permute-start.6 = (f32[2,128,128]{2,1,0:T(8,128)S(1)}, f32[2,128,128]{2,1,0:T(8,128)S(1)}, u32[]{:S(2)}, u32[]{:S(2)}) collective-permute-start(f32[2,128,128]{2,1,0:T(8,128)S(1)} %get-tuple-element.47), channel_id=1, source_target_pairs={{0,15},{1,10},{2,9},{3,12},{4,11},{5,14},{6,13},{7,8},{8,0},{9,1},... | collective-permute-start | bytes 393224 | tf_op jit(solution)/shard_map/ppermute | solution.py:460
  38.3 5.8 %collective-permute-start.7 = (f32[2,128,128]{2,1,0:T(8,128)S(1)}, f32[2,128,128]{2,1,0:T(8,128)S(1)}, u32[]{:S(2)}, u32[]{:S(2)}) collective-permute-start(f32[2,128,128]{2,1,0:T(8,128)S(1)} %get-tuple-element.48), channel_id=1, source_target_pairs={{0,9},{1,8},{2,11},{3,10},{4,13},{5,12},{6,15},{7,14},{8,0},{9,1},... | collective-permute-start | bytes 393224 | tf_op jit(solution)/shard_map/ppermute | solution.py:460
  38.8 5.3 %collective-permute-start.8 = (f32[2,128,128]{2,1,0:T(8,128)S(1)}, f32[2,128,128]{2,1,0:T(8,128)S(1)}, u32[]{:S(2)}, u32[]{:S(2)}) collective-permute-start(f32[2,128,128]{2,1,0:T(8,128)S(1)} %get-tuple-element.49), channel_id=1, source_target_pairs={{0,8},{8,0},{1,9},{9,1},{2,10},{10,2},{3,11},{11,3},{4,12},{12,4},... | collective-permute-start | bytes 393224 | tf_op jit(solution)/shard_map/ppermute | solution.py:452
  38.8 5.6 %collective-permute-start.9 = (f32[5,2,2,128,128]{4,3,2,1,0:T(8,128)S(1)}, f32[5,2,2,128,128]{4,3,2,1,0:T(8,128)S(1)}, u32[]{:S(2)}, u32[]{:S(2)}) collective-permute-start(f32[5,2,2,128,128]{4,3,2,1,0:T(8,128)S(1)} %get-tuple-element.53.two), channel_id=1, source_target_pairs={{0,8},{8,0},{1,9},{9,1},{2,10},{10,2},{3,11},{11,3},{4,12},{12,4},... | collective-permute-start | bytes 3932168 | tf_op jit(solution)/shard_map/ppermute | solution.py:452
